TPU v7x, 256 devices: a whole 4x4x8 slice. The times are simulated.
256 devices in a mesh: blk: 16 (over z_lo, x, core), team: 16 (over y, z_hi).
Axes of the slice: x: 4, y: 4, z: 8 (z_hi: 4, z_lo: 2; z = z_hi * 2 + z_lo), core: 2. Of those that a mesh axis runs over, the one named last changes fastest.
Arguments:
- features: bfloat16 [32768, 256], P(('blk', 'team')), may hold values from -6 to 6
- weight: bfloat16 [256, 256], replicated, may hold values from -0.375 to 0.375
- grad_out: bfloat16 [32768, 256], P(('blk', 'team')), may hold values from -6 to 6
- block_vals: bfloat16 [256, 3, 16, 128, 128], P(('blk', 'team')), as said below
- block_rows: int32 [256, 3, 16], P(('blk', 'team')), may hold values from 0 to 255, as said below
- block_cols: int32 [256, 3, 16], P(('blk', 'team')), may hold values from 0 to 255, as said below
- block_counts: int32 [256, 3], P(('blk', 'team')), may hold values from 0 to 16, as said below
Outputs:
- activations: bfloat16 [32768, 256], P(('blk', 'team'))
- grad_feats: bfloat16 [32768, 256], P(('blk', 'team'))
- grad_weight: float32 [256, 256], replicated
Inputs may be any that keep to these rules, and one draw needn't show every extreme that they name: `block_rows`: on the device at blk index b, every slot, used or not, names a block row of row slab b, that is b * 16 to (b + 1) * 16 - 1. `block_cols`: on the device at blk index b, every slot of offset s, used or not, names a block column of row slab (b + s - 1) mod 16. The first block_counts[d, s] slots of device d and offset s are used, the rest are to be ignored. Offset 1, the device's own slab, is full on every device. `block_vals`: no two used slots name the same block. A is symmetric: whenever block (R, C) is listed, block (C, R) is listed with the transposed values, and a block with R = C is symmetric itself.
All inputs are finite; a program needn't handle non-finite values.
Results may differ from a plain program's by a relative error of at most 0.0061.
Values may be sent and summed in bfloat16 or wider, within the bound.
No kernel may reach another device: no remote copies, remote signals or barrier semaphores. Data moves between devices by JAX's collectives and lax.ppermute only.
A program may use at most 64 MiB of HBM per device.

v0:
```python
import jax
import jax.numpy as jnp
from jax import lax
from jax.sharding import PartitionSpec as P

REACH = 1


def from_behind(block, axis, distance):
    devices = range(lax.axis_size(axis))
    route = [((i - distance) % len(devices), i) for i in devices]
    return lax.ppermute(block, axis, route)


def extended(block, sides, width):
    for axis, dim in sides:
        count = lax.axis_size(axis)
        forward = [(i, i + 1) for i in range(count - 1)]
        forward.append((count - 1, 0))
        backward = [(target, source) for source, target in forward]
        low = lax.ppermute(
            lax.slice_in_dim(block, block.shape[dim] - width, None, axis=dim), axis, forward
        )
        high = lax.ppermute(lax.slice_in_dim(block, 0, width, axis=dim), axis, backward)
        block = jnp.concatenate([low, block, high], axis=dim)
    return block


def aggregate(wide_slab, values, row_ids, col_ids, used_slots, blk_index):
    offsets, slot_count, block_size = (values.shape[0], values.shape[1], values.shape[2])
    feat_dim = wide_slab.shape[1]
    tile_set = wide_slab.reshape(-1, block_size, feat_dim)
    slab_blocks = tile_set.shape[0] // offsets
    slab_count = lax.axis_size("blk")
    slot_ids = jnp.arange(slot_count)
    block_ids = jnp.arange(slab_blocks)
    running = jnp.zeros((slab_blocks, block_size * feat_dim), jnp.float32)
    for offset in range(offsets):
        col_slab = (blk_index + offset - REACH) % slab_count
        sources = offset * slab_blocks + col_ids[offset] - col_slab * slab_blocks
        picked = jnp.take(tile_set, sources, axis=0, mode="clip")
        products = jnp.einsum(
            "kij,kjf->kif", values[offset], picked, preferred_element_type=jnp.float32
        )
        in_use = slot_ids < used_slots[offset]
        targets = row_ids[offset] - blk_index * slab_blocks
        select = ((targets[None, :] == block_ids[:, None]) & in_use[None, :]).astype(jnp.float32)
        running = running + jnp.dot(
            select,
            products.reshape(slot_count, -1),
            precision=lax.Precision.HIGHEST,
            preferred_element_type=jnp.float32,
        )
    return running.reshape(slab_blocks * block_size, feat_dim)


def spread_back(grad_slab, values, row_ids, col_ids, used_slots, blk_index):
    offsets, slot_count, block_size = (values.shape[0], values.shape[1], values.shape[2])
    feat_dim = grad_slab.shape[1]
    tile_set = grad_slab.reshape(-1, block_size, feat_dim)
    slab_blocks = tile_set.shape[0]
    slab_count = lax.axis_size("blk")
    slot_ids = jnp.arange(slot_count)
    block_ids = jnp.arange(slab_blocks)
    running = jnp.zeros((slab_blocks, block_size * feat_dim), jnp.float32)
    for offset in range(offsets):
        col_slab = (blk_index + offset - REACH) % slab_count
        picked = jnp.take(tile_set, row_ids[offset] - blk_index * slab_blocks, axis=0, mode="clip")
        products = jnp.einsum(
            "kji,kjf->kif", values[offset], picked, preferred_element_type=jnp.float32
        )
        in_use = slot_ids < used_slots[offset]
        targets = col_ids[offset] - col_slab * slab_blocks
        select = ((targets[None, :] == block_ids[:, None]) & in_use[None, :]).astype(jnp.float32)
        moved = jnp.dot(
            select,
            products.reshape(slot_count, -1),
            precision=lax.Precision.HIGHEST,
            preferred_element_type=jnp.float32,
        )
        if offset != REACH:
            moved = from_behind(moved, "blk", offset - REACH)
        running = running + moved
    return running.reshape(slab_blocks * block_size, feat_dim)


def on_device(features, weight, grad_out, block_vals, block_rows, block_cols, block_counts):
    blk_index = lax.axis_index("blk")
    rows_dev = features.shape[0]
    team_size = lax.axis_size("team")
    slab_rows = rows_dev * team_size
    values = block_vals[0]
    row_ids = block_rows[0]
    col_ids = block_cols[0]
    used_slots = block_counts[0]
    slab_feats = lax.all_gather(features, "team", axis=0, tiled=True)
    wide_slab = extended(slab_feats, (("blk", 0),), REACH * slab_rows)
    partial_value = aggregate(wide_slab, values, row_ids, col_ids, used_slots, blk_index)
    hidden = lax.psum_scatter(partial_value, "team", scatter_dimension=0, tiled=True).astype(
        jnp.bfloat16
    )
    pre_act = jnp.dot(hidden, weight, preferred_element_type=jnp.float32)
    sig_pre = jax.nn.sigmoid(pre_act)
    activations = (pre_act * sig_pre).astype(jnp.bfloat16)
    grad_pre = (grad_out.astype(jnp.float32) * sig_pre * (1.0 + pre_act * (1.0 - sig_pre))).astype(
        jnp.bfloat16
    )
    local_grad = lax.dot_general(
        hidden, grad_pre, (((0,), (0,)), ((), ())), preferred_element_type=jnp.float32
    )
    node_total = rows_dev * lax.axis_size("blk") * team_size
    grad_weight = lax.psum(local_grad, ("blk", "team")) * node_total ** (-0.5)
    back_rows = lax.dot_general(
        grad_pre, weight, (((1,), (1,)), ((), ())), preferred_element_type=jnp.float32
    ).astype(jnp.bfloat16)
    grad_slab = lax.all_gather(back_rows, "team", axis=0, tiled=True)
    grad_partial = spread_back(grad_slab, values, row_ids, col_ids, used_slots, blk_index)
    grad_feats = lax.psum_scatter(grad_partial, "team", scatter_dimension=0, tiled=True).astype(
        jnp.bfloat16
    )
    return (activations, grad_feats, grad_weight)


def solution(mesh):
    in_specs = (
        P(("blk", "team"), None),
        P(),
        P(("blk", "team"), None),
        P(("blk", "team"), None, None, None, None),
        P(("blk", "team"), None, None),
        P(("blk", "team"), None, None),
        P(("blk", "team"), None),
    )
    out_specs = (P(("blk", "team"), None), P(("blk", "team"), None), P())
    return jax.shard_map(
        on_device, mesh=mesh, in_specs=in_specs, out_specs=out_specs, check_vma=False
    )
```

profile of v0, /device:TPU:2, one launch (start us, length us, event | category | flops | bytes accessed | tf_op | source)
XLA Modules:
  0.0 622.2 jit_solution(1855752278822943925)
XLA Ops:
  7.2 0.0 copy-start
  7.2 0.0 all-gather.3.cloned.1.call-start
  7.2 0.7 all-gather.3.cloned.1.call-update
  7.9 0.0 reduce-scatter.3.cloned.1.call-start
  8.0 59.1 %all-gather.3.cloned.1.call-done = bf16[2048,256]{1,0:T(8,128)(2,1)} async-done(((bf16[128,256]{1,0:T(8,128)(2,1)}), bf16[2048,256]{1,0:T(8,128)(2,1)}) %all-gather.3.cloned.1.call-update) | async-done | bytes 1048592 | tf_op jit(solution)/shard_map/all_gather | solution.py:96
  67.1 0.0 collective-permute-start.1
  67.1 0.5 collective-permute-start
  67.6 1.4 fusion.44
  69.0 0.6 iota_compare_fusion.6
  69.6 0.7 iota_compare_fusion.8
  70.3 0.7 iota_compare_fusion.7
  70.9 0.7 subtract_bitcast_fusion.1
  71.6 0.7 subtract_bitcast_fusion.3
  72.3 7.4 %collective-permute-done.1 = bf16[2048,256]{1,0:T(8,128)(2,1)S(1)} collective-permute-done((bf16[2048,256]{1,0:T(8,128)(2,1)}, bf16[2048,256]{1,0:T(8,128)(2,1)S(1)}, u32[]{:S(2)}, u32[]{:S(2)}) %collective-permute-start.1) | collective-permute-done | bytes 1048608 | tf_op jit(solution)/shard_map/ppermute | solution.py:24
  79.7 1.0 copy-done.7
  80.7 0.9 collective-permute-done
  81.6 2.1 pad_maximum_fusion
  83.8 1.6 gather_fusion.2
  85.4 1.6 gather_fusion.1
  87.0 1.6 gather_fusion
  88.5 3.2 convolution_bitcast_fusion.5
  91.7 2.3 copy.28
  94.0 2.8 convolution_bitcast_fusion.4
  96.9 3.1 copy.29
  100.0 2.9 convolution_bitcast_fusion.3
  102.9 3.0 copy.30
  105.9 1.1 fusion.18
  107.0 0.5 copy-done.2
  107.5 1.2 convolution_add_fusion.2
  108.7 0.4 copy-done.3
  109.1 1.2 convolution_add_fusion.1
  110.3 1.5 reshape.200
  111.8 0.0 reduce-scatter.3.cloned.1.call-update
  111.8 0.0 all-gather.5.cloned.1.call-start
  111.9 87.6 %reduce-scatter.3.cloned.1.call-done = f32[128,256]{1,0:T(8,128)} async-done(((f32[2048,256]{1,0:T(8,128)}), f32[128,256]{1,0:T(8,128)}) %reduce-scatter.3.cloned.1.call-update) | async-done | bytes 131088 | tf_op jit(solution)/shard_map/reduce_scatter | solution.py:99
  199.5 1.7 multiply_convert_fusion.1
  201.2 0.8 convolution_convert_fusion
  202.1 0.0 all-gather.5.cloned.1.call-update
  202.1 0.2 all-reduce.2.cloned.1.call-start
  202.4 51.3 %all-gather.5.cloned.1.call-done = bf16[2048,256]{1,0:T(8,128)(2,1)} async-done(((bf16[128,256]{1,0:T(8,128)(2,1)}), bf16[2048,256]{1,0:T(8,128)(2,1)}) %all-gather.5.cloned.1.call-update) | async-done | bytes 1048592 | tf_op jit(solution)/shard_map/all_gather | solution.py:116
  253.6 2.9 gather_fusion.5
  256.5 0.6 gather_fusion.3
  257.2 2.9 convolution_bitcast_fusion.2
  260.0 2.2 copy.31
  262.2 2.4 fusion.25
  264.7 2.8 convolution_bitcast_fusion
  267.5 2.2 copy.33
  269.7 2.5 fusion.30
  272.2 0.0 collective-permute-start.3
  272.2 1.7 collective-permute-start.2
  274.0 0.9 fusion.13
  274.9 0.0 all-reduce.2.cloned.1.call-update
  274.9 0.0 reduce-scatter.5.cloned.1.call-start
  275.0 0.6 gather_fusion.4
  275.6 2.9 convolution_bitcast_fusion.1
  278.5 2.2 copy.32
  280.7 17.4 %collective-permute-done.3 = f32[16,32768]{1,0:T(8,128)} collective-permute-done((f32[16,32768]{1,0:T(8,128)}, f32[16,32768]{1,0:T(8,128)}, u32[]{:S(2)}, u32[]{:S(2)}) %collective-permute-start.3) | collective-permute-done | bytes 2097184 | tf_op jit(solution)/shard_map/ppermute | solution.py:12
  298.1 4.8 fusion
  302.9 2.7 reshape.205
  305.6 0.0 reduce-scatter.5.cloned.1.call-update
  305.6 217.1 %all-reduce.2.cloned.1.call-done = f32[256,256]{1,0:T(8,128)} async-done(((f32[256,256]{1,0:T(8,128)}), f32[256,256]{1,0:T(8,128)}) %all-reduce.2.cloned.1.call-update) | async-done | bytes 262160 | tf_op jit(solution)/shard_map/psum | solution.py:112
  522.8 1.7 broadcast_multiply_fusion
  524.4 89.6 %reduce-scatter.5.cloned.1.call-done = f32[128,256]{1,0:T(8,128)} async-done(((f32[2048,256]{1,0:T(8,128)}), f32[128,256]{1,0:T(8,128)}) %reduce-scatter.5.cloned.1.call-update) | async-done | bytes 131088 | tf_op jit(solution)/shard_map/reduce_scatter | solution.py:118
  614.1 1.5 convert_element_type.29
  (21 shorter events, 0.1 us)
Async XLA Ops:
  7.2 192.3 %copy-start = (bf16[256,256]{1,0:T(8,128)(2,1)S(1)}, bf16[256,256]{1,0:T(8,128)(2,1)}, u32[]{:S(2)}) copy-start(bf16[256,256]{1,0:T(8,128)(2,1)} %param.8) | copy-start | bytes 393220
  7.2 59.9 %all-gather.3.cloned.1.call-start = ((), (), s32[]{:S(2)}) async-start(), calls=%async_computation.2 | async-start | bytes 1114112 | tf_op jit(solution)/shard_map/all_gather | solution.py:96
  7.9 191.6 %reduce-scatter.3.cloned.1.call-start = ((), (), s32[]{:S(2)}) async-start(), calls=%async_computation.3 | async-start | bytes 2228224 | tf_op jit(solution)/shard_map/reduce_scatter | solution.py:99
  67.1 12.6 %collective-permute-start.1 = (bf16[2048,256]{1,0:T(8,128)(2,1)}, bf16[2048,256]{1,0:T(8,128)(2,1)S(1)}, u32[]{:S(2)}, u32[]{:S(2)}) collective-permute-start(bf16[2048,256]{1,0:T(8,128)(2,1)} %all-gather.3.cloned.1.call-done), channel_id=1, source_target_pairs={{16,0},{32,16},{48,32},{64,48},{80,64},{96,80},{112,96},{128,112},... | collective-permute-start | bytes 3145736 | tf_op jit(solution)/shard_map/ppermute | solution.py:24
  67.1 14.5 %collective-permute-start = (bf16[2048,256]{1,0:T(8,128)(2,1)}, bf16[2048,256]{1,0:T(8,128)(2,1)}, u32[]{:S(2)}, u32[]{:S(2)}) collective-permute-start(bf16[2048,256]{1,0:T(8,128)(2,1)} %all-gather.3.cloned.1.call-done), channel_id=1, source_target_pairs={{0,16},{16,32},{32,48},{48,64},{64,80},{80,96},{96,112},{112,128},... | collective-permute-start | bytes 3145736 | tf_op jit(solution)/shard_map/ppermute | solution.py:21
  79.7 1.0 copy-start.7
  91.7 2.3 copy-start.6
  96.9 3.1 copy-start.4
  105.9 1.6 copy-start.2
  107.5 1.6 copy-start.3
  111.8 89.5 %copy-start.9 = (bf16[128,256]{1,0:T(8,128)(2,1)S(1)}, bf16[128,256]{1,0:T(8,128)(2,1)}, u32[]{:S(2)}) copy-start(bf16[128,256]{1,0:T(8,128)(2,1)} %param.9) | copy-start | bytes 196612
  111.8 141.8 %all-gather.5.cloned.1.call-start = ((), (), s32[]{:S(2)}) async-start(), calls=%async_computation.4 | async-start | bytes 1114112 | tf_op jit(solution)/shard_map/all_gather | solution.py:116
  202.1 320.7 %all-reduce.2.cloned.1.call-start = ((), (), s32[]{:S(2)}) async-start(), calls=%async_computation.6 | async-start | bytes 524288 | tf_op jit(solution)/shard_map/psum | solution.py:112
  253.6 2.9 copy-start.1
  262.2 2.4 copy-start.5
  269.7 4.3 copy-start.8
  272.2 25.9 %collective-permute-start.3 = (f32[16,32768]{1,0:T(8,128)}, f32[16,32768]{1,0:T(8,128)}, u32[]{:S(2)}, u32[]{:S(2)}) collective-permute-start(f32[16,32768]{1,0:T(8,128)} %fusion.30), channel_id=1, source_target_pairs={{240,0},{0,16},{16,32},{32,48},{48,64},{64,80},{80,96},{96,112},{1... | collective-permute-start | bytes 6291464 | tf_op jit(solution)/shard_map/ppermute | solution.py:12
  272.2 25.9 %collective-permute-start.2 = (f32[16,32768]{1,0:T(8,128)}, f32[16,32768]{1,0:T(8,128)}, u32[]{:S(2)}, u32[]{:S(2)}) collective-permute-start(f32[16,32768]{1,0:T(8,128)} %fusion.25), channel_id=1, source_target_pairs={{16,0},{32,16},{48,32},{64,48},{80,64},{96,80},{112,96},{128,112},... | collective-permute-start | bytes 6291464 | tf_op jit(solution)/shard_map/ppermute | solution.py:12
  274.9 339.2 %reduce-scatter.5.cloned.1.call-start = ((), (), s32[]{:S(2)}) async-start(), calls=%async_computation.5 | async-start | bytes 2228224 | tf_op jit(solution)/shard_map/reduce_scatter | solution.py:118
Sparse Core Ops, SparseCore 0:
  10.4 56.5 all-gather.2
  111.9 87.5 reduce-scatter.2
  202.8 50.7 all-gather.4
  275.0 247.6 all-reduce.1
  526.6 87.4 reduce-scatter.4
where the time goes:
time: 623 us; the launch traced here: 622 us
  waiting for transfers between devices  531 us (85%)
  matrix products  34.2 us (5%)
  local copies, waits for them, and re-layouts  31.3 us (5%)
  between operations  14 us (2%)
  other arithmetic  8.71 us (1%)
    psum x1, waiting for transfers between devices, on_device(): grad_weight = lax.psum(local_grad, ('blk', 'team')) * node_total ** (-0.5)  217 us
    reduce_scatter x1, waiting for transfers between devices, on_device(): lax.psum_scatter(grad_partial, 'team', scatter_dimension=0, tiled=True)  89.6 us
    reduce_scatter x1, waiting for transfers between devices, on_device(): lax.psum_scatter(partial_value, 'team', scatter_dimension=0, tiled=True)  87.6 us
    all_gather x1, waiting for transfers between devices, on_device(): slab_feats = lax.all_gather(features, 'team', axis=0, tiled=True)  59.1 us
    all_gather x1, waiting for transfers between devices, on_device(): grad_slab = lax.all_gather(back_rows, 'team', axis=0, tiled=True)  51.3 us
    ppermute x2, waiting for transfers between devices, from_behind(): return lax.ppermute(block, axis, route)  17.4 us
    unnamed x26, local copies, waits for them, and re-layouts  16.9 us
  transfers between devices with their start and end apart: 9, of which 8 were waited for; matrix products, arithmetic and copies ran while one was open for 3% of the time, Pallas kernels for 0%

commit v1 on v0

v1 whole, which is shorter than its diff:
```python
import jax
import jax.numpy as jnp
from jax import lax
from jax.experimental import pallas as pl
from jax.experimental.pallas import tpu as pltpu
from jax.sharding import PartitionSpec as P

BF = jnp.bfloat16
F32 = jnp.float32
VMEM = pltpu.VMEM
SMEM = pltpu.SMEM
HBM_MB = 1 << 20
SIDE = 4


def along_z(k):
    return [(t, (t // SIDE) * SIDE + (t % SIDE + k) % SIDE) for t in range(SIDE * SIDE)]


def along_y(k):
    return [(t, ((t // SIDE + k) % SIDE) * SIDE + t % SIDE) for t in range(SIDE * SIDE)]


def along_blk(k):
    count = lax.axis_size("blk")
    return [(b, (b + k) % count) for b in range(count)]


def gather_side(block, route):
    return [block] + [lax.ppermute(block, "team", route(-k)) for k in range(1, SIDE)]


def aggregate_kernel(place, rows, cols, counts, *refs):
    chunks = refs[:12]
    values = refs[12]
    own, *sends = refs[13:17]
    tiles, blocks, total, tile_sems, block_sems = refs[17:]
    order = (1, 0, 2)
    copies = []
    for n, offset in enumerate(order):
        block_copy = pltpu.make_async_copy(
            values.at[offset], blocks.at[offset], block_sems.at[offset]
        )
        block_copy.start()
        group = [block_copy]
        for c in range(SIDE):
            slot = n * SIDE + c
            copy = pltpu.make_async_copy(
                chunks[slot], tiles.at[offset, pl.ds(c * SIDE, SIDE)], tile_sems.at[slot]
            )
            copy.start()
            group.append(copy)
        copies.append(group)
    my_y, my_z = place[0], place[1]
    total[...] = jnp.zeros_like(total)

    def one(offset, k):
        col = cols[offset, k] & 15
        row = rows[offset, k] & 15
        source = (((col >> 2) - my_y) & 3) * SIDE + ((col - my_z) & 3)
        product = jnp.dot(
            blocks[offset, k], tiles[offset, source], preferred_element_type=F32
        )
        total[row] = total[row] + product

    for offset, group in zip(order, copies):
        for copy in group:
            copy.wait()
        if offset == 1:
            for k in range(16):
                one(offset, k)
        else:

            @pl.loop(0, counts[offset])
            def _(k):
                one(offset, k)

    own[...] = total[pl.ds(my_y * SIDE, SIDE)]
    for k in range(1, SIDE):
        sends[k - 1][...] = total[pl.ds(((my_y + k) & 3) * SIDE, SIDE)].astype(BF)


def aggregate(place, chunks, values, rows, cols, counts):
    quarter = chunks[0].shape
    return pl.pallas_call(
        aggregate_kernel,
        in_specs=[pl.BlockSpec(memory_space=SMEM)] * 4
        + [pl.BlockSpec(memory_space=pl.ANY)] * 13,
        out_specs=[pl.BlockSpec(memory_space=VMEM)] * 4,
        out_shape=[jax.ShapeDtypeStruct(quarter, F32)] + [jax.ShapeDtypeStruct(quarter, BF)] * 3,
        scratch_shapes=[
            pltpu.VMEM((3, 16) + quarter[1:], BF),
            pltpu.VMEM(values.shape, BF),
            pltpu.VMEM((16,) + quarter[1:], F32),
            pltpu.SemaphoreType.DMA((12,)),
            pltpu.SemaphoreType.DMA((3,)),
        ],
        compiler_params=pltpu.CompilerParams(vmem_limit_bytes=24 * HBM_MB),
        name="aggregate",
    )(place, rows, cols, counts, *chunks, values)


def fold_kernel(place, own, one, two, three, kept, *sends):
    my_z = place[1]

    def summed(z):
        return (
            own[z]
            + one[z].astype(F32)
            + two[z].astype(F32)
            + three[z].astype(F32)
        )

    kept[...] = summed(my_z)
    for k in range(1, SIDE):
        sends[k - 1][...] = summed((my_z + k) & 3).astype(BF)


def fold(place, own, arrived):
    piece = own.shape[1:]
    return pl.pallas_call(
        fold_kernel,
        in_specs=[pl.BlockSpec(memory_space=SMEM)] + [pl.BlockSpec(memory_space=VMEM)] * 4,
        out_specs=[pl.BlockSpec(memory_space=VMEM)] * 4,
        out_shape=[jax.ShapeDtypeStruct(piece, F32)] + [jax.ShapeDtypeStruct(piece, BF)] * 3,
        compiler_params=pltpu.CompilerParams(vmem_limit_bytes=16 * HBM_MB),
        name="fold",
    )(place, own, *arrived)


def dense_kernel(own, one, two, three, weight, grad_out, act, back, local_grad):
    hidden = (
        own[...] + one[...].astype(F32) + two[...].astype(F32) + three[...].astype(F32)
    ).astype(BF)
    pre_act = jnp.dot(hidden, weight[...], preferred_element_type=F32)
    sig_pre = jax.nn.sigmoid(pre_act)
    act[...] = (pre_act * sig_pre).astype(BF)
    grad_pre = (
        grad_out[...].astype(F32) * sig_pre * (1.0 + pre_act * (1.0 - sig_pre))
    ).astype(BF)
    back[...] = lax.dot_general(
        grad_pre, weight[...], (((1,), (1,)), ((), ())), preferred_element_type=F32
    ).astype(BF)
    local_grad[...] = lax.dot_general(
        hidden, grad_pre, (((0,), (0,)), ((), ())), preferred_element_type=F32
    )


def dense(own, arrived, weight, grad_out):
    piece = own.shape
    return pl.pallas_call(
        dense_kernel,
        in_specs=[pl.BlockSpec(memory_space=VMEM)] * 6,
        out_specs=[pl.BlockSpec(memory_space=VMEM)] * 3,
        out_shape=[
            jax.ShapeDtypeStruct(piece, BF),
            jax.ShapeDtypeStruct(piece, BF),
            jax.ShapeDtypeStruct(weight.shape, F32),
        ],
        compiler_params=pltpu.CompilerParams(vmem_limit_bytes=16 * HBM_MB),
        name="dense",
    )(own, *arrived, weight, grad_out)


def finish_kernel(own, one, two, three, out):
    out[...] = (
        own[...] + one[...].astype(F32) + two[...].astype(F32) + three[...].astype(F32)
    ).astype(BF)


def finish(own, arrived):
    return pl.pallas_call(
        finish_kernel,
        in_specs=[pl.BlockSpec(memory_space=VMEM)] * 4,
        out_specs=pl.BlockSpec(memory_space=VMEM),
        out_shape=jax.ShapeDtypeStruct(own.shape, BF),
        name="finish",
    )(own, *arrived)


def slab_product(piece, place, values, rows, cols, counts):
    rows_dev, width = piece.shape
    quarter = jnp.concatenate(gather_side(piece, along_z), axis=0)
    quarter = quarter.reshape(SIDE, rows_dev, width)
    own_slab = gather_side(quarter, along_y)
    low = [lax.ppermute(c, "blk", along_blk(1)) for c in own_slab]
    high = [lax.ppermute(c, "blk", along_blk(-1)) for c in own_slab]
    own, *sends = aggregate(place, own_slab + low + high, values, rows, cols, counts)
    arrived = [lax.ppermute(s, "team", along_y(k + 1)) for k, s in enumerate(sends)]
    kept, *sends = fold(place, own, arrived)
    return kept, [lax.ppermute(s, "team", along_z(k + 1)) for k, s in enumerate(sends)]


def on_device(features, weight, grad_out, block_vals, block_rows, block_cols, block_counts):
    member = lax.axis_index("team")
    place = jnp.stack([member // SIDE, member % SIDE]).astype(jnp.int32)
    values, rows, cols, counts = block_vals[0], block_rows[0], block_cols[0], block_counts[0]
    kept, arrived = slab_product(features, place, values, rows, cols, counts)
    activations, back_rows, local_grad = dense(kept, arrived, weight, grad_out)
    kept, arrived = slab_product(back_rows, place, values, rows, cols, counts)
    grad_feats = finish(kept, arrived)
    everyone = ("blk", "team")
    devices = lax.axis_size("blk") * lax.axis_size("team")
    nodes = features.shape[0] * devices
    share = weight.shape[0] // devices
    shares = lax.all_to_all(
        local_grad.reshape(devices, share, -1), everyone, 0, 0, tiled=True
    )
    mine = jnp.sum(shares, axis=0, keepdims=True) * nodes ** (-0.5)
    grad_weight = lax.all_to_all(
        jnp.broadcast_to(mine, shares.shape), everyone, 0, 0, tiled=True
    ).reshape(weight.shape)
    return (activations, grad_feats, grad_weight)


def solution(mesh):
    lanes = P(("blk", "team"))
    return jax.shard_map(
        on_device,
        mesh=mesh,
        in_specs=(lanes, P(), lanes, lanes, lanes, lanes, lanes),
        out_specs=(lanes, lanes, P()),
        check_vma=False,
    )
```

time: 623 us -> 181 us (0.29)
  waiting for transfers between devices: 531 us -> 56.8 us
  starting transfers between devices: 2.64 us -> 96.8 us
  matrix products: 34.2 us -> 0 us
  local copies, waits for them, and re-layouts: 31.3 us -> 7.53 us
  Pallas kernels: 0 us -> 16.8 us
  between operations: 14 us -> 0.82 us
  other arithmetic: 8.71 us -> 2.19 us
    psum x1 -> x0, waiting for transfers between devices: 217 us -> none  [on_device(): grad_weight = lax.psum(local_grad, ('blk', 'team')) * node_total ** (-0.5)]
    reduce_scatter x2 -> x0, waiting for transfers between devices: 177 us -> none  [the longest x1 89.6 us: on_device(): lax.psum_scatter(grad_partial, 'team', scatter_dimension=0, tiled=True)]
    all_gather x2 -> x0, waiting for transfers between devices: 110 us -> none  [the longest x1 59.1 us: on_device(): slab_feats = lax.all_gather(features, 'team', axis=0, tiled=True)]
    ppermute x4 -> x40, starting transfers between devices: 2.26 us -> 69.4 us  [the longest x12 30.9 us: gather_side(): lax.ppermute(block, 'team', route(-k))]
    dot_general x15 -> x0, matrix products: 34.2 us -> none  [the longest x3 9.7 us: spread_back(): jnp.dot(select, products.reshape(slot_count, -1), precision=lax.Precision...]
    all_to_all x0 -> x2, starting transfers between devices: none -> 27.3 us  [the longest x1 15.4 us: on_device(): lax.all_to_all(jnp.broadcast_to(mine, shares.shape), everyone, 0, 0, tile...]
    ppermute x4 -> x40, waiting for transfers between devices: 25.7 us -> 49.3 us  [the longest x6 18.3 us: slab_product(): lax.ppermute(s, 'team', along_y(k + 1))]
    pallas_call x0 -> x6, Pallas kernels: none -> 16.8 us  [the longest x2 13 us: aggregate(): pl.pallas_call(aggregate_kernel, in_specs=[pl.BlockSpec(memory_space=SMEM...]
  transfers between devices with their start and end apart: 9 -> 42, of which waited for: 8 -> 19; matrix products, arithmetic and copies ran while one was open for 3% -> 2% of each run, Pallas kernels for 0% -> 5%
where the time goes in v1:
time: 181 us
  starting transfers between devices  96.8 us (53%)
  waiting for transfers between devices  56.8 us (31%)
  Pallas kernels  16.8 us (9%)
  local copies, waits for them, and re-layouts  7.53 us (4%)
  other arithmetic  2.19 us (1%)
    ppermute x12, starting transfers between devices, gather_side(): lax.ppermute(block, 'team', route(-k))  30.9 us
    ppermute x6, starting transfers between devices, slab_product(): lax.ppermute(s, 'team', along_z(k + 1))  19.2 us
    ppermute x6, waiting for transfers between devices, slab_product(): lax.ppermute(s, 'team', along_y(k + 1))  18.3 us
    ppermute x12, waiting for transfers between devices, gather_side(): lax.ppermute(block, 'team', route(-k))  18.2 us
    all_to_all x1, starting transfers between devices, on_device(): lax.all_to_all(jnp.broadcast_to(mine, shares.shape), everyone, 0, 0, tile...  15.4 us
    pallas_call x2, Pallas kernels, aggregate(): pl.pallas_call(aggregate_kernel, in_specs=[pl.BlockSpec(memory_space=SMEM...  13 us
    ppermute x6, starting transfers between devices, slab_product(): lax.ppermute(s, 'team', along_y(k + 1))  12.4 us
    all_to_all x1, starting transfers between devices, on_device(): lax.all_to_all(local_grad.reshape(devices, share, -1), everyone, 0, 0, ti...  12 us
  transfers between devices with their start and end apart: 42, of which 19 were waited for; matrix products, arithmetic and copies ran while one was open for 2% of the time, Pallas kernels for 5%

profile of v1, /device:TPU:2, one launch (start us, length us, event | category | flops | bytes accessed | tf_op | source)
XLA Modules:
  0.0 181.0 jit_solution(3797980625952479475)
XLA Ops:
  0.6 7.3 %collective-permute-start.1 = (bf16[128,256]{1,0:T(8,128)(2,1)}, bf16[128,256]{1,0:T(8,128)(2,1)S(1)}, u32[]{:S(2)}, u32[]{:S(2)}) collective-permute-start(bf16[128,256]{1,0:T(8,128)(2,1)} %param.7), channel_id=1, source_target_pairs={{0,2},{1,3},{2,0},{3,1},{4,6},{5,7},{6,4},{7,5},{8,10},{9,11},{10,... | collective-permute-start | bytes 196616 | tf_op jit(solution)/shard_map/ppermute | solution.py:30
  7.9 2.9 %collective-permute-start.2 = (bf16[128,256]{1,0:T(8,128)(2,1)}, bf16[128,256]{1,0:T(8,128)(2,1)S(1)}, u32[]{:S(2)}, u32[]{:S(2)}) collective-permute-start(bf16[128,256]{1,0:T(8,128)(2,1)} %param.7), channel_id=1, source_target_pairs={{0,1},{1,2},{2,3},{3,0},{4,5},{5,6},{6,7},{7,4},{8,9},{9,10},{10,1... | collective-permute-start | bytes 196616 | tf_op jit(solution)/shard_map/ppermute | solution.py:30
  10.8 4.2 %collective-permute-done = bf16[128,256]{1,0:T(8,128)(2,1)S(1)} collective-permute-done((bf16[128,256]{1,0:T(8,128)(2,1)}, bf16[128,256]{1,0:T(8,128)(2,1)S(1)}, u32[]{:S(2)}, u32[]{:S(2)}) %collective-permute-start) | collective-permute-done | bytes 65568 | tf_op jit(solution)/shard_map/ppermute | solution.py:30
  15.0 0.9 pad_maximum_fusion
  15.9 1.7 collective-permute-start.5
  17.6 2.9 %collective-permute-start.4 = (bf16[4,128,256]{2,1,0:T(8,128)(2,1)S(1)}, bf16[4,128,256]{2,1,0:T(8,128)(2,1)S(1)}, u32[]{:S(2)}, u32[]{:S(2)}) collective-permute-start(bf16[4,128,256]{2,1,0:T(8,128)(2,1)S(1)} %bitcast.18), channel_id=1, source_target_pairs={{0,8},{1,9},{2,10},{3,11},{4,12},{5,13},{6,14},{7,15},{8,0},{9,1},... | collective-permute-start | bytes 786440 | tf_op jit(solution)/shard_map/ppermute | solution.py:30
  20.7 1.3 collective-permute-start.3
  22.0 3.4 %collective-permute-done.5.refs_3_ = bf16[4,128,256]{2,1,0:T(8,128)(2,1)S(1)} collective-permute-done((bf16[4,128,256]{2,1,0:T(8,128)(2,1)S(1)}, bf16[4,128,256]{2,1,0:T(8,128)(2,1)S(1)}, u32[]{:S(2)}, u32[]{:S(2)}) %collective-permute-start.5) | collective-permute-done | bytes 262176 | tf_op jit(solution)/shard_map/ppermute | solution.py:30
  25.5 0.5 collective-permute-start.9
  26.0 6.3 %collective-permute-done.4.refs_2_ = bf16[4,128,256]{2,1,0:T(8,128)(2,1)S(1)} collective-permute-done((bf16[4,128,256]{2,1,0:T(8,128)(2,1)S(1)}, bf16[4,128,256]{2,1,0:T(8,128)(2,1)S(1)}, u32[]{:S(2)}, u32[]{:S(2)}) %collective-permute-start.4) | collective-permute-done | bytes 262176 | tf_op jit(solution)/shard_map/ppermute | solution.py:30
  32.8 1.2 collective-permute-start.11
  34.1 0.7 copy_bitcast_fusion.1
  34.8 1.4 collective-permute-done.12.refs_10_
  36.2 1.9 %collective-permute-done.8.refs_6_ = bf16[4,128,256]{2,1,0:T(8,128)(2,1)S(1)} collective-permute-done((bf16[4,128,256]{2,1,0:T(8,128)(2,1)S(1)}, bf16[4,128,256]{2,1,0:T(8,128)(2,1)S(1)}, u32[]{:S(2)}, u32[]{:S(2)}) %collective-permute-start.8) | collective-permute-done | bytes 262176 | tf_op jit(solution)/shard_map/ppermute | solution.py:186
  38.1 0.9 collective-permute-done.11.refs_9_
  39.0 1.9 %collective-permute-done.7.refs_5_ = bf16[4,128,256]{2,1,0:T(8,128)(2,1)S(1)} collective-permute-done((bf16[4,128,256]{2,1,0:T(8,128)(2,1)S(1)}, bf16[4,128,256]{2,1,0:T(8,128)(2,1)S(1)}, u32[]{:S(2)}, u32[]{:S(2)}) %collective-permute-start.7) | collective-permute-done | bytes 262176 | tf_op jit(solution)/shard_map/ppermute | solution.py:186
  40.9 1.4 copy-done
  42.3 0.7 copy-done.5
  43.0 6.3 %aggregate.2 = (f32[4,128,256]{2,1,0:T(8,128)S(1)}, bf16[4,128,256]{2,1,0:T(8,128)(2,1)S(1)}, bf16[4,128,256]{2,1,0:T(8,128)(2,1)S(1)}, bf16[4,128,256]{2,1,0:T(8,128)(2,1)S(1)}) custom-call(s32[2]{0:T(128)S(1)} %pad_add_fusion.place, s32[3,16]{1,0:T(4,128)S(1)} %get-tuple-element.42.rows, s32[3,16]{1,0:T(4,128)S(1)} %get-tuple-element.41.cols, ...), custom_call_target="tpu_custom_call" | custom-call | tf_op jit(solution)/shard_map/aggregate/pallas_call | solution.py:85
  49.8 3.6 %collective-permute-start.15 = (bf16[4,128,256]{2,1,0:T(8,128)(2,1)S(1)}, bf16[4,128,256]{2,1,0:T(8,128)(2,1)S(1)}, u32[]{:S(2)}, u32[]{:S(2)}) collective-permute-start(bf16[4,128,256]{2,1,0:T(8,128)(2,1)S(1)} %get-tuple-element.24), channel_id=1, source_target_pairs={{0,8},{1,9},{2,10},{3,11},{4,12},{5,13},{6,14},{7,15},{8,0},{9,1},... | collective-permute-start | bytes 786440 | tf_op jit(solution)/shard_map/ppermute | solution.py:189
  53.4 2.5 %collective-permute-start.16 = (bf16[4,128,256]{2,1,0:T(8,128)(2,1)S(1)}, bf16[4,128,256]{2,1,0:T(8,128)(2,1)S(1)}, u32[]{:S(2)}, u32[]{:S(2)}) collective-permute-start(bf16[4,128,256]{2,1,0:T(8,128)(2,1)S(1)} %get-tuple-element.25), channel_id=1, source_target_pairs={{0,12},{1,13},{2,14},{3,15},{4,0},{5,1},{6,2},{7,3},{8,4},{9,5},{1... | collective-permute-start | bytes 786440 | tf_op jit(solution)/shard_map/ppermute | solution.py:189
  55.9 2.5 %collective-permute-done.14.one = bf16[4,128,256]{2,1,0:T(8,128)(2,1)S(1)} collective-permute-done((bf16[4,128,256]{2,1,0:T(8,128)(2,1)S(1)}, bf16[4,128,256]{2,1,0:T(8,128)(2,1)S(1)}, u32[]{:S(2)}, u32[]{:S(2)}) %collective-permute-start.14) | collective-permute-done | bytes 262176 | tf_op jit(solution)/shard_map/ppermute | solution.py:189
  58.4 6.0 %collective-permute-done.15.two = bf16[4,128,256]{2,1,0:T(8,128)(2,1)S(1)} collective-permute-done((bf16[4,128,256]{2,1,0:T(8,128)(2,1)S(1)}, bf16[4,128,256]{2,1,0:T(8,128)(2,1)S(1)}, u32[]{:S(2)}, u32[]{:S(2)}) %collective-permute-start.15) | collective-permute-done | bytes 262176 | tf_op jit(solution)/shard_map/ppermute | solution.py:189
  64.4 0.7 fold.2
  65.1 0.7 collective-permute-start.17
  65.7 4.9 %collective-permute-start.18 = (bf16[128,256]{1,0:T(8,128)(2,1)S(1)}, bf16[128,256]{1,0:T(8,128)(2,1)S(1)}, u32[]{:S(2)}, u32[]{:S(2)}) collective-permute-start(bf16[128,256]{1,0:T(8,128)(2,1)S(1)} %get-tuple-element.28), channel_id=1, source_target_pairs={{0,2},{1,3},{2,0},{3,1},{4,6},{5,7},{6,4},{7,5},{8,10},{9,11},{10,... | collective-permute-start | bytes 196616 | tf_op jit(solution)/shard_map/ppermute | solution.py:191
  70.6 3.1 %collective-permute-start.19 = (bf16[128,256]{1,0:T(8,128)(2,1)S(1)}, bf16[128,256]{1,0:T(8,128)(2,1)S(1)}, u32[]{:S(2)}, u32[]{:S(2)}) collective-permute-start(bf16[128,256]{1,0:T(8,128)(2,1)S(1)} %get-tuple-element.29), channel_id=1, source_target_pairs={{0,3},{1,0},{2,1},{3,2},{4,7},{5,4},{6,5},{7,6},{8,11},{9,8},{10,9... | collective-permute-start | bytes 196616 | tf_op jit(solution)/shard_map/ppermute | solution.py:191
  73.7 1.7 collective-permute-done.18.two
  75.4 2.0 %collective-permute-done.19.three = bf16[128,256]{1,0:T(8,128)(2,1)S(1)} collective-permute-done((bf16[128,256]{1,0:T(8,128)(2,1)S(1)}, bf16[128,256]{1,0:T(8,128)(2,1)S(1)}, u32[]{:S(2)}, u32[]{:S(2)}) %collective-permute-start.19) | collective-permute-done | bytes 65568 | tf_op jit(solution)/shard_map/ppermute | solution.py:191
  77.4 0.8 dense.1
  78.2 1.9 %collective-permute-start.22 = (bf16[128,256]{1,0:T(8,128)(2,1)S(1)}, bf16[128,256]{1,0:T(8,128)(2,1)S(1)}, u32[]{:S(2)}, u32[]{:S(2)}) collective-permute-start(bf16[128,256]{1,0:T(8,128)(2,1)S(1)} %get-tuple-element.31), channel_id=1, source_target_pairs={{0,1},{1,2},{2,3},{3,0},{4,5},{5,6},{6,7},{7,4},{8,9},{9,10},{10,1... | collective-permute-start | bytes 196616 | tf_op jit(solution)/shard_map/ppermute | solution.py:30
  80.1 4.2 %collective-permute-start.21 = (bf16[128,256]{1,0:T(8,128)(2,1)S(1)}, bf16[128,256]{1,0:T(8,128)(2,1)S(1)}, u32[]{:S(2)}, u32[]{:S(2)}) collective-permute-start(bf16[128,256]{1,0:T(8,128)(2,1)S(1)} %get-tuple-element.31), channel_id=1, source_target_pairs={{0,2},{1,3},{2,0},{3,1},{4,6},{5,7},{6,4},{7,5},{8,10},{9,11},{10,... | collective-permute-start | bytes 196616 | tf_op jit(solution)/shard_map/ppermute | solution.py:30
  84.3 2.4 %collective-permute-start.20 = (bf16[128,256]{1,0:T(8,128)(2,1)S(1)}, bf16[128,256]{1,0:T(8,128)(2,1)S(1)}, u32[]{:S(2)}, u32[]{:S(2)}) collective-permute-start(bf16[128,256]{1,0:T(8,128)(2,1)S(1)} %get-tuple-element.31), channel_id=1, source_target_pairs={{0,3},{1,0},{2,1},{3,2},{4,7},{5,4},{6,5},{7,6},{8,11},{9,8},{10,9... | collective-permute-start | bytes 196616 | tf_op jit(solution)/shard_map/ppermute | solution.py:30
  86.7 2.3 %collective-permute-done.21 = bf16[128,256]{1,0:T(8,128)(2,1)S(1)} collective-permute-done((bf16[128,256]{1,0:T(8,128)(2,1)S(1)}, bf16[128,256]{1,0:T(8,128)(2,1)S(1)}, u32[]{:S(2)}, u32[]{:S(2)}) %collective-permute-start.21) | collective-permute-done | bytes 65568 | tf_op jit(solution)/shard_map/ppermute | solution.py:30
  89.0 0.9 collective-permute-done.20
  89.9 2.1 %collective-permute-start.25 = (bf16[4,128,256]{2,1,0:T(8,128)(2,1)S(1)}, bf16[4,128,256]{2,1,0:T(8,128)(2,1)S(1)}, u32[]{:S(2)}, u32[]{:S(2)}) collective-permute-start(bf16[4,128,256]{2,1,0:T(8,128)(2,1)S(1)} %bitcast.22), channel_id=1, source_target_pairs={{0,4},{1,5},{2,6},{3,7},{4,8},{5,9},{6,10},{7,11},{8,12},{9,13},{1... | collective-permute-start | bytes 786440 | tf_op jit(solution)/shard_map/ppermute | solution.py:30
  92.0 1.0 copy.10
  92.9 12.0 %all-to-all-start = ((f32[256,1,256]{2,1,0:T(1,128)}), f32[256,1,256]{2,1,0:T(1,128)}, u32[]{:S(2)}, u32[]{:S(2)}) async-start(f32[256,1,256]{2,1,0:T(1,128)} %copy.10), calls=%async_computation | async-start | bytes 524288 | tf_op jit(solution)/shard_map/all_to_all | solution.py:206
  105.1 3.2 %collective-permute-start.24 = (bf16[4,128,256]{2,1,0:T(8,128)(2,1)S(1)}, bf16[4,128,256]{2,1,0:T(8,128)(2,1)S(1)}, u32[]{:S(2)}, u32[]{:S(2)}) collective-permute-start(bf16[4,128,256]{2,1,0:T(8,128)(2,1)S(1)} %bitcast.24), channel_id=1, source_target_pairs={{0,8},{1,9},{2,10},{3,11},{4,12},{5,13},{6,14},{7,15},{8,0},{9,1},... | collective-permute-start | bytes 786440 | tf_op jit(solution)/shard_map/ppermute | solution.py:30
  108.3 1.2 collective-permute-start.23
  109.5 1.5 collective-permute-start.33
  110.9 7.5 %all-to-all-done = f32[256,1,256]{2,1,0:T(1,128)} async-done(((f32[256,1,256]{2,1,0:T(1,128)}), f32[256,1,256]{2,1,0:T(1,128)}, u32[]{:S(2)}, u32[]{:S(2)}) %all-to-all-start) | async-done | bytes 262176 | tf_op jit(solution)/shard_map/all_to_all | solution.py:206
  118.5 1.2 reduce_sum.9
  120.0 1.7 collective-permute-start.32
  121.8 1.1 collective-permute-done.23.refs_1_
  122.8 0.7 collective-permute-start.31
  123.5 0.8 broadcast_in_dim.2
  124.4 15.4 %all-to-all-start.1 = ((f32[256,1,256]{2,1,0:T(1,128)}), f32[256,1,256]{2,1,0:T(1,128)}, u32[]{:S(2)}, u32[]{:S(2)}) async-start(f32[256,1,256]{2,1,0:T(1,128)} %broadcast_in_dim.2), calls=%async_computation.1 | async-start | bytes 524288 | tf_op jit(solution)/shard_map/all_to_all | solution.py:210
  139.8 6.7 %aggregate.3 = (f32[4,128,256]{2,1,0:T(8,128)S(1)}, bf16[4,128,256]{2,1,0:T(8,128)(2,1)S(1)}, bf16[4,128,256]{2,1,0:T(8,128)(2,1)S(1)}, bf16[4,128,256]{2,1,0:T(8,128)(2,1)S(1)}) custom-call(s32[2]{0:T(128)S(1)} %pad_add_fusion.place, s32[3,16]{1,0:T(4,128)S(1)} %get-tuple-element.42.rows, s32[3,16]{1,0:T(4,128)S(1)} %get-tuple-element.41.cols, ...), custom_call_target="tpu_custom_call" | custom-call | tf_op jit(solution)/shard_map/aggregate/pallas_call | solution.py:85
  146.5 1.7 collective-permute-start.34
  148.2 2.9 %collective-permute-start.35 = (bf16[4,128,256]{2,1,0:T(8,128)(2,1)S(1)}, bf16[4,128,256]{2,1,0:T(8,128)(2,1)S(1)}, u32[]{:S(2)}, u32[]{:S(2)}) collective-permute-start(bf16[4,128,256]{2,1,0:T(8,128)(2,1)S(1)} %get-tuple-element.34), channel_id=1, source_target_pairs={{0,8},{1,9},{2,10},{3,11},{4,12},{5,13},{6,14},{7,15},{8,0},{9,1},... | collective-permute-start | bytes 786440 | tf_op jit(solution)/shard_map/ppermute | solution.py:189
  151.1 1.2 collective-permute-start.36
  152.4 4.2 %collective-permute-done.34.one = bf16[4,128,256]{2,1,0:T(8,128)(2,1)S(1)} collective-permute-done((bf16[4,128,256]{2,1,0:T(8,128)(2,1)S(1)}, bf16[4,128,256]{2,1,0:T(8,128)(2,1)S(1)}, u32[]{:S(2)}, u32[]{:S(2)}) %collective-permute-start.34) | collective-permute-done | bytes 262176 | tf_op jit(solution)/shard_map/ppermute | solution.py:189
  156.5 5.6 %collective-permute-done.35.two = bf16[4,128,256]{2,1,0:T(8,128)(2,1)S(1)} collective-permute-done((bf16[4,128,256]{2,1,0:T(8,128)(2,1)S(1)}, bf16[4,128,256]{2,1,0:T(8,128)(2,1)S(1)}, u32[]{:S(2)}, u32[]{:S(2)}) %collective-permute-start.35) | collective-permute-done | bytes 262176 | tf_op jit(solution)/shard_map/ppermute | solution.py:189
  162.2 0.7 fold.3
  162.8 0.6 copy-done.2
  163.5 3.0 %collective-permute-start.37 = (bf16[128,256]{1,0:T(8,128)(2,1)S(1)}, bf16[128,256]{1,0:T(8,128)(2,1)S(1)}, u32[]{:S(2)}, u32[]{:S(2)}) collective-permute-start(bf16[128,256]{1,0:T(8,128)(2,1)S(1)} %get-tuple-element.37), channel_id=1, source_target_pairs={{0,1},{1,2},{2,3},{3,0},{4,5},{5,6},{6,7},{7,4},{8,9},{9,10},{10,1... | collective-permute-start | bytes 196616 | tf_op jit(solution)/shard_map/ppermute | solution.py:191
  166.5 4.8 %collective-permute-start.38 = (bf16[128,256]{1,0:T(8,128)(2,1)S(1)}, bf16[128,256]{1,0:T(8,128)(2,1)S(1)}, u32[]{:S(2)}, u32[]{:S(2)}) collective-permute-start(bf16[128,256]{1,0:T(8,128)(2,1)S(1)} %get-tuple-element.38), channel_id=1, source_target_pairs={{0,2},{1,3},{2,0},{3,1},{4,6},{5,7},{6,4},{7,5},{8,10},{9,11},{10,... | collective-permute-start | bytes 196616 | tf_op jit(solution)/shard_map/ppermute | solution.py:191
  171.3 2.7 %collective-permute-start.39 = (bf16[128,256]{1,0:T(8,128)(2,1)S(1)}, bf16[128,256]{1,0:T(8,128)(2,1)S(1)}, u32[]{:S(2)}, u32[]{:S(2)}) collective-permute-start(bf16[128,256]{1,0:T(8,128)(2,1)S(1)} %get-tuple-element.39), channel_id=1, source_target_pairs={{0,3},{1,0},{2,1},{3,2},{4,7},{5,4},{6,5},{7,6},{8,11},{9,8},{10,9... | collective-permute-start | bytes 196616 | tf_op jit(solution)/shard_map/ppermute | solution.py:191
  174.1 1.7 collective-permute-done.38.two
  175.8 1.3 collective-permute-done.39.three
  177.1 0.6 copy-done.9
  177.7 1.6 finish.1
  179.3 1.7 copy.17
  (55 shorter events, 1.9 us)
Async XLA Ops:
  0.6 10.2 %collective-permute-start.1 = (bf16[128,256]{1,0:T(8,128)(2,1)}, bf16[128,256]{1,0:T(8,128)(2,1)S(1)}, u32[]{:S(2)}, u32[]{:S(2)}) collective-permute-start(bf16[128,256]{1,0:T(8,128)(2,1)} %param.7), channel_id=1, source_target_pairs={{0,2},{1,3},{2,0},{3,1},{4,6},{5,7},{6,4},{7,5},{8,10},{9,11},{10,... | collective-permute-start | bytes 196616 | tf_op jit(solution)/shard_map/ppermute | solution.py:30
  7.9 7.1 %collective-permute-start = (bf16[128,256]{1,0:T(8,128)(2,1)}, bf16[128,256]{1,0:T(8,128)(2,1)S(1)}, u32[]{:S(2)}, u32[]{:S(2)}) collective-permute-start(bf16[128,256]{1,0:T(8,128)(2,1)} %param.7), channel_id=1, source_target_pairs={{0,3},{1,0},{2,1},{3,2},{4,7},{5,4},{6,5},{7,6},{8,11},{9,8},{10,9... | collective-permute-start | bytes 196616 | tf_op jit(solution)/shard_map/ppermute | solution.py:30
  7.9 7.1 %collective-permute-start.2 = (bf16[128,256]{1,0:T(8,128)(2,1)}, bf16[128,256]{1,0:T(8,128)(2,1)S(1)}, u32[]{:S(2)}, u32[]{:S(2)}) collective-permute-start(bf16[128,256]{1,0:T(8,128)(2,1)} %param.7), channel_id=1, source_target_pairs={{0,1},{1,2},{2,3},{3,0},{4,5},{5,6},{6,7},{7,4},{8,9},{9,10},{10,1... | collective-permute-start | bytes 196616 | tf_op jit(solution)/shard_map/ppermute | solution.py:30
  15.9 9.6 %collective-permute-start.5 = (bf16[4,128,256]{2,1,0:T(8,128)(2,1)S(1)}, bf16[4,128,256]{2,1,0:T(8,128)(2,1)S(1)}, u32[]{:S(2)}, u32[]{:S(2)}) collective-permute-start(bf16[4,128,256]{2,1,0:T(8,128)(2,1)S(1)} %bitcast.16), channel_id=1, source_target_pairs={{0,4},{1,5},{2,6},{3,7},{4,8},{5,9},{6,10},{7,11},{8,12},{9,13},{1... | collective-permute-start | bytes 786440 | tf_op jit(solution)/shard_map/ppermute | solution.py:30
  17.5 7.9 %collective-permute-start.10 = (bf16[4,128,256]{2,1,0:T(8,128)(2,1)S(1)}, bf16[4,128,256]{2,1,0:T(8,128)(2,1)S(1)}, u32[]{:S(2)}, u32[]{:S(2)}) collective-permute-start(bf16[4,128,256]{2,1,0:T(8,128)(2,1)S(1)} %bitcast.17), channel_id=1, source_target_pairs={{0,240},{16,0},{32,16},{48,32},{64,48},{80,64},{96,80},{112,96},{1... | collective-permute-start | bytes 786440 | tf_op jit(solution)/shard_map/ppermute | solution.py:187
  17.6 14.7 %collective-permute-start.4 = (bf16[4,128,256]{2,1,0:T(8,128)(2,1)S(1)}, bf16[4,128,256]{2,1,0:T(8,128)(2,1)S(1)}, u32[]{:S(2)}, u32[]{:S(2)}) collective-permute-start(bf16[4,128,256]{2,1,0:T(8,128)(2,1)S(1)} %bitcast.18), channel_id=1, source_target_pairs={{0,8},{1,9},{2,10},{3,11},{4,12},{5,13},{6,14},{7,15},{8,0},{9,1},... | collective-permute-start | bytes 786440 | tf_op jit(solution)/shard_map/ppermute | solution.py:30
  20.5 11.8 %collective-permute-start.6 = (bf16[4,128,256]{2,1,0:T(8,128)(2,1)S(1)}, bf16[4,128,256]{2,1,0:T(8,128)(2,1)S(1)}, u32[]{:S(2)}, u32[]{:S(2)}) collective-permute-start(bf16[4,128,256]{2,1,0:T(8,128)(2,1)S(1)} %bitcast.19), channel_id=1, source_target_pairs={{0,16},{16,32},{32,48},{48,64},{64,80},{80,96},{96,112},{112,128},... | collective-permute-start | bytes 786440 | tf_op jit(solution)/shard_map/ppermute | solution.py:186
  20.7 12.1 %collective-permute-start.3 = (bf16[4,128,256]{2,1,0:T(8,128)(2,1)S(1)}, bf16[4,128,256]{2,1,0:T(8,128)(2,1)S(1)}, u32[]{:S(2)}, u32[]{:S(2)}) collective-permute-start(bf16[4,128,256]{2,1,0:T(8,128)(2,1)S(1)} %bitcast.20), channel_id=1, source_target_pairs={{0,12},{1,13},{2,14},{3,15},{4,0},{5,1},{6,2},{7,3},{8,4},{9,5},{1... | collective-permute-start | bytes 786440 | tf_op jit(solution)/shard_map/ppermute | solution.py:30
  25.5 8.6 %collective-permute-start.13 = (bf16[4,128,256]{2,1,0:T(8,128)(2,1)S(1)}, bf16[4,128,256]{2,1,0:T(8,128)(2,1)S(1)}, u32[]{:S(2)}, u32[]{:S(2)}) collective-permute-start(bf16[4,128,256]{2,1,0:T(8,128)(2,1)S(1)} %collective-permute-done.5.refs_3_), channel_id=1, source_target_pairs={{0,240},{16,0},{32,16},{48,32},{64,48},{80,64},{96,80},{112,96},{1... | collective-permute-start | bytes 786440 | tf_op jit(solution)/shard_map/ppermute | solution.py:187
  25.5 9.3 %collective-permute-start.9 = (bf16[4,128,256]{2,1,0:T(8,128)(2,1)S(1)}, bf16[4,128,256]{2,1,0:T(8,128)(2,1)S(1)}, u32[]{:S(2)}, u32[]{:S(2)}) collective-permute-start(bf16[4,128,256]{2,1,0:T(8,128)(2,1)S(1)} %collective-permute-done.5.refs_3_), channel_id=1, source_target_pairs={{0,16},{16,32},{32,48},{48,64},{64,80},{80,96},{96,112},{112,128},... | collective-permute-start | bytes 786440 | tf_op jit(solution)/shard_map/ppermute | solution.py:186
  32.3 3.9 %collective-permute-start.12 = (bf16[4,128,256]{2,1,0:T(8,128)(2,1)S(1)}, bf16[4,128,256]{2,1,0:T(8,128)(2,1)S(1)}, u32[]{:S(2)}, u32[]{:S(2)}) collective-permute-start(bf16[4,128,256]{2,1,0:T(8,128)(2,1)S(1)} %collective-permute-done.4.refs_2_), channel_id=1, source_target_pairs={{0,240},{16,0},{32,16},{48,32},{64,48},{80,64},{96,80},{112,96},{1... | collective-permute-start | bytes 786440 | tf_op jit(solution)/shard_map/ppermute | solution.py:187
  32.3 5.8 %collective-permute-start.8 = (bf16[4,128,256]{2,1,0:T(8,128)(2,1)S(1)}, bf16[4,128,256]{2,1,0:T(8,128)(2,1)S(1)}, u32[]{:S(2)}, u32[]{:S(2)}) collective-permute-start(bf16[4,128,256]{2,1,0:T(8,128)(2,1)S(1)} %collective-permute-done.4.refs_2_), channel_id=1, source_target_pairs={{0,16},{16,32},{32,48},{48,64},{64,80},{80,96},{96,112},{112,128},... | collective-permute-start | bytes 786440 | tf_op jit(solution)/shard_map/ppermute | solution.py:186
  32.8 6.2 %collective-permute-start.11 = (bf16[4,128,256]{2,1,0:T(8,128)(2,1)S(1)}, bf16[4,128,256]{2,1,0:T(8,128)(2,1)S(1)}, u32[]{:S(2)}, u32[]{:S(2)}) collective-permute-start(bf16[4,128,256]{2,1,0:T(8,128)(2,1)S(1)} %collective-permute-done.3.refs_1_), channel_id=1, source_target_pairs={{0,240},{16,0},{32,16},{48,32},{64,48},{80,64},{96,80},{112,96},{1... | collective-permute-start | bytes 786440 | tf_op jit(solution)/shard_map/ppermute | solution.py:187
  34.0 6.9 %collective-permute-start.7 = (bf16[4,128,256]{2,1,0:T(8,128)(2,1)S(1)}, bf16[4,128,256]{2,1,0:T(8,128)(2,1)S(1)}, u32[]{:S(2)}, u32[]{:S(2)}) collective-permute-start(bf16[4,128,256]{2,1,0:T(8,128)(2,1)S(1)} %collective-permute-done.3.refs_1_), channel_id=1, source_target_pairs={{0,16},{16,32},{32,48},{48,64},{64,80},{80,96},{96,112},{112,128},... | collective-permute-start | bytes 786440 | tf_op jit(solution)/shard_map/ppermute | solution.py:186
  40.9 1.4 copy-start
  42.3 0.7 copy-start.5
  42.9 34.5 %copy-start.3 = (bf16[256,256]{1,0:T(8,128)(2,1)S(1)}, bf16[256,256]{1,0:T(8,128)(2,1)}, u32[]{:S(2)}) copy-start(bf16[256,256]{1,0:T(8,128)(2,1)} %weight.1) | copy-start | bytes 393220
  42.9 34.5 %copy-start.4 = (bf16[128,256]{1,0:T(8,128)(2,1)S(1)}, bf16[128,256]{1,0:T(8,128)(2,1)}, u32[]{:S(2)}) copy-start(bf16[128,256]{1,0:T(8,128)(2,1)} %grad_out.1) | copy-start | bytes 196612
  49.3 9.1 %collective-permute-start.14 = (bf16[4,128,256]{2,1,0:T(8,128)(2,1)S(1)}, bf16[4,128,256]{2,1,0:T(8,128)(2,1)S(1)}, u32[]{:S(2)}, u32[]{:S(2)}) collective-permute-start(bf16[4,128,256]{2,1,0:T(8,128)(2,1)S(1)} %get-tuple-element.23), channel_id=1, source_target_pairs={{0,4},{1,5},{2,6},{3,7},{4,8},{5,9},{6,10},{7,11},{8,12},{9,13},{1... | collective-permute-start | bytes 786440 | tf_op jit(solution)/shard_map/ppermute | solution.py:189
  49.8 14.6 %collective-permute-start.15 = (bf16[4,128,256]{2,1,0:T(8,128)(2,1)S(1)}, bf16[4,128,256]{2,1,0:T(8,128)(2,1)S(1)}, u32[]{:S(2)}, u32[]{:S(2)}) collective-permute-start(bf16[4,128,256]{2,1,0:T(8,128)(2,1)S(1)} %get-tuple-element.24), channel_id=1, source_target_pairs={{0,8},{1,9},{2,10},{3,11},{4,12},{5,13},{6,14},{7,15},{8,0},{9,1},... | collective-permute-start | bytes 786440 | tf_op jit(solution)/shard_map/ppermute | solution.py:189
  53.4 11.1 %collective-permute-start.16 = (bf16[4,128,256]{2,1,0:T(8,128)(2,1)S(1)}, bf16[4,128,256]{2,1,0:T(8,128)(2,1)S(1)}, u32[]{:S(2)}, u32[]{:S(2)}) collective-permute-start(bf16[4,128,256]{2,1,0:T(8,128)(2,1)S(1)} %get-tuple-element.25), channel_id=1, source_target_pairs={{0,12},{1,13},{2,14},{3,15},{4,0},{5,1},{6,2},{7,3},{8,4},{9,5},{1... | collective-permute-start | bytes 786440 | tf_op jit(solution)/shard_map/ppermute | solution.py:189
  65.1 8.6 %collective-permute-start.17 = (bf16[128,256]{1,0:T(8,128)(2,1)S(1)}, bf16[128,256]{1,0:T(8,128)(2,1)S(1)}, u32[]{:S(2)}, u32[]{:S(2)}) collective-permute-start(bf16[128,256]{1,0:T(8,128)(2,1)S(1)} %get-tuple-element.27), channel_id=1, source_target_pairs={{0,1},{1,2},{2,3},{3,0},{4,5},{5,6},{6,7},{7,4},{8,9},{9,10},{10,1... | collective-permute-start | bytes 196616 | tf_op jit(solution)/shard_map/ppermute | solution.py:191
  65.7 9.7 %collective-permute-start.18 = (bf16[128,256]{1,0:T(8,128)(2,1)S(1)}, bf16[128,256]{1,0:T(8,128)(2,1)S(1)}, u32[]{:S(2)}, u32[]{:S(2)}) collective-permute-start(bf16[128,256]{1,0:T(8,128)(2,1)S(1)} %get-tuple-element.28), channel_id=1, source_target_pairs={{0,2},{1,3},{2,0},{3,1},{4,6},{5,7},{6,4},{7,5},{8,10},{9,11},{10,... | collective-permute-start | bytes 196616 | tf_op jit(solution)/shard_map/ppermute | solution.py:191
  70.6 6.8 %collective-permute-start.19 = (bf16[128,256]{1,0:T(8,128)(2,1)S(1)}, bf16[128,256]{1,0:T(8,128)(2,1)S(1)}, u32[]{:S(2)}, u32[]{:S(2)}) collective-permute-start(bf16[128,256]{1,0:T(8,128)(2,1)S(1)} %get-tuple-element.29), channel_id=1, source_target_pairs={{0,3},{1,0},{2,1},{3,2},{4,7},{5,4},{6,5},{7,6},{8,11},{9,8},{10,9... | collective-permute-start | bytes 196616 | tf_op jit(solution)/shard_map/ppermute | solution.py:191
  77.4 62.4 %copy-start.1 = (bf16[1,3,16,128,128]{4,3,2,1,0:T(8,128)(2,1)S(1)}, bf16[1,3,16,128,128]{4,3,2,1,0:T(8,128)(2,1)}, u32[]{:S(2)}) copy-start(bf16[1,3,16,128,128]{4,3,2,1,0:T(8,128)(2,1)} %param.10) | copy-start | bytes 4718596
  77.4 62.4 %copy-start.6 = (s32[1,3]{1,0:T(1,128)S(1)}, s32[1,3]{1,0:T(1,128)}, u32[]{:S(2)}) copy-start(s32[1,3]{1,0:T(1,128)} %param.13) | copy-start | bytes 40
  78.2 8.5 %collective-permute-start.22 = (bf16[128,256]{1,0:T(8,128)(2,1)S(1)}, bf16[128,256]{1,0:T(8,128)(2,1)S(1)}, u32[]{:S(2)}, u32[]{:S(2)}) collective-permute-start(bf16[128,256]{1,0:T(8,128)(2,1)S(1)} %get-tuple-element.31), channel_id=1, source_target_pairs={{0,1},{1,2},{2,3},{3,0},{4,5},{5,6},{6,7},{7,4},{8,9},{9,10},{10,1... | collective-permute-start | bytes 196616 | tf_op jit(solution)/shard_map/ppermute | solution.py:30
  80.1 8.9 %collective-permute-start.21 = (bf16[128,256]{1,0:T(8,128)(2,1)S(1)}, bf16[128,256]{1,0:T(8,128)(2,1)S(1)}, u32[]{:S(2)}, u32[]{:S(2)}) collective-permute-start(bf16[128,256]{1,0:T(8,128)(2,1)S(1)} %get-tuple-element.31), channel_id=1, source_target_pairs={{0,2},{1,3},{2,0},{3,1},{4,6},{5,7},{6,4},{7,5},{8,10},{9,11},{10,... | collective-permute-start | bytes 196616 | tf_op jit(solution)/shard_map/ppermute | solution.py:30
  84.3 5.6 %collective-permute-start.20 = (bf16[128,256]{1,0:T(8,128)(2,1)S(1)}, bf16[128,256]{1,0:T(8,128)(2,1)S(1)}, u32[]{:S(2)}, u32[]{:S(2)}) collective-permute-start(bf16[128,256]{1,0:T(8,128)(2,1)S(1)} %get-tuple-element.31), channel_id=1, source_target_pairs={{0,3},{1,0},{2,1},{3,2},{4,7},{5,4},{6,5},{7,6},{8,11},{9,8},{10,9... | collective-permute-start | bytes 196616 | tf_op jit(solution)/shard_map/ppermute | solution.py:30
  89.9 19.5 %collective-permute-start.25 = (bf16[4,128,256]{2,1,0:T(8,128)(2,1)S(1)}, bf16[4,128,256]{2,1,0:T(8,128)(2,1)S(1)}, u32[]{:S(2)}, u32[]{:S(2)}) collective-permute-start(bf16[4,128,256]{2,1,0:T(8,128)(2,1)S(1)} %bitcast.22), channel_id=1, source_target_pairs={{0,4},{1,5},{2,6},{3,7},{4,8},{5,9},{6,10},{7,11},{8,12},{9,13},{1... | collective-permute-start | bytes 786440 | tf_op jit(solution)/shard_map/ppermute | solution.py:30
  92.9 25.5 %all-to-all-start = ((f32[256,1,256]{2,1,0:T(1,128)}), f32[256,1,256]{2,1,0:T(1,128)}, u32[]{:S(2)}, u32[]{:S(2)}) async-start(f32[256,1,256]{2,1,0:T(1,128)} %copy.10), calls=%async_computation | async-start | bytes 524288 | tf_op jit(solution)/shard_map/all_to_all | solution.py:206
  104.9 14.8 %collective-permute-start.30 = (bf16[4,128,256]{2,1,0:T(8,128)(2,1)S(1)}, bf16[4,128,256]{2,1,0:T(8,128)(2,1)S(1)}, u32[]{:S(2)}, u32[]{:S(2)}) collective-permute-start(bf16[4,128,256]{2,1,0:T(8,128)(2,1)S(1)} %bitcast.23), channel_id=1, source_target_pairs={{0,240},{16,0},{32,16},{48,32},{64,48},{80,64},{96,80},{112,96},{1... | collective-permute-start | bytes 786440 | tf_op jit(solution)/shard_map/ppermute | solution.py:187
  105.1 14.9 %collective-permute-start.24 = (bf16[4,128,256]{2,1,0:T(8,128)(2,1)S(1)}, bf16[4,128,256]{2,1,0:T(8,128)(2,1)S(1)}, u32[]{:S(2)}, u32[]{:S(2)}) collective-permute-start(bf16[4,128,256]{2,1,0:T(8,128)(2,1)S(1)} %bitcast.24), channel_id=1, source_target_pairs={{0,8},{1,9},{2,10},{3,11},{4,12},{5,13},{6,14},{7,15},{8,0},{9,1},... | collective-permute-start | bytes 786440 | tf_op jit(solution)/shard_map/ppermute | solution.py:30
  108.3 13.5 %collective-permute-start.26 = (bf16[4,128,256]{2,1,0:T(8,128)(2,1)S(1)}, bf16[4,128,256]{2,1,0:T(8,128)(2,1)S(1)}, u32[]{:S(2)}, u32[]{:S(2)}) collective-permute-start(bf16[4,128,256]{2,1,0:T(8,128)(2,1)S(1)} %bitcast.25), channel_id=1, source_target_pairs={{0,16},{16,32},{32,48},{48,64},{64,80},{80,96},{96,112},{112,128},... | collective-permute-start | bytes 786440 | tf_op jit(solution)/shard_map/ppermute | solution.py:186
  108.3 14.5 %collective-permute-start.23 = (bf16[4,128,256]{2,1,0:T(8,128)(2,1)S(1)}, bf16[4,128,256]{2,1,0:T(8,128)(2,1)S(1)}, u32[]{:S(2)}, u32[]{:S(2)}) collective-permute-start(bf16[4,128,256]{2,1,0:T(8,128)(2,1)S(1)} %bitcast.26), channel_id=1, source_target_pairs={{0,12},{1,13},{2,14},{3,15},{4,0},{5,1},{6,2},{7,3},{8,4},{9,5},{1... | collective-permute-start | bytes 786440 | tf_op jit(solution)/shard_map/ppermute | solution.py:30
  109.5 14.0 %collective-permute-start.33 = (bf16[4,128,256]{2,1,0:T(8,128)(2,1)S(1)}, bf16[4,128,256]{2,1,0:T(8,128)(2,1)S(1)}, u32[]{:S(2)}, u32[]{:S(2)}) collective-permute-start(bf16[4,128,256]{2,1,0:T(8,128)(2,1)S(1)} %collective-permute-done.25.refs_3_), channel_id=1, source_target_pairs={{0,240},{16,0},{32,16},{48,32},{64,48},{80,64},{96,80},{112,96},{1... | collective-permute-start | bytes 786440 | tf_op jit(solution)/shard_map/ppermute | solution.py:187
  119.7 20.0 %collective-permute-start.29 = (bf16[4,128,256]{2,1,0:T(8,128)(2,1)S(1)}, bf16[4,128,256]{2,1,0:T(8,128)(2,1)}, u32[]{:S(2)}, u32[]{:S(2)}) collective-permute-start(bf16[4,128,256]{2,1,0:T(8,128)(2,1)S(1)} %collective-permute-done.25.refs_3_), channel_id=1, source_target_pairs={{0,16},{16,32},{32,48},{48,64},{64,80},{80,96},{96,112},{112,128},... | collective-permute-start | bytes 786440 | tf_op jit(solution)/shard_map/ppermute | solution.py:186
  120.0 19.7 %collective-permute-start.32 = (bf16[4,128,256]{2,1,0:T(8,128)(2,1)S(1)}, bf16[4,128,256]{2,1,0:T(8,128)(2,1)}, u32[]{:S(2)}, u32[]{:S(2)}) collective-permute-start(bf16[4,128,256]{2,1,0:T(8,128)(2,1)S(1)} %collective-permute-done.24.refs_2_), channel_id=1, source_target_pairs={{0,240},{16,0},{32,16},{48,32},{64,48},{80,64},{96,80},{112,96},{1... | collective-permute-start | bytes 786440 | tf_op jit(solution)/shard_map/ppermute | solution.py:187
  121.8 18.0 %collective-permute-start.28 = (bf16[4,128,256]{2,1,0:T(8,128)(2,1)S(1)}, bf16[4,128,256]{2,1,0:T(8,128)(2,1)}, u32[]{:S(2)}, u32[]{:S(2)}) collective-permute-start(bf16[4,128,256]{2,1,0:T(8,128)(2,1)S(1)} %collective-permute-done.24.refs_2_), channel_id=1, source_target_pairs={{0,16},{16,32},{32,48},{48,64},{64,80},{80,96},{96,112},{112,128},... | collective-permute-start | bytes 786440 | tf_op jit(solution)/shard_map/ppermute | solution.py:186
  122.8 16.9 %collective-permute-start.31 = (bf16[4,128,256]{2,1,0:T(8,128)(2,1)S(1)}, bf16[4,128,256]{2,1,0:T(8,128)(2,1)}, u32[]{:S(2)}, u32[]{:S(2)}) collective-permute-start(bf16[4,128,256]{2,1,0:T(8,128)(2,1)S(1)} %collective-permute-done.23.refs_1_), channel_id=1, source_target_pairs={{0,240},{16,0},{32,16},{48,32},{64,48},{80,64},{96,80},{112,96},{1... | collective-permute-start | bytes 786440 | tf_op jit(solution)/shard_map/ppermute | solution.py:187
  123.5 16.3 %collective-permute-start.27 = (bf16[4,128,256]{2,1,0:T(8,128)(2,1)S(1)}, bf16[4,128,256]{2,1,0:T(8,128)(2,1)}, u32[]{:S(2)}, u32[]{:S(2)}) collective-permute-start(bf16[4,128,256]{2,1,0:T(8,128)(2,1)S(1)} %collective-permute-done.23.refs_1_), channel_id=1, source_target_pairs={{0,16},{16,32},{32,48},{48,64},{64,80},{80,96},{96,112},{112,128},... | collective-permute-start | bytes 786440 | tf_op jit(solution)/shard_map/ppermute | solution.py:186
  124.4 54.9 %all-to-all-start.1 = ((f32[256,1,256]{2,1,0:T(1,128)}), f32[256,1,256]{2,1,0:T(1,128)}, u32[]{:S(2)}, u32[]{:S(2)}) async-start(f32[256,1,256]{2,1,0:T(1,128)} %broadcast_in_dim.2), calls=%async_computation.1 | async-start | bytes 524288 | tf_op jit(solution)/shard_map/all_to_all | solution.py:210
  146.5 10.0 %collective-permute-start.34 = (bf16[4,128,256]{2,1,0:T(8,128)(2,1)S(1)}, bf16[4,128,256]{2,1,0:T(8,128)(2,1)S(1)}, u32[]{:S(2)}, u32[]{:S(2)}) collective-permute-start(bf16[4,128,256]{2,1,0:T(8,128)(2,1)S(1)} %get-tuple-element.33), channel_id=1, source_target_pairs={{0,4},{1,5},{2,6},{3,7},{4,8},{5,9},{6,10},{7,11},{8,12},{9,13},{1... | collective-permute-start | bytes 786440 | tf_op jit(solution)/shard_map/ppermute | solution.py:189
  148.2 14.0 %collective-permute-start.35 = (bf16[4,128,256]{2,1,0:T(8,128)(2,1)S(1)}, bf16[4,128,256]{2,1,0:T(8,128)(2,1)S(1)}, u32[]{:S(2)}, u32[]{:S(2)}) collective-permute-start(bf16[4,128,256]{2,1,0:T(8,128)(2,1)S(1)} %get-tuple-element.34), channel_id=1, source_target_pairs={{0,8},{1,9},{2,10},{3,11},{4,12},{5,13},{6,14},{7,15},{8,0},{9,1},... | collective-permute-start | bytes 786440 | tf_op jit(solution)/shard_map/ppermute | solution.py:189
  151.1 11.1 %collective-permute-start.36 = (bf16[4,128,256]{2,1,0:T(8,128)(2,1)S(1)}, bf16[4,128,256]{2,1,0:T(8,128)(2,1)S(1)}, u32[]{:S(2)}, u32[]{:S(2)}) collective-permute-start(bf16[4,128,256]{2,1,0:T(8,128)(2,1)S(1)} %get-tuple-element.35), channel_id=1, source_target_pairs={{0,12},{1,13},{2,14},{3,15},{4,0},{5,1},{6,2},{7,3},{8,4},{9,5},{1... | collective-permute-start | bytes 786440 | tf_op jit(solution)/shard_map/ppermute | solution.py:189
  162.8 0.7 copy-start.2
  163.5 10.6 %collective-permute-start.37 = (bf16[128,256]{1,0:T(8,128)(2,1)S(1)}, bf16[128,256]{1,0:T(8,128)(2,1)S(1)}, u32[]{:S(2)}, u32[]{:S(2)}) collective-permute-start(bf16[128,256]{1,0:T(8,128)(2,1)S(1)} %get-tuple-element.37), channel_id=1, source_target_pairs={{0,1},{1,2},{2,3},{3,0},{4,5},{5,6},{6,7},{7,4},{8,9},{9,10},{10,1... | collective-permute-start | bytes 196616 | tf_op jit(solution)/shard_map/ppermute | solution.py:191
  166.5 9.2 %collective-permute-start.38 = (bf16[128,256]{1,0:T(8,128)(2,1)S(1)}, bf16[128,256]{1,0:T(8,128)(2,1)S(1)}, u32[]{:S(2)}, u32[]{:S(2)}) collective-permute-start(bf16[128,256]{1,0:T(8,128)(2,1)S(1)} %get-tuple-element.38), channel_id=1, source_target_pairs={{0,2},{1,3},{2,0},{3,1},{4,6},{5,7},{6,4},{7,5},{8,10},{9,11},{10,... | collective-permute-start | bytes 196616 | tf_op jit(solution)/shard_map/ppermute | solution.py:191
  171.3 5.7 %collective-permute-start.39 = (bf16[128,256]{1,0:T(8,128)(2,1)S(1)}, bf16[128,256]{1,0:T(8,128)(2,1)S(1)}, u32[]{:S(2)}, u32[]{:S(2)}) collective-permute-start(bf16[128,256]{1,0:T(8,128)(2,1)S(1)} %get-tuple-element.39), channel_id=1, source_target_pairs={{0,3},{1,0},{2,1},{3,2},{4,7},{5,4},{6,5},{7,6},{8,11},{9,8},{10,9... | collective-permute-start | bytes 196616 | tf_op jit(solution)/shard_map/ppermute | solution.py:191
  174.1 3.0 %copy-start.7 = (bf16[128,256]{1,0:T(8,128)(2,1)}, bf16[128,256]{1,0:T(8,128)(2,1)S(1)}, u32[]{:S(2)}) copy-start(bf16[128,256]{1,0:T(8,128)(2,1)S(1)} %collective-permute-done.37.one) | copy-start | bytes 196612
  175.8 1.3 copy-start.8
  177.1 0.6 copy-start.9

commit v2 on v1

v2 whole, which is shorter than its diff:
```python
import functools

import jax
import jax.numpy as jnp
from jax import lax
from jax.experimental import pallas as pl
from jax.experimental.pallas import tpu as pltpu
from jax.sharding import PartitionSpec as P

BF = jnp.bfloat16
F32 = jnp.float32
VMEM = pltpu.VMEM
SMEM = pltpu.SMEM
MIB = 1 << 20
SIDE = 4
PARTS = 1
TURNS = (1, 3, 2)
SLOTS = 16
COUNTS, ROWS, COLS = 3, 16, 64


def along_z(k):
    return [(t, (t // SIDE) * SIDE + (t % SIDE + k) % SIDE) for t in range(SIDE * SIDE)]


def along_y(k):
    return [(t, ((t // SIDE + k) % SIDE) * SIDE + t % SIDE) for t in range(SIDE * SIDE)]


def flipped(bit):
    return [(b, b ^ bit) for b in range(lax.axis_size("blk"))]


def outer():
    count = lax.axis_size("blk")
    return [(b, (b + 1 if b % 2 else b - 1) % count) for b in range(count)]


def whole(space=VMEM):
    return pl.BlockSpec(memory_space=space)


def call(kernel, outs, operands, specs, scratch=(), limit=16, name=None):
    return pl.pallas_call(
        kernel,
        in_specs=specs,
        out_specs=[whole()] * len(outs),
        out_shape=[jax.ShapeDtypeStruct(shape, kind) for shape, kind in outs],
        scratch_shapes=list(scratch),
        compiler_params=pltpu.CompilerParams(vmem_limit_bytes=limit * MIB),
        name=name or kernel.__name__.removesuffix("_kernel"),
    )(*operands)


def split(value):
    parts = []
    for _ in range(PARTS):
        parts.append(value.astype(BF))
        value = value - parts[-1].astype(F32)
    return jnp.stack(parts)


def joined(parts):
    total = parts[0].astype(F32)
    for n in range(1, PARTS):
        total = total + parts[n].astype(F32)
    return total


def aggregate_kernel(layout, meta, values, *refs):
    chunks = refs[: len(layout)]
    own, *sends = refs[len(layout) : len(layout) + SIDE]
    tiles, blocks, total, tile_sems, block_sem = refs[len(layout) + SIDE :]
    block_copy = pltpu.make_async_copy(values.at[0], blocks, block_sem)
    block_copy.start()
    copies = [[], [], []]
    for chunk, (group, places) in zip(chunks, layout):
        for n, place in enumerate(places):
            copy = pltpu.make_async_copy(
                chunk.at[pl.ds(n * 2 * SIDE, 2 * SIDE)],
                tiles.at[group, pl.ds(place * 2 * SIDE, 2 * SIDE)],
                tile_sems.at[group, place],
            )
            copy.start()
            copies[group].append(copy)
    my_y, my_z, near_offset = meta[0], meta[1], meta[2]
    total[...] = jnp.zeros_like(total)

    def one(group, offset, k):
        at = offset * SLOTS + k
        col = meta[COLS + at] & 15
        row = meta[ROWS + at] & 15
        source = (((col >> 2) - my_y) & 3) * SIDE + ((col - my_z) & 3)
        tile = tiles[group, pl.ds(2 * source, 2)].reshape(total.shape[1:])
        product = jnp.dot(blocks[offset, k], tile, preferred_element_type=F32)
        total[row] = total[row] + product

    block_copy.wait()
    for group in range(3):
        for copy in copies[group]:
            copy.wait()
        if group == 0:
            for k in range(SLOTS):
                one(0, 1, k)
        else:
            offset = near_offset if group == 1 else 2 - near_offset

            @pl.loop(0, meta[COUNTS + offset])
            def _(k):
                one(group, offset, k)

    own[...] = total[pl.ds(my_y * SIDE, SIDE)]
    for k, send in enumerate(sends, 1):
        share = total[pl.ds(((my_y + k) & 3) * SIDE, SIDE)].astype(BF)
        send[...] = share.reshape(send.shape)


def aggregate(meta, slabs, values):
    half, width = slabs[0][0].shape[1:]
    rows_dev = 2 * half
    chunks = [chunk for chunk, _, _ in slabs]
    layout = tuple((group, places) for _, group, places in slabs)
    return call(
        functools.partial(aggregate_kernel, layout),
        [((SIDE, rows_dev, width), F32)] + [((2 * SIDE, half, width), BF)] * 3,
        [meta, values] + chunks,
        [whole(SMEM)] + [whole(pl.ANY)] * (1 + len(chunks)),
        [
            pltpu.VMEM((3, 2 * SLOTS, half, width), BF),
            pltpu.VMEM(values.shape[1:], BF),
            pltpu.VMEM((SLOTS, rows_dev, width), F32),
            pltpu.SemaphoreType.DMA((3, SIDE)),
            pltpu.SemaphoreType.DMA,
        ],
        limit=28,
        name="aggregate",
    )


def fold_body(meta, own, arrived, kept, sends):
    my_z = meta[1]

    def summed(z):
        total = own[z]
        for share in arrived:
            total = total + share[pl.ds(2 * z, 2)].astype(F32).reshape(total.shape)
        return total

    kept[...] = summed(my_z)
    for k, send in enumerate(sends, 1):
        share = summed((my_z + k) & 3).astype(BF)
        send[pl.ds(0, 2)] = share.reshape(2, -1, share.shape[1])


def fold_kernel(meta, own, one, two, three, kept, *sends):
    fold_body(meta, own, (one, two, three), kept, sends)


def fold_grad_kernel(meta, own, one, two, three, grad, kept, kept_grad, *sends):
    fold_body(meta, own, (one, two, three), kept, sends)
    parts = split(grad[...])
    kept_grad[...] = joined(parts)
    for send in sends:
        send[pl.ds(2, PARTS)] = parts


def summed_rows(own, arrived):
    total = own[...]
    for share in arrived:
        total = total + share[pl.ds(0, 2)].astype(F32).reshape(total.shape)
    return total.astype(BF)


def dense_kernel(meta, own, one, two, three, weight, grad_out, act, back, quarter_grad, *rest):
    sends, local_grad = rest[:3], rest[3]
    hidden = summed_rows(own, (one, two, three))
    pre_act = jnp.dot(hidden, weight[...], preferred_element_type=F32)
    sig_pre = jax.nn.sigmoid(pre_act)
    act[...] = (pre_act * sig_pre).astype(BF)
    grad_pre = (
        grad_out[...].astype(F32) * sig_pre * (1.0 + pre_act * (1.0 - sig_pre))
    ).astype(BF)
    rows = lax.dot_general(
        grad_pre, weight[...], (((1,), (1,)), ((), ())), preferred_element_type=F32
    ).astype(BF)
    back[...] = rows
    local_grad[...] = lax.dot_general(
        hidden, grad_pre, (((0,), (0,)), ((), ())), preferred_element_type=F32
    ).reshape(local_grad.shape)
    my_z = meta[1]
    quarter_grad[...] = local_grad[my_z]
    for k, send in enumerate(sends, 1):
        send[pl.ds(0, 2)] = rows.reshape(2, -1, rows.shape[1])
        send[2] = local_grad[(my_z - k) & 3].astype(BF)


def spread_kernel(back, one, two, three, grad, message):
    units = [back[...].reshape(2, -1, back.shape[1])]
    total = grad[...]
    for ref in (one, two, three):
        units.append(ref[pl.ds(0, 2)])
        total = total + ref[2].astype(F32)
    for k, unit in enumerate(units):
        message[pl.ds(2 * k, 2)] = unit
    message[pl.ds(2 * SIDE, PARTS)] = split(total)


def side_of(block, route, order=(1, 2, 3)):
    got = {0: block}
    for k in order:
        got[k] = lax.ppermute(block, "team", route(-k))
    return [got[k] for k in range(SIDE)]


def three_ways(sends, route):
    return [lax.ppermute(s, "team", route(k)) for k, s in enumerate(sends, 1)]


def slabs_of(message):
    near = {0: lax.ppermute(message, "blk", flipped(1))}
    messages = {0: message}
    for k in TURNS:
        messages[k] = lax.ppermute(message, "team", along_y(-k))
    order = (0,) + TURNS
    far = {}
    for k in order:
        far[k] = lax.ppermute(messages[k], "blk", outer())
        if k:
            near[k] = lax.ppermute(messages[k], "blk", flipped(1))
    groups = [(0, messages), (1, near), (2, far)]
    return messages, [(group[k], n, (k,)) for n, group in groups for k in order]


def grad_of(message):
    total = message[2 * SIDE].astype(F32)
    for n in range(1, PARTS):
        total = total + message[2 * SIDE + n].astype(F32)
    return total


def on_device(features, weight, grad_out, block_vals, block_rows, block_cols, block_counts):
    member = lax.axis_index("team")
    near_offset = 2 - 2 * (lax.axis_index("blk") % 2)
    rows_dev, width = features.shape
    devices = lax.axis_size("blk") * lax.axis_size("team")
    meta = jnp.concatenate(
        [
            jnp.stack([member // SIDE, member % SIDE, near_offset]).astype(jnp.int32),
            block_counts.reshape(-1),
            jnp.zeros((ROWS - COUNTS - block_counts.size,), jnp.int32),
            block_rows.reshape(-1),
            block_cols.reshape(-1),
        ]
    )
    small = (rows_dev, width)
    part = weight.shape[0] // SIDE
    half = rows_dev // 2

    quarter = jnp.concatenate(side_of(features, along_z), axis=0)
    quarter = quarter.reshape(2 * SIDE, half, width)
    own, *sends = aggregate(meta, slabs_of(quarter)[1], block_vals)
    arrived = three_ways(sends, along_y)
    kept, *sends = call(
        fold_kernel,
        [(small, F32)] + [((2, half, width), BF)] * 3,
        [meta, own, *arrived],
        [whole(SMEM)] + [whole()] * 4,
    )
    arrived = three_ways(sends, along_z)

    activations, back, quarter_grad, *sends = call(
        dense_kernel,
        [(small, BF), (small, BF), ((part, weight.shape[1]), F32)] + [((3, half, width), BF)] * 3,
        [meta, kept, *arrived, weight, grad_out],
        [whole(SMEM)] + [whole()] * 6,
        [pltpu.VMEM((SIDE, part, weight.shape[1]), F32)],
    )
    arrived = [lax.ppermute(s, "team", along_z(-k)) for k, s in enumerate(sends, 1)]
    [message] = call(
        spread_kernel,
        [((2 * SIDE + PARTS, half, width), BF)],
        [back, *arrived, quarter_grad],
        [whole()] * 5,
    )
    messages, slabs = slabs_of(message)
    zero, one, two, three = [grad_of(messages[k]) for k in range(SIDE)]
    grad = (zero + two) + (one + three)
    for bit in (1, 2):
        grad = grad + lax.ppermute(grad, "blk", flipped(bit))
    meta, grad = lax.optimization_barrier((meta, grad))
    for bit in (8, 4):
        grad = grad + lax.ppermute(grad, "blk", flipped(bit))
    own, *sends = aggregate(meta, slabs, block_vals)
    arrived = three_ways(sends, along_y)
    kept, kept_grad, *sends = call(
        fold_grad_kernel,
        [(small, F32), (grad.shape, F32)] + [((2 + PARTS, half, width), BF)] * 3,
        [meta, own, *arrived, grad],
        [whole(SMEM)] + [whole()] * 5,
    )
    arrived = three_ways(sends, along_z)
    scale = (rows_dev * devices) ** (-0.5)

    def finish_kernel(meta, own, grad, one, two, three, out, grad_weight):
        out[...] = summed_rows(own, (one, two, three))
        my_z = meta[1]
        grad_weight[my_z] = grad[...] * scale
        for k, ref in enumerate((one, two, three), 1):
            grad_weight[(my_z - k) & 3] = joined(ref[pl.ds(2, PARTS)]) * scale

    grad_feats, grad_weight = call(
        finish_kernel,
        [(small, BF), ((SIDE,) + grad.shape, F32)],
        [meta, kept, kept_grad, *arrived],
        [whole(SMEM)] + [whole()] * 5,
    )
    return (activations, grad_feats, grad_weight.reshape(weight.shape))


def solution(mesh):
    lanes = P(("blk", "team"))
    return jax.shard_map(
        on_device,
        mesh=mesh,
        in_specs=(lanes, P(), lanes, lanes, lanes, lanes, lanes),
        out_specs=(lanes, lanes, P()),
        check_vma=False,
    )
```

time: 181 us -> 160 us (0.88); the launches traced: 181 us -> 158 us
  starting transfers between devices: 96.8 us -> 71.4 us
  waiting for transfers between devices: 56.8 us -> 68.3 us
  local copies, waits for them, and re-layouts: 7.53 us -> 2.32 us
  Pallas kernels: 16.8 us -> 12.6 us
    all_to_all x2 -> x0, starting transfers between devices: 27.3 us -> none  [the longest x1 15.4 us: on_device(): lax.all_to_all(jnp.broadcast_to(mine, shares.shape), everyone, 0, 0, tile...]
    ppermute x40 -> x44, waiting for transfers between devices: 49.3 us -> 68.3 us  [the longest x12 20.8 us: three_ways(): return [lax.ppermute(s, 'team', route(k)) for k, s in enumerate(sends, 1)]]
    all_to_all x2 -> x0, waiting for transfers between devices: 7.53 us -> none  [the longest x1 7.53 us: on_device(): lax.all_to_all(local_grad.reshape(devices, share, -1), everyone, 0, 0, ti...]
    unnamed x22 -> x6, local copies, waits for them, and re-layouts: 5.72 us -> 1.42 us
    pallas_call x6 -> x7, Pallas kernels: 16.8 us -> 12.6 us  [call(): pl.pallas_call(kernel, in_specs=specs, out_specs=[whole()] * len(outs), o...]
    ppermute x40 -> x44, starting transfers between devices: 69.4 us -> 71.4 us  [the longest x12 28.7 us: three_ways(): return [lax.ppermute(s, 'team', route(k)) for k, s in enumerate(sends, 1)]]
  transfers between devices with their start and end apart: 42 -> 44, of which waited for: 19 -> 25; matrix products, arithmetic and copies ran while one was open for 2% -> 1% of each run, Pallas kernels for 5% -> 0%
where the time goes in v2:
time: 160 us; the launch traced here: 158 us
  starting transfers between devices  71.4 us (45%)
  waiting for transfers between devices  68.3 us (43%)
  Pallas kernels  12.6 us (8%)
  local copies, waits for them, and re-layouts  2.32 us (1%)
  other arithmetic  2.31 us (1%)
    ppermute x12, starting transfers between devices, three_ways(): return [lax.ppermute(s, 'team', route(k)) for k, s in enumerate(sends, 1)]  28.7 us
    ppermute x12, waiting for transfers between devices, three_ways(): return [lax.ppermute(s, 'team', route(k)) for k, s in enumerate(sends, 1)]  20.8 us
    ppermute x6, waiting for transfers between devices, slabs_of(): messages[k] = lax.ppermute(message, 'team', along_y(-k))  16.6 us
    pallas_call x7, Pallas kernels, call(): pl.pallas_call(kernel, in_specs=specs, out_specs=[whole()] * len(outs), o...  12.6 us
    ppermute x6, starting transfers between devices, slabs_of(): messages[k] = lax.ppermute(message, 'team', along_y(-k))  12 us
    ppermute x4, waiting for transfers between devices, on_device(): grad = grad + lax.ppermute(grad, 'blk', flipped(bit))  10.7 us
    ppermute x3, starting transfers between devices, side_of(): got[k] = lax.ppermute(block, 'team', route(-k))  10.2 us
    ppermute x8, waiting for transfers between devices, slabs_of(): far[k] = lax.ppermute(messages[k], 'blk', outer())  8.3 us
  transfers between devices with their start and end apart: 44, of which 25 were waited for; matrix products, arithmetic and copies ran while one was open for 1% of the time, Pallas kernels for 0%

profile of v2, /device:TPU:2, one launch (start us, length us, event | category | flops | bytes accessed | tf_op | source)
XLA Modules:
  0.0 157.7 jit_solution(18179012704846500408)
XLA Ops:
  0.6 7.3 %collective-permute-start.1 = (bf16[128,256]{1,0:T(8,128)(2,1)}, bf16[128,256]{1,0:T(8,128)(2,1)S(1)}, u32[]{:S(2)}, u32[]{:S(2)}) collective-permute-start(bf16[128,256]{1,0:T(8,128)(2,1)} %param.7), channel_id=1, source_target_pairs={{0,2},{1,3},{2,0},{3,1},{4,6},{5,7},{6,4},{7,5},{8,10},{9,11},{10,... | collective-permute-start | bytes 196616 | tf_op jit(solution)/shard_map/ppermute | solution.py:211
  7.9 2.9 %collective-permute-start.2 = (bf16[128,256]{1,0:T(8,128)(2,1)}, bf16[128,256]{1,0:T(8,128)(2,1)S(1)}, u32[]{:S(2)}, u32[]{:S(2)}) collective-permute-start(bf16[128,256]{1,0:T(8,128)(2,1)} %param.7), channel_id=1, source_target_pairs={{0,1},{1,2},{2,3},{3,0},{4,5},{5,6},{6,7},{7,4},{8,9},{9,10},{10,1... | collective-permute-start | bytes 196616 | tf_op jit(solution)/shard_map/ppermute | solution.py:211
  10.8 4.2 %collective-permute-done = bf16[128,256]{1,0:T(8,128)(2,1)S(1)} collective-permute-done((bf16[128,256]{1,0:T(8,128)(2,1)}, bf16[128,256]{1,0:T(8,128)(2,1)S(1)}, u32[]{:S(2)}, u32[]{:S(2)}) %collective-permute-start) | collective-permute-done | bytes 65568 | tf_op jit(solution)/shard_map/ppermute | solution.py:211
  15.0 0.9 pad_maximum_fusion
  15.9 3.3 %collective-permute-start.5 = (bf16[8,64,256]{2,1,0:T(8,128)(2,1)S(1)}, bf16[8,64,256]{2,1,0:T(8,128)(2,1)S(1)}, u32[]{:S(2)}, u32[]{:S(2)}) collective-permute-start(bf16[8,64,256]{2,1,0:T(8,128)(2,1)S(1)} %bitcast.8), channel_id=1, source_target_pairs={{0,8},{1,9},{2,10},{3,11},{4,12},{5,13},{6,14},{7,15},{8,0},{9,1},... | collective-permute-start | bytes 786440 | tf_op jit(solution)/shard_map/ppermute | solution.py:223
  19.2 0.7 collective-permute-start.4
  19.9 1.3 collective-permute-start.6
  21.2 2.6 %collective-permute-start.3 = (bf16[8,64,256]{2,1,0:T(8,128)(2,1)S(1)}, bf16[8,64,256]{2,1,0:T(8,128)(2,1)S(1)}, u32[]{:S(2)}, u32[]{:S(2)}) collective-permute-start(bf16[8,64,256]{2,1,0:T(8,128)(2,1)S(1)} %bitcast.12), channel_id=1, source_target_pairs={{0,12},{1,13},{2,14},{3,15},{4,0},{5,1},{6,2},{7,3},{8,4},{9,5},{1... | collective-permute-start | bytes 786440 | tf_op jit(solution)/shard_map/ppermute | solution.py:223
  23.7 2.9 %collective-permute-done.5.refs_3_ = bf16[8,64,256]{2,1,0:T(8,128)(2,1)S(1)} collective-permute-done((bf16[8,64,256]{2,1,0:T(8,128)(2,1)S(1)}, bf16[8,64,256]{2,1,0:T(8,128)(2,1)S(1)}, u32[]{:S(2)}, u32[]{:S(2)}) %collective-permute-start.5) | collective-permute-done | bytes 262176 | tf_op jit(solution)/shard_map/ppermute | solution.py:223
  26.7 1.6 %collective-permute-start.9 = (bf16[8,64,256]{2,1,0:T(8,128)(2,1)S(1)}, bf16[8,64,256]{2,1,0:T(8,128)(2,1)S(1)}, u32[]{:S(2)}, u32[]{:S(2)}) collective-permute-start(bf16[8,64,256]{2,1,0:T(8,128)(2,1)S(1)} %collective-permute-done.5.refs_3_), channel_id=1, source_target_pairs={{0,16},{16,0},{32,48},{48,32},{64,80},{80,64},{96,112},{112,96},{1... | collective-permute-start | bytes 786440 | tf_op jit(solution)/shard_map/ppermute | solution.py:229
  28.3 3.0 %collective-permute-done.4.refs_2_ = bf16[8,64,256]{2,1,0:T(8,128)(2,1)S(1)} collective-permute-done((bf16[8,64,256]{2,1,0:T(8,128)(2,1)S(1)}, bf16[8,64,256]{2,1,0:T(8,128)(2,1)S(1)}, u32[]{:S(2)}, u32[]{:S(2)}) %collective-permute-start.4) | collective-permute-done | bytes 262176 | tf_op jit(solution)/shard_map/ppermute | solution.py:223
  31.3 1.6 %collective-permute-start.8 = (bf16[8,64,256]{2,1,0:T(8,128)(2,1)S(1)}, bf16[8,64,256]{2,1,0:T(8,128)(2,1)S(1)}, u32[]{:S(2)}, u32[]{:S(2)}) collective-permute-start(bf16[8,64,256]{2,1,0:T(8,128)(2,1)S(1)} %collective-permute-done.4.refs_2_), channel_id=1, source_target_pairs={{0,16},{16,0},{32,48},{48,32},{64,80},{80,64},{96,112},{112,96},{1... | collective-permute-start | bytes 786440 | tf_op jit(solution)/shard_map/ppermute | solution.py:229
  32.9 0.9 collective-permute-start.11
  34.2 0.7 reduce
  35.0 0.7 reduce.1
  35.8 0.7 concatenate.6.meta
  36.5 0.5 collective-permute-done.12.refs_10_
  37.1 2.8 %collective-permute-done.11.refs_9_ = bf16[8,64,256]{2,1,0:T(8,128)(2,1)S(1)} collective-permute-done((bf16[8,64,256]{2,1,0:T(8,128)(2,1)S(1)}, bf16[8,64,256]{2,1,0:T(8,128)(2,1)S(1)}, u32[]{:S(2)}, u32[]{:S(2)}) %collective-permute-start.11) | collective-permute-done | bytes 262176 | tf_op jit(solution)/shard_map/ppermute | solution.py:227
  39.9 1.4 copy-done
  41.3 4.3 %aggregate.2 = (f32[4,128,256]{2,1,0:T(8,128)S(1)}, bf16[8,64,256]{2,1,0:T(8,128)(2,1)S(1)}, bf16[8,64,256]{2,1,0:T(8,128)(2,1)S(1)}, bf16[8,64,256]{2,1,0:T(8,128)(2,1)S(1)}) custom-call(s32[112]{0:T(128)S(1)} %concatenate.6.meta, bf16[1,3,16,128,128]{4,3,2,1,0:T(8,128)(2,1)S(1)} %copy-done, bf16[8,64,256]{2,1,0:T(8,128)(2,1)S(1)} %bitcast.13, ...), custom_call_target="tpu_custom_call" | custom-call | tf_op jit(solution)/shard_map/aggregate/pallas_call | solution.py:44
  45.6 2.2 %collective-permute-start.14 = (bf16[8,64,256]{2,1,0:T(8,128)(2,1)S(1)}, bf16[8,64,256]{2,1,0:T(8,128)(2,1)S(1)}, u32[]{:S(2)}, u32[]{:S(2)}) collective-permute-start(bf16[8,64,256]{2,1,0:T(8,128)(2,1)S(1)} %get-tuple-element.31), channel_id=1, source_target_pairs={{0,4},{1,5},{2,6},{3,7},{4,8},{5,9},{6,10},{7,11},{8,12},{9,13},{1... | collective-permute-start | bytes 786440 | tf_op jit(solution)/shard_map/ppermute | solution.py:216
  47.7 2.1 %collective-permute-start.15 = (bf16[8,64,256]{2,1,0:T(8,128)(2,1)S(1)}, bf16[8,64,256]{2,1,0:T(8,128)(2,1)S(1)}, u32[]{:S(2)}, u32[]{:S(2)}) collective-permute-start(bf16[8,64,256]{2,1,0:T(8,128)(2,1)S(1)} %get-tuple-element.32), channel_id=1, source_target_pairs={{0,8},{1,9},{2,10},{3,11},{4,12},{5,13},{6,14},{7,15},{8,0},{9,1},... | collective-permute-start | bytes 786440 | tf_op jit(solution)/shard_map/ppermute | solution.py:216
  49.8 2.5 %collective-permute-start.16 = (bf16[8,64,256]{2,1,0:T(8,128)(2,1)S(1)}, bf16[8,64,256]{2,1,0:T(8,128)(2,1)S(1)}, u32[]{:S(2)}, u32[]{:S(2)}) collective-permute-start(bf16[8,64,256]{2,1,0:T(8,128)(2,1)S(1)} %get-tuple-element.33), channel_id=1, source_target_pairs={{0,12},{1,13},{2,14},{3,15},{4,0},{5,1},{6,2},{7,3},{8,4},{9,5},{1... | collective-permute-start | bytes 786440 | tf_op jit(solution)/shard_map/ppermute | solution.py:216
  52.4 3.9 %collective-permute-done.14.one = bf16[8,64,256]{2,1,0:T(8,128)(2,1)S(1)} collective-permute-done((bf16[8,64,256]{2,1,0:T(8,128)(2,1)S(1)}, bf16[8,64,256]{2,1,0:T(8,128)(2,1)S(1)}, u32[]{:S(2)}, u32[]{:S(2)}) %collective-permute-start.14) | collective-permute-done | bytes 262176 | tf_op jit(solution)/shard_map/ppermute | solution.py:216
  56.3 5.6 %collective-permute-done.15.two = bf16[8,64,256]{2,1,0:T(8,128)(2,1)S(1)} collective-permute-done((bf16[8,64,256]{2,1,0:T(8,128)(2,1)S(1)}, bf16[8,64,256]{2,1,0:T(8,128)(2,1)S(1)}, u32[]{:S(2)}, u32[]{:S(2)}) %collective-permute-start.15) | collective-permute-done | bytes 262176 | tf_op jit(solution)/shard_map/ppermute | solution.py:216
  62.3 0.7 fold.1
  63.3 4.9 %collective-permute-start.18 = (bf16[2,64,256]{2,1,0:T(8,128)(2,1)S(1)}, bf16[2,64,256]{2,1,0:T(8,128)(2,1)S(1)}, u32[]{:S(2)}, u32[]{:S(2)}) collective-permute-start(bf16[2,64,256]{2,1,0:T(8,128)(2,1)S(1)} %get-tuple-element.36), channel_id=1, source_target_pairs={{0,2},{1,3},{2,0},{3,1},{4,6},{5,7},{6,4},{7,5},{8,10},{9,11},{10,... | collective-permute-start | bytes 196616 | tf_op jit(solution)/shard_map/ppermute | solution.py:216
  68.2 2.6 %collective-permute-start.19 = (bf16[2,64,256]{2,1,0:T(8,128)(2,1)S(1)}, bf16[2,64,256]{2,1,0:T(8,128)(2,1)S(1)}, u32[]{:S(2)}, u32[]{:S(2)}) collective-permute-start(bf16[2,64,256]{2,1,0:T(8,128)(2,1)S(1)} %get-tuple-element.37), channel_id=1, source_target_pairs={{0,3},{1,0},{2,1},{3,2},{4,7},{5,4},{6,5},{7,6},{8,11},{9,8},{10,9... | collective-permute-start | bytes 196616 | tf_op jit(solution)/shard_map/ppermute | solution.py:216
  70.9 2.0 %collective-permute-done.18.two = bf16[2,64,256]{2,1,0:T(8,128)(2,1)S(1)} collective-permute-done((bf16[2,64,256]{2,1,0:T(8,128)(2,1)S(1)}, bf16[2,64,256]{2,1,0:T(8,128)(2,1)S(1)}, u32[]{:S(2)}, u32[]{:S(2)}) %collective-permute-start.18) | collective-permute-done | bytes 65568 | tf_op jit(solution)/shard_map/ppermute | solution.py:216
  72.9 0.8 collective-permute-done.19.three
  73.7 1.4 dense.1
  75.1 3.5 %collective-permute-start.20 = (bf16[3,64,256]{2,1,0:T(8,128)(2,1)S(1)}, bf16[3,64,256]{2,1,0:T(8,128)(2,1)S(1)}, u32[]{:S(2)}, u32[]{:S(2)}) collective-permute-start(bf16[3,64,256]{2,1,0:T(8,128)(2,1)S(1)} %get-tuple-element.40), channel_id=1, source_target_pairs={{0,3},{1,0},{2,1},{3,2},{4,7},{5,4},{6,5},{7,6},{8,11},{9,8},{10,9... | collective-permute-start | bytes 294920 | tf_op jit(solution)/shard_map/ppermute | solution.py:278
  78.6 2.9 %collective-permute-start.21 = (bf16[3,64,256]{2,1,0:T(8,128)(2,1)S(1)}, bf16[3,64,256]{2,1,0:T(8,128)(2,1)S(1)}, u32[]{:S(2)}, u32[]{:S(2)}) collective-permute-start(bf16[3,64,256]{2,1,0:T(8,128)(2,1)S(1)} %get-tuple-element.41), channel_id=1, source_target_pairs={{0,2},{1,3},{2,0},{3,1},{4,6},{5,7},{6,4},{7,5},{8,10},{9,11},{10,... | collective-permute-start | bytes 294920 | tf_op jit(solution)/shard_map/ppermute | solution.py:278
  81.5 0.7 collective-permute-start.22
  82.2 1.3 collective-permute-done.20.one
  83.6 6.1 %collective-permute-done.21.two = bf16[3,64,256]{2,1,0:T(8,128)(2,1)S(1)} collective-permute-done((bf16[3,64,256]{2,1,0:T(8,128)(2,1)S(1)}, bf16[3,64,256]{2,1,0:T(8,128)(2,1)S(1)}, u32[]{:S(2)}, u32[]{:S(2)}) %collective-permute-start.21) | collective-permute-done | bytes 98336 | tf_op jit(solution)/shard_map/ppermute | solution.py:278
  90.0 1.3 collective-permute-start.25
  91.3 2.0 %collective-permute-start.24 = (bf16[9,64,256]{2,1,0:T(8,128)(2,1)S(1)}, bf16[9,64,256]{2,1,0:T(8,128)(2,1)S(1)}, u32[]{:S(2)}, u32[]{:S(2)}) collective-permute-start(bf16[9,64,256]{2,1,0:T(8,128)(2,1)S(1)} %spread.1.refs_0_), channel_id=1, source_target_pairs={{0,12},{1,13},{2,14},{3,15},{4,0},{5,1},{6,2},{7,3},{8,4},{9,5},{1... | collective-permute-start | bytes 884744 | tf_op jit(solution)/shard_map/ppermute | solution.py:223
  93.3 2.2 %collective-permute-start.23 = (bf16[9,64,256]{2,1,0:T(8,128)(2,1)S(1)}, bf16[9,64,256]{2,1,0:T(8,128)(2,1)S(1)}, u32[]{:S(2)}, u32[]{:S(2)}) collective-permute-start(bf16[9,64,256]{2,1,0:T(8,128)(2,1)S(1)} %spread.1.refs_0_), channel_id=1, source_target_pairs={{0,8},{1,9},{2,10},{3,11},{4,12},{5,13},{6,14},{7,15},{8,0},{9,1},... | collective-permute-start | bytes 884744 | tf_op jit(solution)/shard_map/ppermute | solution.py:223
  95.9 4.0 %collective-permute-done.25.refs_2_ = bf16[9,64,256]{2,1,0:T(8,128)(2,1)S(1)} collective-permute-done((bf16[9,64,256]{2,1,0:T(8,128)(2,1)S(1)}, bf16[9,64,256]{2,1,0:T(8,128)(2,1)S(1)}, u32[]{:S(2)}, u32[]{:S(2)}) %collective-permute-start.25) | collective-permute-done | bytes 294944 | tf_op jit(solution)/shard_map/ppermute | solution.py:223
  99.9 4.9 %collective-permute-done.24.refs_1_ = bf16[9,64,256]{2,1,0:T(8,128)(2,1)S(1)} collective-permute-done((bf16[9,64,256]{2,1,0:T(8,128)(2,1)S(1)}, bf16[9,64,256]{2,1,0:T(8,128)(2,1)S(1)}, u32[]{:S(2)}, u32[]{:S(2)}) %collective-permute-start.24) | collective-permute-done | bytes 294944 | tf_op jit(solution)/shard_map/ppermute | solution.py:223
  104.8 1.8 %collective-permute-done.23.refs_3_ = bf16[9,64,256]{2,1,0:T(8,128)(2,1)S(1)} collective-permute-done((bf16[9,64,256]{2,1,0:T(8,128)(2,1)S(1)}, bf16[9,64,256]{2,1,0:T(8,128)(2,1)S(1)}, u32[]{:S(2)}, u32[]{:S(2)}) %collective-permute-start.23) | collective-permute-done | bytes 294944 | tf_op jit(solution)/shard_map/ppermute | solution.py:223
  106.7 1.2 collective-permute-done.26
  108.3 1.9 %collective-permute-start.33 = (bf16[9,64,256]{2,1,0:T(8,128)(2,1)S(1)}, bf16[9,64,256]{2,1,0:T(8,128)(2,1)S(1)}, u32[]{:S(2)}, u32[]{:S(2)}) collective-permute-start(bf16[9,64,256]{2,1,0:T(8,128)(2,1)S(1)} %collective-permute-done.24.refs_1_), channel_id=1, source_target_pairs={{0,240},{16,32},{32,16},{48,64},{64,48},{80,96},{96,80},{112,128},... | collective-permute-start | bytes 884744 | tf_op jit(solution)/shard_map/ppermute | solution.py:227
  110.2 1.4 collective-permute-start.29
  111.6 1.4 collective-permute-done.27
  113.0 1.2 collective-permute-start.35
  114.2 1.2 collective-permute-done.33.refs_9_
  115.4 3.8 %collective-permute-done.35.refs_11_ = bf16[9,64,256]{2,1,0:T(8,128)(2,1)S(1)} collective-permute-done((bf16[9,64,256]{2,1,0:T(8,128)(2,1)S(1)}, bf16[9,64,256]{2,1,0:T(8,128)(2,1)S(1)}, u32[]{:S(2)}, u32[]{:S(2)}) %collective-permute-start.35) | collective-permute-done | bytes 294944 | tf_op jit(solution)/shard_map/ppermute | solution.py:227
  119.2 4.3 %aggregate.3 = (f32[4,128,256]{2,1,0:T(8,128)S(1)}, bf16[8,64,256]{2,1,0:T(8,128)(2,1)S(1)}, bf16[8,64,256]{2,1,0:T(8,128)(2,1)S(1)}, bf16[8,64,256]{2,1,0:T(8,128)(2,1)S(1)}) custom-call(s32[112]{0:T(128)S(1)} %concatenate.6.meta, bf16[1,3,16,128,128]{4,3,2,1,0:T(8,128)(2,1)S(1)} %copy-done, bf16[9,64,256]{2,1,0:T(8,128)(2,1)S(1)} %spread.1.refs_0_, ...), custom_call_target="tpu_custom_call" | custom-call | tf_op jit(solution)/shard_map/aggregate/pallas_call | solution.py:44
  123.4 1.5 collective-permute-start.36
  125.0 2.8 %collective-permute-start.37 = (bf16[8,64,256]{2,1,0:T(8,128)(2,1)S(1)}, bf16[8,64,256]{2,1,0:T(8,128)(2,1)S(1)}, u32[]{:S(2)}, u32[]{:S(2)}) collective-permute-start(bf16[8,64,256]{2,1,0:T(8,128)(2,1)S(1)} %get-tuple-element.47), channel_id=1, source_target_pairs={{0,8},{1,9},{2,10},{3,11},{4,12},{5,13},{6,14},{7,15},{8,0},{9,1},... | collective-permute-start | bytes 786440 | tf_op jit(solution)/shard_map/ppermute | solution.py:216
  127.8 1.4 collective-permute-start.38
  129.2 4.2 %collective-permute-done.39 = f32[64,256]{1,0:T(8,128)S(1)} collective-permute-done((f32[64,256]{1,0:T(8,128)S(1)}, f32[64,256]{1,0:T(8,128)S(1)}, u32[]{:S(2)}, u32[]{:S(2)}) %collective-permute-start.39) | collective-permute-done | bytes 65568 | tf_op jit(solution)/shard_map/ppermute | solution.py:292
  133.4 2.0 %collective-permute-start.40 = (f32[64,256]{1,0:T(8,128)S(1)}, f32[64,256]{1,0:T(8,128)S(1)}, u32[]{:S(2)}, u32[]{:S(2)}) collective-permute-start(f32[64,256]{1,0:T(8,128)S(1)} %add.42), channel_id=1, source_target_pairs={{0,64},{16,80},{32,96},{48,112},{64,0},{80,16},{96,32},{112,48},{1... | collective-permute-start | bytes 196616 | tf_op jit(solution)/shard_map/ppermute | solution.py:292
  135.4 3.9 %collective-permute-done.40 = f32[64,256]{1,0:T(8,128)S(1)} collective-permute-done((f32[64,256]{1,0:T(8,128)S(1)}, f32[64,256]{1,0:T(8,128)S(1)}, u32[]{:S(2)}, u32[]{:S(2)}) %collective-permute-start.40) | collective-permute-done | bytes 65568 | tf_op jit(solution)/shard_map/ppermute | solution.py:292
  139.3 1.1 collective-permute-done.37.two
  140.4 0.7 fold_grad.1
  141.0 2.2 %collective-permute-start.41 = (bf16[3,64,256]{2,1,0:T(8,128)(2,1)S(1)}, bf16[3,64,256]{2,1,0:T(8,128)(2,1)S(1)}, u32[]{:S(2)}, u32[]{:S(2)}) collective-permute-start(bf16[3,64,256]{2,1,0:T(8,128)(2,1)S(1)} %get-tuple-element.52), channel_id=1, source_target_pairs={{0,1},{1,2},{2,3},{3,0},{4,5},{5,6},{6,7},{7,4},{8,9},{9,10},{10,1... | collective-permute-start | bytes 294920 | tf_op jit(solution)/shard_map/ppermute | solution.py:216
  143.2 2.4 %collective-permute-start.42 = (bf16[3,64,256]{2,1,0:T(8,128)(2,1)S(1)}, bf16[3,64,256]{2,1,0:T(8,128)(2,1)S(1)}, u32[]{:S(2)}, u32[]{:S(2)}) collective-permute-start(bf16[3,64,256]{2,1,0:T(8,128)(2,1)S(1)} %get-tuple-element.53), channel_id=1, source_target_pairs={{0,2},{1,3},{2,0},{3,1},{4,6},{5,7},{6,4},{7,5},{8,10},{9,11},{10,... | collective-permute-start | bytes 294920 | tf_op jit(solution)/shard_map/ppermute | solution.py:216
  145.6 3.9 %collective-permute-start.43 = (bf16[3,64,256]{2,1,0:T(8,128)(2,1)S(1)}, bf16[3,64,256]{2,1,0:T(8,128)(2,1)S(1)}, u32[]{:S(2)}, u32[]{:S(2)}) collective-permute-start(bf16[3,64,256]{2,1,0:T(8,128)(2,1)S(1)} %get-tuple-element.54), channel_id=1, source_target_pairs={{0,3},{1,0},{2,1},{3,2},{4,7},{5,4},{6,5},{7,6},{8,11},{9,8},{10,9... | collective-permute-start | bytes 294920 | tf_op jit(solution)/shard_map/ppermute | solution.py:216
  149.5 5.1 %collective-permute-done.42.two = bf16[3,64,256]{2,1,0:T(8,128)(2,1)S(1)} collective-permute-done((bf16[3,64,256]{2,1,0:T(8,128)(2,1)S(1)}, bf16[3,64,256]{2,1,0:T(8,128)(2,1)S(1)}, u32[]{:S(2)}, u32[]{:S(2)}) %collective-permute-start.42) | collective-permute-done | bytes 98336 | tf_op jit(solution)/shard_map/ppermute | solution.py:216
  154.6 1.8 %collective-permute-done.43.three = bf16[3,64,256]{2,1,0:T(8,128)(2,1)S(1)} collective-permute-done((bf16[3,64,256]{2,1,0:T(8,128)(2,1)S(1)}, bf16[3,64,256]{2,1,0:T(8,128)(2,1)S(1)}, u32[]{:S(2)}, u32[]{:S(2)}) %collective-permute-start.43) | collective-permute-done | bytes 98336 | tf_op jit(solution)/shard_map/ppermute | solution.py:216
  156.4 1.3 finish.1
  (49 shorter events, 2.8 us)
Async XLA Ops:
  0.6 10.2 %collective-permute-start.1 = (bf16[128,256]{1,0:T(8,128)(2,1)}, bf16[128,256]{1,0:T(8,128)(2,1)S(1)}, u32[]{:S(2)}, u32[]{:S(2)}) collective-permute-start(bf16[128,256]{1,0:T(8,128)(2,1)} %param.7), channel_id=1, source_target_pairs={{0,2},{1,3},{2,0},{3,1},{4,6},{5,7},{6,4},{7,5},{8,10},{9,11},{10,... | collective-permute-start | bytes 196616 | tf_op jit(solution)/shard_map/ppermute | solution.py:211
  7.9 7.1 %collective-permute-start = (bf16[128,256]{1,0:T(8,128)(2,1)}, bf16[128,256]{1,0:T(8,128)(2,1)S(1)}, u32[]{:S(2)}, u32[]{:S(2)}) collective-permute-start(bf16[128,256]{1,0:T(8,128)(2,1)} %param.7), channel_id=1, source_target_pairs={{0,3},{1,0},{2,1},{3,2},{4,7},{5,4},{6,5},{7,6},{8,11},{9,8},{10,9... | collective-permute-start | bytes 196616 | tf_op jit(solution)/shard_map/ppermute | solution.py:211
  7.9 7.1 %collective-permute-start.2 = (bf16[128,256]{1,0:T(8,128)(2,1)}, bf16[128,256]{1,0:T(8,128)(2,1)S(1)}, u32[]{:S(2)}, u32[]{:S(2)}) collective-permute-start(bf16[128,256]{1,0:T(8,128)(2,1)} %param.7), channel_id=1, source_target_pairs={{0,1},{1,2},{2,3},{3,0},{4,5},{5,6},{6,7},{7,4},{8,9},{9,10},{10,1... | collective-permute-start | bytes 196616 | tf_op jit(solution)/shard_map/ppermute | solution.py:211
  15.9 10.8 %collective-permute-start.5 = (bf16[8,64,256]{2,1,0:T(8,128)(2,1)S(1)}, bf16[8,64,256]{2,1,0:T(8,128)(2,1)S(1)}, u32[]{:S(2)}, u32[]{:S(2)}) collective-permute-start(bf16[8,64,256]{2,1,0:T(8,128)(2,1)S(1)} %bitcast.8), channel_id=1, source_target_pairs={{0,8},{1,9},{2,10},{3,11},{4,12},{5,13},{6,14},{7,15},{8,0},{9,1},... | collective-permute-start | bytes 786440 | tf_op jit(solution)/shard_map/ppermute | solution.py:223
  19.2 7.5 %collective-permute-start.10 = (bf16[8,64,256]{2,1,0:T(8,128)(2,1)S(1)}, bf16[8,64,256]{2,1,0:T(8,128)(2,1)S(1)}, u32[]{:S(2)}, u32[]{:S(2)}) collective-permute-start(bf16[8,64,256]{2,1,0:T(8,128)(2,1)S(1)} %bitcast.9), channel_id=1, source_target_pairs={{0,240},{16,32},{32,16},{48,64},{64,48},{80,96},{96,80},{112,128},... | collective-permute-start | bytes 786440 | tf_op jit(solution)/shard_map/ppermute | solution.py:227
  19.2 12.1 %collective-permute-start.4 = (bf16[8,64,256]{2,1,0:T(8,128)(2,1)S(1)}, bf16[8,64,256]{2,1,0:T(8,128)(2,1)S(1)}, u32[]{:S(2)}, u32[]{:S(2)}) collective-permute-start(bf16[8,64,256]{2,1,0:T(8,128)(2,1)S(1)} %bitcast.10), channel_id=1, source_target_pairs={{0,4},{1,5},{2,6},{3,7},{4,8},{5,9},{6,10},{7,11},{8,12},{9,13},{1... | collective-permute-start | bytes 786440 | tf_op jit(solution)/shard_map/ppermute | solution.py:223
  19.9 11.4 %collective-permute-start.6 = (bf16[8,64,256]{2,1,0:T(8,128)(2,1)S(1)}, bf16[8,64,256]{2,1,0:T(8,128)(2,1)S(1)}, u32[]{:S(2)}, u32[]{:S(2)}) collective-permute-start(bf16[8,64,256]{2,1,0:T(8,128)(2,1)S(1)} %bitcast.11), channel_id=1, source_target_pairs={{0,16},{16,0},{32,48},{48,32},{64,80},{80,64},{96,112},{112,96},{1... | collective-permute-start | bytes 786440 | tf_op jit(solution)/shard_map/ppermute | solution.py:220
  21.2 11.7 %collective-permute-start.3 = (bf16[8,64,256]{2,1,0:T(8,128)(2,1)S(1)}, bf16[8,64,256]{2,1,0:T(8,128)(2,1)S(1)}, u32[]{:S(2)}, u32[]{:S(2)}) collective-permute-start(bf16[8,64,256]{2,1,0:T(8,128)(2,1)S(1)} %bitcast.12), channel_id=1, source_target_pairs={{0,12},{1,13},{2,14},{3,15},{4,0},{5,1},{6,2},{7,3},{8,4},{9,5},{1... | collective-permute-start | bytes 786440 | tf_op jit(solution)/shard_map/ppermute | solution.py:223
  26.7 7.1 %collective-permute-start.13 = (bf16[8,64,256]{2,1,0:T(8,128)(2,1)S(1)}, bf16[8,64,256]{2,1,0:T(8,128)(2,1)S(1)}, u32[]{:S(2)}, u32[]{:S(2)}) collective-permute-start(bf16[8,64,256]{2,1,0:T(8,128)(2,1)S(1)} %collective-permute-done.5.refs_3_), channel_id=1, source_target_pairs={{0,240},{16,32},{32,16},{48,64},{64,48},{80,96},{96,80},{112,128},... | collective-permute-start | bytes 786440 | tf_op jit(solution)/shard_map/ppermute | solution.py:227
  26.7 9.9 %collective-permute-start.9 = (bf16[8,64,256]{2,1,0:T(8,128)(2,1)S(1)}, bf16[8,64,256]{2,1,0:T(8,128)(2,1)S(1)}, u32[]{:S(2)}, u32[]{:S(2)}) collective-permute-start(bf16[8,64,256]{2,1,0:T(8,128)(2,1)S(1)} %collective-permute-done.5.refs_3_), channel_id=1, source_target_pairs={{0,16},{16,0},{32,48},{48,32},{64,80},{80,64},{96,112},{112,96},{1... | collective-permute-start | bytes 786440 | tf_op jit(solution)/shard_map/ppermute | solution.py:229
  31.3 5.8 %collective-permute-start.12 = (bf16[8,64,256]{2,1,0:T(8,128)(2,1)S(1)}, bf16[8,64,256]{2,1,0:T(8,128)(2,1)S(1)}, u32[]{:S(2)}, u32[]{:S(2)}) collective-permute-start(bf16[8,64,256]{2,1,0:T(8,128)(2,1)S(1)} %collective-permute-done.4.refs_2_), channel_id=1, source_target_pairs={{0,240},{16,32},{32,16},{48,64},{64,48},{80,96},{96,80},{112,128},... | collective-permute-start | bytes 786440 | tf_op jit(solution)/shard_map/ppermute | solution.py:227
  31.3 5.8 %collective-permute-start.8 = (bf16[8,64,256]{2,1,0:T(8,128)(2,1)S(1)}, bf16[8,64,256]{2,1,0:T(8,128)(2,1)S(1)}, u32[]{:S(2)}, u32[]{:S(2)}) collective-permute-start(bf16[8,64,256]{2,1,0:T(8,128)(2,1)S(1)} %collective-permute-done.4.refs_2_), channel_id=1, source_target_pairs={{0,16},{16,0},{32,48},{48,32},{64,80},{80,64},{96,112},{112,96},{1... | collective-permute-start | bytes 786440 | tf_op jit(solution)/shard_map/ppermute | solution.py:229
  32.9 7.0 %collective-permute-start.11 = (bf16[8,64,256]{2,1,0:T(8,128)(2,1)S(1)}, bf16[8,64,256]{2,1,0:T(8,128)(2,1)S(1)}, u32[]{:S(2)}, u32[]{:S(2)}) collective-permute-start(bf16[8,64,256]{2,1,0:T(8,128)(2,1)S(1)} %collective-permute-done.3.refs_1_), channel_id=1, source_target_pairs={{0,240},{16,32},{32,16},{48,64},{64,48},{80,96},{96,80},{112,128},... | collective-permute-start | bytes 786440 | tf_op jit(solution)/shard_map/ppermute | solution.py:227
  33.8 6.1 %collective-permute-start.7 = (bf16[8,64,256]{2,1,0:T(8,128)(2,1)S(1)}, bf16[8,64,256]{2,1,0:T(8,128)(2,1)S(1)}, u32[]{:S(2)}, u32[]{:S(2)}) collective-permute-start(bf16[8,64,256]{2,1,0:T(8,128)(2,1)S(1)} %collective-permute-done.3.refs_1_), channel_id=1, source_target_pairs={{0,16},{16,0},{32,48},{48,32},{64,80},{80,64},{96,112},{112,96},{1... | collective-permute-start | bytes 786440 | tf_op jit(solution)/shard_map/ppermute | solution.py:229
  39.9 1.4 copy-start
  41.3 32.4 %copy-start.1 = (bf16[256,256]{1,0:T(8,128)(2,1)S(1)}, bf16[256,256]{1,0:T(8,128)(2,1)}, u32[]{:S(2)}) copy-start(bf16[256,256]{1,0:T(8,128)(2,1)} %weight.1) | copy-start | bytes 393220
  41.3 32.4 %copy-start.2 = (bf16[128,256]{1,0:T(8,128)(2,1)S(1)}, bf16[128,256]{1,0:T(8,128)(2,1)}, u32[]{:S(2)}) copy-start(bf16[128,256]{1,0:T(8,128)(2,1)} %grad_out.1) | copy-start | bytes 196612
  45.6 10.7 %collective-permute-start.14 = (bf16[8,64,256]{2,1,0:T(8,128)(2,1)S(1)}, bf16[8,64,256]{2,1,0:T(8,128)(2,1)S(1)}, u32[]{:S(2)}, u32[]{:S(2)}) collective-permute-start(bf16[8,64,256]{2,1,0:T(8,128)(2,1)S(1)} %get-tuple-element.31), channel_id=1, source_target_pairs={{0,4},{1,5},{2,6},{3,7},{4,8},{5,9},{6,10},{7,11},{8,12},{9,13},{1... | collective-permute-start | bytes 786440 | tf_op jit(solution)/shard_map/ppermute | solution.py:216
  47.7 14.1 %collective-permute-start.15 = (bf16[8,64,256]{2,1,0:T(8,128)(2,1)S(1)}, bf16[8,64,256]{2,1,0:T(8,128)(2,1)S(1)}, u32[]{:S(2)}, u32[]{:S(2)}) collective-permute-start(bf16[8,64,256]{2,1,0:T(8,128)(2,1)S(1)} %get-tuple-element.32), channel_id=1, source_target_pairs={{0,8},{1,9},{2,10},{3,11},{4,12},{5,13},{6,14},{7,15},{8,0},{9,1},... | collective-permute-start | bytes 786440 | tf_op jit(solution)/shard_map/ppermute | solution.py:216
  49.8 12.5 %collective-permute-start.16 = (bf16[8,64,256]{2,1,0:T(8,128)(2,1)S(1)}, bf16[8,64,256]{2,1,0:T(8,128)(2,1)S(1)}, u32[]{:S(2)}, u32[]{:S(2)}) collective-permute-start(bf16[8,64,256]{2,1,0:T(8,128)(2,1)S(1)} %get-tuple-element.33), channel_id=1, source_target_pairs={{0,12},{1,13},{2,14},{3,15},{4,0},{5,1},{6,2},{7,3},{8,4},{9,5},{1... | collective-permute-start | bytes 786440 | tf_op jit(solution)/shard_map/ppermute | solution.py:216
  63.0 7.9 %collective-permute-start.17 = (bf16[2,64,256]{2,1,0:T(8,128)(2,1)S(1)}, bf16[2,64,256]{2,1,0:T(8,128)(2,1)S(1)}, u32[]{:S(2)}, u32[]{:S(2)}) collective-permute-start(bf16[2,64,256]{2,1,0:T(8,128)(2,1)S(1)} %get-tuple-element.35), channel_id=1, source_target_pairs={{0,1},{1,2},{2,3},{3,0},{4,5},{5,6},{6,7},{7,4},{8,9},{9,10},{10,1... | collective-permute-start | bytes 196616 | tf_op jit(solution)/shard_map/ppermute | solution.py:216
  63.3 9.6 %collective-permute-start.18 = (bf16[2,64,256]{2,1,0:T(8,128)(2,1)S(1)}, bf16[2,64,256]{2,1,0:T(8,128)(2,1)S(1)}, u32[]{:S(2)}, u32[]{:S(2)}) collective-permute-start(bf16[2,64,256]{2,1,0:T(8,128)(2,1)S(1)} %get-tuple-element.36), channel_id=1, source_target_pairs={{0,2},{1,3},{2,0},{3,1},{4,6},{5,7},{6,4},{7,5},{8,10},{9,11},{10,... | collective-permute-start | bytes 196616 | tf_op jit(solution)/shard_map/ppermute | solution.py:216
  68.2 5.5 %collective-permute-start.19 = (bf16[2,64,256]{2,1,0:T(8,128)(2,1)S(1)}, bf16[2,64,256]{2,1,0:T(8,128)(2,1)S(1)}, u32[]{:S(2)}, u32[]{:S(2)}) collective-permute-start(bf16[2,64,256]{2,1,0:T(8,128)(2,1)S(1)} %get-tuple-element.37), channel_id=1, source_target_pairs={{0,3},{1,0},{2,1},{3,2},{4,7},{5,4},{6,5},{7,6},{8,11},{9,8},{10,9... | collective-permute-start | bytes 196616 | tf_op jit(solution)/shard_map/ppermute | solution.py:216
  75.1 8.5 %collective-permute-start.20 = (bf16[3,64,256]{2,1,0:T(8,128)(2,1)S(1)}, bf16[3,64,256]{2,1,0:T(8,128)(2,1)S(1)}, u32[]{:S(2)}, u32[]{:S(2)}) collective-permute-start(bf16[3,64,256]{2,1,0:T(8,128)(2,1)S(1)} %get-tuple-element.40), channel_id=1, source_target_pairs={{0,3},{1,0},{2,1},{3,2},{4,7},{5,4},{6,5},{7,6},{8,11},{9,8},{10,9... | collective-permute-start | bytes 294920 | tf_op jit(solution)/shard_map/ppermute | solution.py:278
  78.6 11.0 %collective-permute-start.21 = (bf16[3,64,256]{2,1,0:T(8,128)(2,1)S(1)}, bf16[3,64,256]{2,1,0:T(8,128)(2,1)S(1)}, u32[]{:S(2)}, u32[]{:S(2)}) collective-permute-start(bf16[3,64,256]{2,1,0:T(8,128)(2,1)S(1)} %get-tuple-element.41), channel_id=1, source_target_pairs={{0,2},{1,3},{2,0},{3,1},{4,6},{5,7},{6,4},{7,5},{8,10},{9,11},{10,... | collective-permute-start | bytes 294920 | tf_op jit(solution)/shard_map/ppermute | solution.py:278
  81.5 8.4 %collective-permute-start.22 = (bf16[3,64,256]{2,1,0:T(8,128)(2,1)S(1)}, bf16[3,64,256]{2,1,0:T(8,128)(2,1)S(1)}, u32[]{:S(2)}, u32[]{:S(2)}) collective-permute-start(bf16[3,64,256]{2,1,0:T(8,128)(2,1)S(1)} %get-tuple-element.42), channel_id=1, source_target_pairs={{0,1},{1,2},{2,3},{3,0},{4,5},{5,6},{6,7},{7,4},{8,9},{9,10},{10,1... | collective-permute-start | bytes 294920 | tf_op jit(solution)/shard_map/ppermute | solution.py:278
  90.0 9.9 %collective-permute-start.25 = (bf16[9,64,256]{2,1,0:T(8,128)(2,1)S(1)}, bf16[9,64,256]{2,1,0:T(8,128)(2,1)S(1)}, u32[]{:S(2)}, u32[]{:S(2)}) collective-permute-start(bf16[9,64,256]{2,1,0:T(8,128)(2,1)S(1)} %spread.1.refs_0_), channel_id=1, source_target_pairs={{0,4},{1,5},{2,6},{3,7},{4,8},{5,9},{6,10},{7,11},{8,12},{9,13},{1... | collective-permute-start | bytes 884744 | tf_op jit(solution)/shard_map/ppermute | solution.py:223
  91.3 13.5 %collective-permute-start.24 = (bf16[9,64,256]{2,1,0:T(8,128)(2,1)S(1)}, bf16[9,64,256]{2,1,0:T(8,128)(2,1)S(1)}, u32[]{:S(2)}, u32[]{:S(2)}) collective-permute-start(bf16[9,64,256]{2,1,0:T(8,128)(2,1)S(1)} %spread.1.refs_0_), channel_id=1, source_target_pairs={{0,12},{1,13},{2,14},{3,15},{4,0},{5,1},{6,2},{7,3},{8,4},{9,5},{1... | collective-permute-start | bytes 884744 | tf_op jit(solution)/shard_map/ppermute | solution.py:223
  93.3 13.3 %collective-permute-start.23 = (bf16[9,64,256]{2,1,0:T(8,128)(2,1)S(1)}, bf16[9,64,256]{2,1,0:T(8,128)(2,1)S(1)}, u32[]{:S(2)}, u32[]{:S(2)}) collective-permute-start(bf16[9,64,256]{2,1,0:T(8,128)(2,1)S(1)} %spread.1.refs_0_), channel_id=1, source_target_pairs={{0,8},{1,9},{2,10},{3,11},{4,12},{5,13},{6,14},{7,15},{8,0},{9,1},... | collective-permute-start | bytes 884744 | tf_op jit(solution)/shard_map/ppermute | solution.py:223
  95.4 12.9 %collective-permute-start.32 = (bf16[9,64,256]{2,1,0:T(8,128)(2,1)S(1)}, bf16[9,64,256]{2,1,0:T(8,128)(2,1)S(1)}, u32[]{:S(2)}, u32[]{:S(2)}) collective-permute-start(bf16[9,64,256]{2,1,0:T(8,128)(2,1)S(1)} %spread.1.refs_0_), channel_id=1, source_target_pairs={{0,240},{16,32},{32,16},{48,64},{64,48},{80,96},{96,80},{112,128},... | collective-permute-start | bytes 884744 | tf_op jit(solution)/shard_map/ppermute | solution.py:227
  95.4 14.8 %collective-permute-start.28 = (bf16[9,64,256]{2,1,0:T(8,128)(2,1)S(1)}, bf16[9,64,256]{2,1,0:T(8,128)(2,1)S(1)}, u32[]{:S(2)}, u32[]{:S(2)}) collective-permute-start(bf16[9,64,256]{2,1,0:T(8,128)(2,1)S(1)} %spread.1.refs_0_), channel_id=1, source_target_pairs={{0,16},{16,0},{32,48},{48,32},{64,80},{80,64},{96,112},{112,96},{1... | collective-permute-start | bytes 884744 | tf_op jit(solution)/shard_map/ppermute | solution.py:220
  99.9 14.3 %collective-permute-start.34 = (bf16[9,64,256]{2,1,0:T(8,128)(2,1)S(1)}, bf16[9,64,256]{2,1,0:T(8,128)(2,1)S(1)}, u32[]{:S(2)}, u32[]{:S(2)}) collective-permute-start(bf16[9,64,256]{2,1,0:T(8,128)(2,1)S(1)} %collective-permute-done.25.refs_2_), channel_id=1, source_target_pairs={{0,240},{16,32},{32,16},{48,64},{64,48},{80,96},{96,80},{112,128},... | collective-permute-start | bytes 884744 | tf_op jit(solution)/shard_map/ppermute | solution.py:227
  106.6 1.3 collective-permute-start.26
  108.0 5.0 %collective-permute-start.27 = (f32[64,256]{1,0:T(8,128)S(1)}, f32[64,256]{1,0:T(8,128)S(1)}, u32[]{:S(2)}, u32[]{:S(2)}) collective-permute-start(f32[64,256]{1,0:T(8,128)S(1)} %add.40), channel_id=1, source_target_pairs={{0,32},{16,48},{32,0},{48,16},{64,96},{80,112},{96,64},{112,80},{1... | collective-permute-start | bytes 196616 | tf_op jit(solution)/shard_map/ppermute | solution.py:289
  108.1 6.1 %collective-permute-start.30 = (bf16[9,64,256]{2,1,0:T(8,128)(2,1)S(1)}, bf16[9,64,256]{2,1,0:T(8,128)(2,1)S(1)}, u32[]{:S(2)}, u32[]{:S(2)}) collective-permute-start(bf16[9,64,256]{2,1,0:T(8,128)(2,1)S(1)} %collective-permute-done.25.refs_2_), channel_id=1, source_target_pairs={{0,16},{16,0},{32,48},{48,32},{64,80},{80,64},{96,112},{112,96},{1... | collective-permute-start | bytes 884744 | tf_op jit(solution)/shard_map/ppermute | solution.py:229
  108.3 7.1 %collective-permute-start.33 = (bf16[9,64,256]{2,1,0:T(8,128)(2,1)S(1)}, bf16[9,64,256]{2,1,0:T(8,128)(2,1)S(1)}, u32[]{:S(2)}, u32[]{:S(2)}) collective-permute-start(bf16[9,64,256]{2,1,0:T(8,128)(2,1)S(1)} %collective-permute-done.24.refs_1_), channel_id=1, source_target_pairs={{0,240},{16,32},{32,16},{48,64},{64,48},{80,96},{96,80},{112,128},... | collective-permute-start | bytes 884744 | tf_op jit(solution)/shard_map/ppermute | solution.py:227
  110.2 5.2 %collective-permute-start.29 = (bf16[9,64,256]{2,1,0:T(8,128)(2,1)S(1)}, bf16[9,64,256]{2,1,0:T(8,128)(2,1)S(1)}, u32[]{:S(2)}, u32[]{:S(2)}) collective-permute-start(bf16[9,64,256]{2,1,0:T(8,128)(2,1)S(1)} %collective-permute-done.24.refs_1_), channel_id=1, source_target_pairs={{0,16},{16,0},{32,48},{48,32},{64,80},{80,64},{96,112},{112,96},{1... | collective-permute-start | bytes 884744 | tf_op jit(solution)/shard_map/ppermute | solution.py:229
  113.0 6.1 %collective-permute-start.35 = (bf16[9,64,256]{2,1,0:T(8,128)(2,1)S(1)}, bf16[9,64,256]{2,1,0:T(8,128)(2,1)S(1)}, u32[]{:S(2)}, u32[]{:S(2)}) collective-permute-start(bf16[9,64,256]{2,1,0:T(8,128)(2,1)S(1)} %collective-permute-done.23.refs_3_), channel_id=1, source_target_pairs={{0,240},{16,32},{32,16},{48,64},{64,48},{80,96},{96,80},{112,128},... | collective-permute-start | bytes 884744 | tf_op jit(solution)/shard_map/ppermute | solution.py:227
  114.2 5.0 %collective-permute-start.31 = (bf16[9,64,256]{2,1,0:T(8,128)(2,1)S(1)}, bf16[9,64,256]{2,1,0:T(8,128)(2,1)S(1)}, u32[]{:S(2)}, u32[]{:S(2)}) collective-permute-start(bf16[9,64,256]{2,1,0:T(8,128)(2,1)S(1)} %collective-permute-done.23.refs_3_), channel_id=1, source_target_pairs={{0,16},{16,0},{32,48},{48,32},{64,80},{80,64},{96,112},{112,96},{1... | collective-permute-start | bytes 884744 | tf_op jit(solution)/shard_map/ppermute | solution.py:229
  123.4 15.8 %collective-permute-start.36 = (bf16[8,64,256]{2,1,0:T(8,128)(2,1)S(1)}, bf16[8,64,256]{2,1,0:T(8,128)(2,1)S(1)}, u32[]{:S(2)}, u32[]{:S(2)}) collective-permute-start(bf16[8,64,256]{2,1,0:T(8,128)(2,1)S(1)} %get-tuple-element.46), channel_id=1, source_target_pairs={{0,4},{1,5},{2,6},{3,7},{4,8},{5,9},{6,10},{7,11},{8,12},{9,13},{1... | collective-permute-start | bytes 786440 | tf_op jit(solution)/shard_map/ppermute | solution.py:216
  125.0 15.4 %collective-permute-start.37 = (bf16[8,64,256]{2,1,0:T(8,128)(2,1)S(1)}, bf16[8,64,256]{2,1,0:T(8,128)(2,1)S(1)}, u32[]{:S(2)}, u32[]{:S(2)}) collective-permute-start(bf16[8,64,256]{2,1,0:T(8,128)(2,1)S(1)} %get-tuple-element.47), channel_id=1, source_target_pairs={{0,8},{1,9},{2,10},{3,11},{4,12},{5,13},{6,14},{7,15},{8,0},{9,1},... | collective-permute-start | bytes 786440 | tf_op jit(solution)/shard_map/ppermute | solution.py:216
  127.8 12.6 %collective-permute-start.38 = (bf16[8,64,256]{2,1,0:T(8,128)(2,1)S(1)}, bf16[8,64,256]{2,1,0:T(8,128)(2,1)S(1)}, u32[]{:S(2)}, u32[]{:S(2)}) collective-permute-start(bf16[8,64,256]{2,1,0:T(8,128)(2,1)S(1)} %get-tuple-element.48), channel_id=1, source_target_pairs={{0,12},{1,13},{2,14},{3,15},{4,0},{5,1},{6,2},{7,3},{8,4},{9,5},{1... | collective-permute-start | bytes 786440 | tf_op jit(solution)/shard_map/ppermute | solution.py:216
  129.1 4.3 %collective-permute-start.39 = (f32[64,256]{1,0:T(8,128)S(1)}, f32[64,256]{1,0:T(8,128)S(1)}, u32[]{:S(2)}, u32[]{:S(2)}) collective-permute-start(f32[64,256]{1,0:T(8,128)S(1)} %add.41), channel_id=1, source_target_pairs={{0,128},{16,144},{32,160},{48,176},{64,192},{80,208},{96,224},{112... | collective-permute-start | bytes 196616 | tf_op jit(solution)/shard_map/ppermute | solution.py:292
  133.4 5.9 %collective-permute-start.40 = (f32[64,256]{1,0:T(8,128)S(1)}, f32[64,256]{1,0:T(8,128)S(1)}, u32[]{:S(2)}, u32[]{:S(2)}) collective-permute-start(f32[64,256]{1,0:T(8,128)S(1)} %add.42), channel_id=1, source_target_pairs={{0,64},{16,80},{32,96},{48,112},{64,0},{80,16},{96,32},{112,48},{1... | collective-permute-start | bytes 196616 | tf_op jit(solution)/shard_map/ppermute | solution.py:292
  141.0 8.4 %collective-permute-start.41 = (bf16[3,64,256]{2,1,0:T(8,128)(2,1)S(1)}, bf16[3,64,256]{2,1,0:T(8,128)(2,1)S(1)}, u32[]{:S(2)}, u32[]{:S(2)}) collective-permute-start(bf16[3,64,256]{2,1,0:T(8,128)(2,1)S(1)} %get-tuple-element.52), channel_id=1, source_target_pairs={{0,1},{1,2},{2,3},{3,0},{4,5},{5,6},{6,7},{7,4},{8,9},{9,10},{10,1... | collective-permute-start | bytes 294920 | tf_op jit(solution)/shard_map/ppermute | solution.py:216
  143.2 11.3 %collective-permute-start.42 = (bf16[3,64,256]{2,1,0:T(8,128)(2,1)S(1)}, bf16[3,64,256]{2,1,0:T(8,128)(2,1)S(1)}, u32[]{:S(2)}, u32[]{:S(2)}) collective-permute-start(bf16[3,64,256]{2,1,0:T(8,128)(2,1)S(1)} %get-tuple-element.53), channel_id=1, source_target_pairs={{0,2},{1,3},{2,0},{3,1},{4,6},{5,7},{6,4},{7,5},{8,10},{9,11},{10,... | collective-permute-start | bytes 294920 | tf_op jit(solution)/shard_map/ppermute | solution.py:216
  145.6 10.7 %collective-permute-start.43 = (bf16[3,64,256]{2,1,0:T(8,128)(2,1)S(1)}, bf16[3,64,256]{2,1,0:T(8,128)(2,1)S(1)}, u32[]{:S(2)}, u32[]{:S(2)}) collective-permute-start(bf16[3,64,256]{2,1,0:T(8,128)(2,1)S(1)} %get-tuple-element.54), channel_id=1, source_target_pairs={{0,3},{1,0},{2,1},{3,2},{4,7},{5,4},{6,5},{7,6},{8,11},{9,8},{10,9... | collective-permute-start | bytes 294920 | tf_op jit(solution)/shard_map/ppermute | solution.py:216

commit v3 on v2

--- a/solution.py
+++ b/solution.py
@@ -16,6 +16,7 @@
 PARTS = 1
 TURNS = (1, 3, 2)
 SLOTS = 16
+TOGETHER = 8
 COUNTS, ROWS, COLS = 3, 16, 64
 
 
@@ -67,47 +68,49 @@
     return total
 
 
-def aggregate_kernel(layout, meta, values, *refs):
+def keep_kernel(values, kept, sem):
+    copy = pltpu.make_async_copy(values.at[0], kept, sem)
+    copy.start()
+    copy.wait()
+
+
+def aggregate_kernel(layout, meta, blocks, *refs):
     chunks = refs[: len(layout)]
     own, *sends = refs[len(layout) : len(layout) + SIDE]
-    tiles, blocks, total, tile_sems, block_sem = refs[len(layout) + SIDE :]
-    block_copy = pltpu.make_async_copy(values.at[0], blocks, block_sem)
-    block_copy.start()
-    copies = [[], [], []]
-    for chunk, (group, places) in zip(chunks, layout):
-        for n, place in enumerate(places):
-            copy = pltpu.make_async_copy(
-                chunk.at[pl.ds(n * 2 * SIDE, 2 * SIDE)],
-                tiles.at[group, pl.ds(place * 2 * SIDE, 2 * SIDE)],
-                tile_sems.at[group, place],
-            )
-            copy.start()
-            copies[group].append(copy)
+    tiles, total = refs[len(layout) + SIDE :]
     my_y, my_z, near_offset = meta[0], meta[1], meta[2]
     total[...] = jnp.zeros_like(total)
 
-    def one(group, offset, k):
+    def one(group, offset, k, count=None):
         at = offset * SLOTS + k
         col = meta[COLS + at] & 15
         row = meta[ROWS + at] & 15
         source = (((col >> 2) - my_y) & 3) * SIDE + ((col - my_z) & 3)
         tile = tiles[group, pl.ds(2 * source, 2)].reshape(total.shape[1:])
         product = jnp.dot(blocks[offset, k], tile, preferred_element_type=F32)
+        if count is not None:
+            product = jnp.where(k < count, product, 0.0)
         total[row] = total[row] + product
 
-    block_copy.wait()
     for group in range(3):
-        for copy in copies[group]:
-            copy.wait()
+        for chunk, (at, places) in zip(chunks, layout):
+            if at == group:
+                for n, place in enumerate(places):
+                    tiles[group, pl.ds(place * 2 * SIDE, 2 * SIDE)] = chunk[
+                        pl.ds(n * 2 * SIDE, 2 * SIDE)
+                    ]
         if group == 0:
             for k in range(SLOTS):
                 one(0, 1, k)
         else:
             offset = near_offset if group == 1 else 2 - near_offset
 
-            @pl.loop(0, meta[COUNTS + offset])
-            def _(k):
-                one(group, offset, k)
+            count = meta[COUNTS + offset]
+
+            @pl.loop(0, (count + TOGETHER - 1) // TOGETHER)
+            def _(n):
+                for k in range(TOGETHER):
+                    one(group, offset, n * TOGETHER + k, count)
 
     own[...] = total[pl.ds(my_y * SIDE, SIDE)]
     for k, send in enumerate(sends, 1):
@@ -115,7 +118,7 @@
         send[...] = share.reshape(send.shape)
 
 
-def aggregate(meta, slabs, values):
+def aggregate(meta, slabs, blocks):
     half, width = slabs[0][0].shape[1:]
     rows_dev = 2 * half
     chunks = [chunk for chunk, _, _ in slabs]
@@ -123,14 +126,11 @@
     return call(
         functools.partial(aggregate_kernel, layout),
         [((SIDE, rows_dev, width), F32)] + [((2 * SIDE, half, width), BF)] * 3,
-        [meta, values] + chunks,
-        [whole(SMEM)] + [whole(pl.ANY)] * (1 + len(chunks)),
+        [meta, blocks] + chunks,
+        [whole(SMEM)] + [whole()] * (1 + len(chunks)),
         [
             pltpu.VMEM((3, 2 * SLOTS, half, width), BF),
-            pltpu.VMEM(values.shape[1:], BF),
             pltpu.VMEM((SLOTS, rows_dev, width), F32),
-            pltpu.SemaphoreType.DMA((3, SIDE)),
-            pltpu.SemaphoreType.DMA,
         ],
         limit=28,
         name="aggregate",
@@ -256,9 +256,16 @@
     part = weight.shape[0] // SIDE
     half = rows_dev // 2
 
+    [blocks] = call(
+        keep_kernel,
+        [(block_vals.shape[1:], BF)],
+        [block_vals],
+        [whole(pl.ANY)],
+        [pltpu.SemaphoreType.DMA],
+    )
     quarter = jnp.concatenate(side_of(features, along_z), axis=0)
     quarter = quarter.reshape(2 * SIDE, half, width)
-    own, *sends = aggregate(meta, slabs_of(quarter)[1], block_vals)
+    own, *sends = aggregate(meta, slabs_of(quarter)[1], blocks)
     arrived = three_ways(sends, along_y)
     kept, *sends = call(
         fold_kernel,
@@ -290,7 +297,7 @@
     meta, grad = lax.optimization_barrier((meta, grad))
     for bit in (8, 4):
         grad = grad + lax.ppermute(grad, "blk", flipped(bit))
-    own, *sends = aggregate(meta, slabs, block_vals)
+    own, *sends = aggregate(meta, slabs, blocks)
     arrived = three_ways(sends, along_y)
     kept, kept_grad, *sends = call(
         fold_grad_kernel,

time: 160 us -> 155 us (0.969)
  Pallas kernels: 12.6 us -> 9.39 us
  waiting for transfers between devices: 68.3 us -> 65.3 us
  starting transfers between devices: 71.4 us -> 73.6 us
    ppermute x4, waiting for transfers between devices: 10.7 us -> 7.12 us  [on_device(): grad = grad + lax.ppermute(grad, 'blk', flipped(bit))]
    ppermute x4, starting transfers between devices: 2.23 us -> 5.65 us  [on_device(): grad = grad + lax.ppermute(grad, 'blk', flipped(bit))]
    pallas_call x7 -> x8, Pallas kernels: 12.6 us -> 9.39 us  [call(): pl.pallas_call(kernel, in_specs=specs, out_specs=[whole()] * len(outs), o...]
    ppermute x12, starting transfers between devices: 28.7 us -> 26 us  [three_ways(): return [lax.ppermute(s, 'team', route(k)) for k, s in enumerate(sends, 1)]]
    ppermute x12, waiting for transfers between devices: 20.8 us -> 22.7 us  [three_ways(): return [lax.ppermute(s, 'team', route(k)) for k, s in enumerate(sends, 1)]]
    ppermute x6, starting transfers between devices: 5.29 us -> 6.98 us  [slabs_of(): near[k] = lax.ppermute(messages[k], 'blk', flipped(1))]
  transfers between devices with their start and end apart: 44 -> 44, of which waited for: 25 -> 26; matrix products, arithmetic and copies ran while one was open for 1% -> 1% of each run, Pallas kernels for 0% -> 0%
where the time goes in v3:
time: 155 us; the launch traced here: 154 us
  starting transfers between devices  73.6 us (47%)
  waiting for transfers between devices  65.3 us (42%)
  Pallas kernels  9.39 us (6%)
  other arithmetic  2.31 us (1%)
  local copies, waits for them, and re-layouts  2.17 us (1%)
    ppermute x12, starting transfers between devices, three_ways(): return [lax.ppermute(s, 'team', route(k)) for k, s in enumerate(sends, 1)]  26 us
    ppermute x12, waiting for transfers between devices, three_ways(): return [lax.ppermute(s, 'team', route(k)) for k, s in enumerate(sends, 1)]  22.7 us
    ppermute x6, waiting for transfers between devices, slabs_of(): messages[k] = lax.ppermute(message, 'team', along_y(-k))  16.5 us
    ppermute x6, starting transfers between devices, slabs_of(): messages[k] = lax.ppermute(message, 'team', along_y(-k))  12.3 us
    ppermute x3, starting transfers between devices, side_of(): got[k] = lax.ppermute(block, 'team', route(-k))  10.2 us
    pallas_call x8, Pallas kernels, call(): pl.pallas_call(kernel, in_specs=specs, out_specs=[whole()] * len(outs), o...  9.39 us
    ppermute x3, waiting for transfers between devices, on_device(): lax.ppermute(s, 'team', along_z(-k))  7.97 us
    ppermute x4, waiting for transfers between devices, on_device(): grad = grad + lax.ppermute(grad, 'blk', flipped(bit))  7.12 us
  transfers between devices with their start and end apart: 44, of which 26 were waited for; matrix products, arithmetic and copies ran while one was open for 1% of the time, Pallas kernels for 0%

profile of v3, /device:TPU:2, one launch (start us, length us, event | category | flops | bytes accessed | tf_op | source)
XLA Modules:
  0.0 153.6 jit_solution(5350216564820690780)
XLA Ops:
  0.6 7.3 %collective-permute-start.1 = (bf16[128,256]{1,0:T(8,128)(2,1)}, bf16[128,256]{1,0:T(8,128)(2,1)S(1)}, u32[]{:S(2)}, u32[]{:S(2)}) collective-permute-start(bf16[128,256]{1,0:T(8,128)(2,1)} %param.7), channel_id=1, source_target_pairs={{0,2},{1,3},{2,0},{3,1},{4,6},{5,7},{6,4},{7,5},{8,10},{9,11},{10,... | collective-permute-start | bytes 196616 | tf_op jit(solution)/shard_map/ppermute | solution.py:211
  7.9 2.9 %collective-permute-start.2 = (bf16[128,256]{1,0:T(8,128)(2,1)}, bf16[128,256]{1,0:T(8,128)(2,1)S(1)}, u32[]{:S(2)}, u32[]{:S(2)}) collective-permute-start(bf16[128,256]{1,0:T(8,128)(2,1)} %param.7), channel_id=1, source_target_pairs={{0,1},{1,2},{2,3},{3,0},{4,5},{5,6},{6,7},{7,4},{8,9},{9,10},{10,1... | collective-permute-start | bytes 196616 | tf_op jit(solution)/shard_map/ppermute | solution.py:211
  10.8 4.2 %collective-permute-done = bf16[128,256]{1,0:T(8,128)(2,1)S(1)} collective-permute-done((bf16[128,256]{1,0:T(8,128)(2,1)}, bf16[128,256]{1,0:T(8,128)(2,1)S(1)}, u32[]{:S(2)}, u32[]{:S(2)}) %collective-permute-start) | collective-permute-done | bytes 65568 | tf_op jit(solution)/shard_map/ppermute | solution.py:211
  15.0 0.9 pad_maximum_fusion
  15.9 3.3 %collective-permute-start.5 = (bf16[8,64,256]{2,1,0:T(8,128)(2,1)S(1)}, bf16[8,64,256]{2,1,0:T(8,128)(2,1)S(1)}, u32[]{:S(2)}, u32[]{:S(2)}) collective-permute-start(bf16[8,64,256]{2,1,0:T(8,128)(2,1)S(1)} %bitcast.8), channel_id=1, source_target_pairs={{0,8},{1,9},{2,10},{3,11},{4,12},{5,13},{6,14},{7,15},{8,0},{9,1},... | collective-permute-start | bytes 786440 | tf_op jit(solution)/shard_map/ppermute | solution.py:223
  19.2 0.7 collective-permute-start.4
  19.9 1.3 collective-permute-start.6
  21.2 2.6 %collective-permute-start.3 = (bf16[8,64,256]{2,1,0:T(8,128)(2,1)S(1)}, bf16[8,64,256]{2,1,0:T(8,128)(2,1)S(1)}, u32[]{:S(2)}, u32[]{:S(2)}) collective-permute-start(bf16[8,64,256]{2,1,0:T(8,128)(2,1)S(1)} %bitcast.12), channel_id=1, source_target_pairs={{0,12},{1,13},{2,14},{3,15},{4,0},{5,1},{6,2},{7,3},{8,4},{9,5},{1... | collective-permute-start | bytes 786440 | tf_op jit(solution)/shard_map/ppermute | solution.py:223
  23.7 2.9 %collective-permute-done.5.refs_3_ = bf16[8,64,256]{2,1,0:T(8,128)(2,1)S(1)} collective-permute-done((bf16[8,64,256]{2,1,0:T(8,128)(2,1)S(1)}, bf16[8,64,256]{2,1,0:T(8,128)(2,1)S(1)}, u32[]{:S(2)}, u32[]{:S(2)}) %collective-permute-start.5) | collective-permute-done | bytes 262176 | tf_op jit(solution)/shard_map/ppermute | solution.py:223
  26.7 1.6 %collective-permute-start.9 = (bf16[8,64,256]{2,1,0:T(8,128)(2,1)S(1)}, bf16[8,64,256]{2,1,0:T(8,128)(2,1)}, u32[]{:S(2)}, u32[]{:S(2)}) collective-permute-start(bf16[8,64,256]{2,1,0:T(8,128)(2,1)S(1)} %collective-permute-done.5.refs_3_), channel_id=1, source_target_pairs={{0,16},{16,0},{32,48},{48,32},{64,80},{80,64},{96,112},{112,96},{1... | collective-permute-start | bytes 786440 | tf_op jit(solution)/shard_map/ppermute | solution.py:229
  28.3 3.0 %collective-permute-done.4.refs_2_ = bf16[8,64,256]{2,1,0:T(8,128)(2,1)S(1)} collective-permute-done((bf16[8,64,256]{2,1,0:T(8,128)(2,1)S(1)}, bf16[8,64,256]{2,1,0:T(8,128)(2,1)S(1)}, u32[]{:S(2)}, u32[]{:S(2)}) %collective-permute-start.4) | collective-permute-done | bytes 262176 | tf_op jit(solution)/shard_map/ppermute | solution.py:223
  31.3 1.6 %collective-permute-start.8 = (bf16[8,64,256]{2,1,0:T(8,128)(2,1)S(1)}, bf16[8,64,256]{2,1,0:T(8,128)(2,1)}, u32[]{:S(2)}, u32[]{:S(2)}) collective-permute-start(bf16[8,64,256]{2,1,0:T(8,128)(2,1)S(1)} %collective-permute-done.4.refs_2_), channel_id=1, source_target_pairs={{0,16},{16,0},{32,48},{48,32},{64,80},{80,64},{96,112},{112,96},{1... | collective-permute-start | bytes 786440 | tf_op jit(solution)/shard_map/ppermute | solution.py:229
  32.9 0.9 collective-permute-start.11
  34.2 0.7 reduce
  35.0 0.7 reduce.1
  35.8 1.4 copy-done
  38.0 2.0 %collective-permute-done.11.refs_9_ = bf16[8,64,256]{2,1,0:T(8,128)(2,1)} collective-permute-done((bf16[8,64,256]{2,1,0:T(8,128)(2,1)S(1)}, bf16[8,64,256]{2,1,0:T(8,128)(2,1)}, u32[]{:S(2)}, u32[]{:S(2)}) %collective-permute-start.11) | collective-permute-done | bytes 262176 | tf_op jit(solution)/shard_map/ppermute | solution.py:227
  40.0 3.0 %aggregate.2 = (f32[4,128,256]{2,1,0:T(8,128)S(1)}, bf16[8,64,256]{2,1,0:T(8,128)(2,1)S(1)}, bf16[8,64,256]{2,1,0:T(8,128)(2,1)S(1)}, bf16[8,64,256]{2,1,0:T(8,128)(2,1)S(1)}) custom-call(s32[112]{0:T(128)S(1)} %concatenate.6.meta, bf16[3,16,128,128]{3,2,1,0:T(8,128)(2,1)S(1)} %keep.1.blocks, bf16[8,64,256]{2,1,0:T(8,128)(2,1)S(1)} %bitcast.13, ...), custom_call_target="tpu_custom_call" | custom-call | tf_op jit(solution)/shard_map/aggregate/pallas_call | solution.py:45
  43.0 2.2 %collective-permute-start.14 = (bf16[8,64,256]{2,1,0:T(8,128)(2,1)S(1)}, bf16[8,64,256]{2,1,0:T(8,128)(2,1)S(1)}, u32[]{:S(2)}, u32[]{:S(2)}) collective-permute-start(bf16[8,64,256]{2,1,0:T(8,128)(2,1)S(1)} %get-tuple-element.31), channel_id=1, source_target_pairs={{0,4},{1,5},{2,6},{3,7},{4,8},{5,9},{6,10},{7,11},{8,12},{9,13},{1... | collective-permute-start | bytes 786440 | tf_op jit(solution)/shard_map/ppermute | solution.py:216
  45.1 1.5 collective-permute-start.15
  46.6 2.5 %collective-permute-start.16 = (bf16[8,64,256]{2,1,0:T(8,128)(2,1)S(1)}, bf16[8,64,256]{2,1,0:T(8,128)(2,1)S(1)}, u32[]{:S(2)}, u32[]{:S(2)}) collective-permute-start(bf16[8,64,256]{2,1,0:T(8,128)(2,1)S(1)} %get-tuple-element.33), channel_id=1, source_target_pairs={{0,12},{1,13},{2,14},{3,15},{4,0},{5,1},{6,2},{7,3},{8,4},{9,5},{1... | collective-permute-start | bytes 786440 | tf_op jit(solution)/shard_map/ppermute | solution.py:216
  49.2 3.9 %collective-permute-done.14.one = bf16[8,64,256]{2,1,0:T(8,128)(2,1)S(1)} collective-permute-done((bf16[8,64,256]{2,1,0:T(8,128)(2,1)S(1)}, bf16[8,64,256]{2,1,0:T(8,128)(2,1)S(1)}, u32[]{:S(2)}, u32[]{:S(2)}) %collective-permute-start.14) | collective-permute-done | bytes 262176 | tf_op jit(solution)/shard_map/ppermute | solution.py:216
  53.0 5.5 %collective-permute-done.15.two = bf16[8,64,256]{2,1,0:T(8,128)(2,1)S(1)} collective-permute-done((bf16[8,64,256]{2,1,0:T(8,128)(2,1)S(1)}, bf16[8,64,256]{2,1,0:T(8,128)(2,1)S(1)}, u32[]{:S(2)}, u32[]{:S(2)}) %collective-permute-start.15) | collective-permute-done | bytes 262176 | tf_op jit(solution)/shard_map/ppermute | solution.py:216
  58.8 0.7 fold.1
  59.7 4.6 %collective-permute-start.18 = (bf16[2,64,256]{2,1,0:T(8,128)(2,1)S(1)}, bf16[2,64,256]{2,1,0:T(8,128)(2,1)S(1)}, u32[]{:S(2)}, u32[]{:S(2)}) collective-permute-start(bf16[2,64,256]{2,1,0:T(8,128)(2,1)S(1)} %get-tuple-element.36), channel_id=1, source_target_pairs={{0,2},{1,3},{2,0},{3,1},{4,6},{5,7},{6,4},{7,5},{8,10},{9,11},{10,... | collective-permute-start | bytes 196616 | tf_op jit(solution)/shard_map/ppermute | solution.py:216
  64.3 3.0 %collective-permute-start.19 = (bf16[2,64,256]{2,1,0:T(8,128)(2,1)S(1)}, bf16[2,64,256]{2,1,0:T(8,128)(2,1)S(1)}, u32[]{:S(2)}, u32[]{:S(2)}) collective-permute-start(bf16[2,64,256]{2,1,0:T(8,128)(2,1)S(1)} %get-tuple-element.37), channel_id=1, source_target_pairs={{0,3},{1,0},{2,1},{3,2},{4,7},{5,4},{6,5},{7,6},{8,11},{9,8},{10,9... | collective-permute-start | bytes 196616 | tf_op jit(solution)/shard_map/ppermute | solution.py:216
  67.3 0.7 collective-permute-done.17.one
  68.0 1.2 collective-permute-done.18.two
  69.2 2.1 %collective-permute-done.19.three = bf16[2,64,256]{2,1,0:T(8,128)(2,1)S(1)} collective-permute-done((bf16[2,64,256]{2,1,0:T(8,128)(2,1)S(1)}, bf16[2,64,256]{2,1,0:T(8,128)(2,1)S(1)}, u32[]{:S(2)}, u32[]{:S(2)}) %collective-permute-start.19) | collective-permute-done | bytes 65568 | tf_op jit(solution)/shard_map/ppermute | solution.py:216
  71.3 1.4 dense.1
  72.7 3.6 %collective-permute-start.20 = (bf16[3,64,256]{2,1,0:T(8,128)(2,1)S(1)}, bf16[3,64,256]{2,1,0:T(8,128)(2,1)S(1)}, u32[]{:S(2)}, u32[]{:S(2)}) collective-permute-start(bf16[3,64,256]{2,1,0:T(8,128)(2,1)S(1)} %get-tuple-element.40), channel_id=1, source_target_pairs={{0,3},{1,0},{2,1},{3,2},{4,7},{5,4},{6,5},{7,6},{8,11},{9,8},{10,9... | collective-permute-start | bytes 294920 | tf_op jit(solution)/shard_map/ppermute | solution.py:285
  76.3 2.4 %collective-permute-start.21 = (bf16[3,64,256]{2,1,0:T(8,128)(2,1)S(1)}, bf16[3,64,256]{2,1,0:T(8,128)(2,1)S(1)}, u32[]{:S(2)}, u32[]{:S(2)}) collective-permute-start(bf16[3,64,256]{2,1,0:T(8,128)(2,1)S(1)} %get-tuple-element.41), channel_id=1, source_target_pairs={{0,2},{1,3},{2,0},{3,1},{4,6},{5,7},{6,4},{7,5},{8,10},{9,11},{10,... | collective-permute-start | bytes 294920 | tf_op jit(solution)/shard_map/ppermute | solution.py:285
  79.0 5.1 %collective-permute-done.20.one = bf16[3,64,256]{2,1,0:T(8,128)(2,1)S(1)} collective-permute-done((bf16[3,64,256]{2,1,0:T(8,128)(2,1)S(1)}, bf16[3,64,256]{2,1,0:T(8,128)(2,1)S(1)}, u32[]{:S(2)}, u32[]{:S(2)}) %collective-permute-start.20) | collective-permute-done | bytes 98336 | tf_op jit(solution)/shard_map/ppermute | solution.py:285
  84.1 2.5 %collective-permute-done.21.two = bf16[3,64,256]{2,1,0:T(8,128)(2,1)S(1)} collective-permute-done((bf16[3,64,256]{2,1,0:T(8,128)(2,1)S(1)}, bf16[3,64,256]{2,1,0:T(8,128)(2,1)S(1)}, u32[]{:S(2)}, u32[]{:S(2)}) %collective-permute-start.21) | collective-permute-done | bytes 98336 | tf_op jit(solution)/shard_map/ppermute | solution.py:285
  87.0 1.6 %collective-permute-start.25 = (bf16[9,64,256]{2,1,0:T(8,128)(2,1)S(1)}, bf16[9,64,256]{2,1,0:T(8,128)(2,1)S(1)}, u32[]{:S(2)}, u32[]{:S(2)}) collective-permute-start(bf16[9,64,256]{2,1,0:T(8,128)(2,1)S(1)} %spread.1.refs_0_), channel_id=1, source_target_pairs={{0,4},{1,5},{2,6},{3,7},{4,8},{5,9},{6,10},{7,11},{8,12},{9,13},{1... | collective-permute-start | bytes 884744 | tf_op jit(solution)/shard_map/ppermute | solution.py:223
  88.6 2.8 %collective-permute-start.24 = (bf16[9,64,256]{2,1,0:T(8,128)(2,1)S(1)}, bf16[9,64,256]{2,1,0:T(8,128)(2,1)S(1)}, u32[]{:S(2)}, u32[]{:S(2)}) collective-permute-start(bf16[9,64,256]{2,1,0:T(8,128)(2,1)S(1)} %spread.1.refs_0_), channel_id=1, source_target_pairs={{0,12},{1,13},{2,14},{3,15},{4,0},{5,1},{6,2},{7,3},{8,4},{9,5},{1... | collective-permute-start | bytes 884744 | tf_op jit(solution)/shard_map/ppermute | solution.py:223
  91.4 1.4 collective-permute-start.23
  92.8 2.0 %collective-permute-start.28 = (bf16[9,64,256]{2,1,0:T(8,128)(2,1)S(1)}, bf16[9,64,256]{2,1,0:T(8,128)(2,1)S(1)}, u32[]{:S(2)}, u32[]{:S(2)}) collective-permute-start(bf16[9,64,256]{2,1,0:T(8,128)(2,1)S(1)} %spread.1.refs_0_), channel_id=1, source_target_pairs={{0,16},{16,0},{32,48},{48,32},{64,80},{80,64},{96,112},{112,96},{1... | collective-permute-start | bytes 884744 | tf_op jit(solution)/shard_map/ppermute | solution.py:220
  94.9 3.5 %collective-permute-done.25.refs_2_ = bf16[9,64,256]{2,1,0:T(8,128)(2,1)S(1)} collective-permute-done((bf16[9,64,256]{2,1,0:T(8,128)(2,1)S(1)}, bf16[9,64,256]{2,1,0:T(8,128)(2,1)S(1)}, u32[]{:S(2)}, u32[]{:S(2)}) %collective-permute-start.25) | collective-permute-done | bytes 294944 | tf_op jit(solution)/shard_map/ppermute | solution.py:223
  98.4 5.2 %collective-permute-done.24.refs_1_ = bf16[9,64,256]{2,1,0:T(8,128)(2,1)S(1)} collective-permute-done((bf16[9,64,256]{2,1,0:T(8,128)(2,1)S(1)}, bf16[9,64,256]{2,1,0:T(8,128)(2,1)S(1)}, u32[]{:S(2)}, u32[]{:S(2)}) %collective-permute-start.24) | collective-permute-done | bytes 294944 | tf_op jit(solution)/shard_map/ppermute | solution.py:223
  103.6 1.8 %collective-permute-done.23.refs_3_ = bf16[9,64,256]{2,1,0:T(8,128)(2,1)S(1)} collective-permute-done((bf16[9,64,256]{2,1,0:T(8,128)(2,1)S(1)}, bf16[9,64,256]{2,1,0:T(8,128)(2,1)S(1)}, u32[]{:S(2)}, u32[]{:S(2)}) %collective-permute-start.23) | collective-permute-done | bytes 294944 | tf_op jit(solution)/shard_map/ppermute | solution.py:223
  105.6 1.2 collective-permute-done.26
  107.2 1.9 %collective-permute-start.33 = (bf16[9,64,256]{2,1,0:T(8,128)(2,1)S(1)}, bf16[9,64,256]{2,1,0:T(8,128)(2,1)S(1)}, u32[]{:S(2)}, u32[]{:S(2)}) collective-permute-start(bf16[9,64,256]{2,1,0:T(8,128)(2,1)S(1)} %collective-permute-done.24.refs_1_), channel_id=1, source_target_pairs={{0,240},{16,32},{32,16},{48,64},{64,48},{80,96},{96,80},{112,128},... | collective-permute-start | bytes 884744 | tf_op jit(solution)/shard_map/ppermute | solution.py:227
  109.1 1.7 %collective-permute-start.29 = (bf16[9,64,256]{2,1,0:T(8,128)(2,1)S(1)}, bf16[9,64,256]{2,1,0:T(8,128)(2,1)S(1)}, u32[]{:S(2)}, u32[]{:S(2)}) collective-permute-start(bf16[9,64,256]{2,1,0:T(8,128)(2,1)S(1)} %collective-permute-done.24.refs_1_), channel_id=1, source_target_pairs={{0,16},{16,0},{32,48},{48,32},{64,80},{80,64},{96,112},{112,96},{1... | collective-permute-start | bytes 884744 | tf_op jit(solution)/shard_map/ppermute | solution.py:229
  110.8 1.1 collective-permute-done.27
  111.9 1.4 collective-permute-start.31
  113.3 1.0 collective-permute-done.33.refs_9_
  114.2 3.8 %collective-permute-done.35.refs_11_ = bf16[9,64,256]{2,1,0:T(8,128)(2,1)S(1)} collective-permute-done((bf16[9,64,256]{2,1,0:T(8,128)(2,1)S(1)}, bf16[9,64,256]{2,1,0:T(8,128)(2,1)S(1)}, u32[]{:S(2)}, u32[]{:S(2)}) %collective-permute-start.35) | collective-permute-done | bytes 294944 | tf_op jit(solution)/shard_map/ppermute | solution.py:227
  118.0 2.3 %aggregate.3 = (f32[4,128,256]{2,1,0:T(8,128)S(1)}, bf16[8,64,256]{2,1,0:T(8,128)(2,1)S(1)}, bf16[8,64,256]{2,1,0:T(8,128)(2,1)S(1)}, bf16[8,64,256]{2,1,0:T(8,128)(2,1)S(1)}) custom-call(s32[112]{0:T(128)S(1)} %concatenate.6.meta, bf16[3,16,128,128]{3,2,1,0:T(8,128)(2,1)S(1)} %keep.1.blocks, bf16[9,64,256]{2,1,0:T(8,128)(2,1)S(1)} %spread.1.refs_0_, ...), custom_call_target="tpu_custom_call" | custom-call | tf_op jit(solution)/shard_map/aggregate/pallas_call | solution.py:45
  120.3 1.5 collective-permute-start.36
  121.8 2.2 %collective-permute-start.37 = (bf16[8,64,256]{2,1,0:T(8,128)(2,1)S(1)}, bf16[8,64,256]{2,1,0:T(8,128)(2,1)S(1)}, u32[]{:S(2)}, u32[]{:S(2)}) collective-permute-start(bf16[8,64,256]{2,1,0:T(8,128)(2,1)S(1)} %get-tuple-element.47), channel_id=1, source_target_pairs={{0,8},{1,9},{2,10},{3,11},{4,12},{5,13},{6,14},{7,15},{8,0},{9,1},... | collective-permute-start | bytes 786440 | tf_op jit(solution)/shard_map/ppermute | solution.py:216
  124.6 1.7 %collective-permute-start.39 = (f32[64,256]{1,0:T(8,128)S(1)}, f32[64,256]{1,0:T(8,128)S(1)}, u32[]{:S(2)}, u32[]{:S(2)}) collective-permute-start(f32[64,256]{1,0:T(8,128)S(1)} %add.41), channel_id=1, source_target_pairs={{0,128},{16,144},{32,160},{48,176},{64,192},{80,208},{96,224},{112... | collective-permute-start | bytes 196616 | tf_op jit(solution)/shard_map/ppermute | solution.py:299
  126.3 2.6 %collective-permute-done.39 = f32[64,256]{1,0:T(8,128)S(1)} collective-permute-done((f32[64,256]{1,0:T(8,128)S(1)}, f32[64,256]{1,0:T(8,128)S(1)}, u32[]{:S(2)}, u32[]{:S(2)}) %collective-permute-start.39) | collective-permute-done | bytes 65568 | tf_op jit(solution)/shard_map/ppermute | solution.py:299
  128.9 3.8 %collective-permute-start.40 = (f32[64,256]{1,0:T(8,128)S(1)}, f32[64,256]{1,0:T(8,128)S(1)}, u32[]{:S(2)}, u32[]{:S(2)}) collective-permute-start(f32[64,256]{1,0:T(8,128)S(1)} %add.42), channel_id=1, source_target_pairs={{0,64},{16,80},{32,96},{48,112},{64,0},{80,16},{96,32},{112,48},{1... | collective-permute-start | bytes 196616 | tf_op jit(solution)/shard_map/ppermute | solution.py:299
  132.6 2.2 %collective-permute-done.40 = f32[64,256]{1,0:T(8,128)S(1)} collective-permute-done((f32[64,256]{1,0:T(8,128)S(1)}, f32[64,256]{1,0:T(8,128)S(1)}, u32[]{:S(2)}, u32[]{:S(2)}) %collective-permute-start.40) | collective-permute-done | bytes 65568 | tf_op jit(solution)/shard_map/ppermute | solution.py:299
  134.9 1.7 %collective-permute-done.37.two = bf16[8,64,256]{2,1,0:T(8,128)(2,1)S(1)} collective-permute-done((bf16[8,64,256]{2,1,0:T(8,128)(2,1)S(1)}, bf16[8,64,256]{2,1,0:T(8,128)(2,1)S(1)}, u32[]{:S(2)}, u32[]{:S(2)}) %collective-permute-start.37) | collective-permute-done | bytes 262176 | tf_op jit(solution)/shard_map/ppermute | solution.py:216
  136.6 0.7 fold_grad.1
  137.3 1.3 collective-permute-start.41
  138.6 3.6 %collective-permute-start.42 = (bf16[3,64,256]{2,1,0:T(8,128)(2,1)S(1)}, bf16[3,64,256]{2,1,0:T(8,128)(2,1)S(1)}, u32[]{:S(2)}, u32[]{:S(2)}) collective-permute-start(bf16[3,64,256]{2,1,0:T(8,128)(2,1)S(1)} %get-tuple-element.53), channel_id=1, source_target_pairs={{0,2},{1,3},{2,0},{3,1},{4,6},{5,7},{6,4},{7,5},{8,10},{9,11},{10,... | collective-permute-start | bytes 294920 | tf_op jit(solution)/shard_map/ppermute | solution.py:216
  142.2 2.8 %collective-permute-start.43 = (bf16[3,64,256]{2,1,0:T(8,128)(2,1)S(1)}, bf16[3,64,256]{2,1,0:T(8,128)(2,1)S(1)}, u32[]{:S(2)}, u32[]{:S(2)}) collective-permute-start(bf16[3,64,256]{2,1,0:T(8,128)(2,1)S(1)} %get-tuple-element.54), channel_id=1, source_target_pairs={{0,3},{1,0},{2,1},{3,2},{4,7},{5,4},{6,5},{7,6},{8,11},{9,8},{10,9... | collective-permute-start | bytes 294920 | tf_op jit(solution)/shard_map/ppermute | solution.py:216
  145.0 1.8 %collective-permute-done.41.one = bf16[3,64,256]{2,1,0:T(8,128)(2,1)S(1)} collective-permute-done((bf16[3,64,256]{2,1,0:T(8,128)(2,1)S(1)}, bf16[3,64,256]{2,1,0:T(8,128)(2,1)S(1)}, u32[]{:S(2)}, u32[]{:S(2)}) %collective-permute-start.41) | collective-permute-done | bytes 98336 | tf_op jit(solution)/shard_map/ppermute | solution.py:216
  146.7 1.5 collective-permute-done.42.two
  148.2 4.1 %collective-permute-done.43.three = bf16[3,64,256]{2,1,0:T(8,128)(2,1)S(1)} collective-permute-done((bf16[3,64,256]{2,1,0:T(8,128)(2,1)S(1)}, bf16[3,64,256]{2,1,0:T(8,128)(2,1)S(1)}, u32[]{:S(2)}, u32[]{:S(2)}) %collective-permute-start.43) | collective-permute-done | bytes 98336 | tf_op jit(solution)/shard_map/ppermute | solution.py:216
  152.3 1.3 finish.1
  (52 shorter events, 3.7 us)
Async XLA Ops:
  0.6 10.2 %collective-permute-start.1 = (bf16[128,256]{1,0:T(8,128)(2,1)}, bf16[128,256]{1,0:T(8,128)(2,1)S(1)}, u32[]{:S(2)}, u32[]{:S(2)}) collective-permute-start(bf16[128,256]{1,0:T(8,128)(2,1)} %param.7), channel_id=1, source_target_pairs={{0,2},{1,3},{2,0},{3,1},{4,6},{5,7},{6,4},{7,5},{8,10},{9,11},{10,... | collective-permute-start | bytes 196616 | tf_op jit(solution)/shard_map/ppermute | solution.py:211
  7.9 7.1 %collective-permute-start = (bf16[128,256]{1,0:T(8,128)(2,1)}, bf16[128,256]{1,0:T(8,128)(2,1)S(1)}, u32[]{:S(2)}, u32[]{:S(2)}) collective-permute-start(bf16[128,256]{1,0:T(8,128)(2,1)} %param.7), channel_id=1, source_target_pairs={{0,3},{1,0},{2,1},{3,2},{4,7},{5,4},{6,5},{7,6},{8,11},{9,8},{10,9... | collective-permute-start | bytes 196616 | tf_op jit(solution)/shard_map/ppermute | solution.py:211
  7.9 7.1 %collective-permute-start.2 = (bf16[128,256]{1,0:T(8,128)(2,1)}, bf16[128,256]{1,0:T(8,128)(2,1)S(1)}, u32[]{:S(2)}, u32[]{:S(2)}) collective-permute-start(bf16[128,256]{1,0:T(8,128)(2,1)} %param.7), channel_id=1, source_target_pairs={{0,1},{1,2},{2,3},{3,0},{4,5},{5,6},{6,7},{7,4},{8,9},{9,10},{10,1... | collective-permute-start | bytes 196616 | tf_op jit(solution)/shard_map/ppermute | solution.py:211
  15.9 10.8 %collective-permute-start.5 = (bf16[8,64,256]{2,1,0:T(8,128)(2,1)S(1)}, bf16[8,64,256]{2,1,0:T(8,128)(2,1)S(1)}, u32[]{:S(2)}, u32[]{:S(2)}) collective-permute-start(bf16[8,64,256]{2,1,0:T(8,128)(2,1)S(1)} %bitcast.8), channel_id=1, source_target_pairs={{0,8},{1,9},{2,10},{3,11},{4,12},{5,13},{6,14},{7,15},{8,0},{9,1},... | collective-permute-start | bytes 786440 | tf_op jit(solution)/shard_map/ppermute | solution.py:223
  19.2 7.5 %collective-permute-start.10 = (bf16[8,64,256]{2,1,0:T(8,128)(2,1)S(1)}, bf16[8,64,256]{2,1,0:T(8,128)(2,1)S(1)}, u32[]{:S(2)}, u32[]{:S(2)}) collective-permute-start(bf16[8,64,256]{2,1,0:T(8,128)(2,1)S(1)} %bitcast.9), channel_id=1, source_target_pairs={{0,240},{16,32},{32,16},{48,64},{64,48},{80,96},{96,80},{112,128},... | collective-permute-start | bytes 786440 | tf_op jit(solution)/shard_map/ppermute | solution.py:227
  19.2 12.1 %collective-permute-start.4 = (bf16[8,64,256]{2,1,0:T(8,128)(2,1)S(1)}, bf16[8,64,256]{2,1,0:T(8,128)(2,1)S(1)}, u32[]{:S(2)}, u32[]{:S(2)}) collective-permute-start(bf16[8,64,256]{2,1,0:T(8,128)(2,1)S(1)} %bitcast.10), channel_id=1, source_target_pairs={{0,4},{1,5},{2,6},{3,7},{4,8},{5,9},{6,10},{7,11},{8,12},{9,13},{1... | collective-permute-start | bytes 786440 | tf_op jit(solution)/shard_map/ppermute | solution.py:223
  19.9 11.4 %collective-permute-start.6 = (bf16[8,64,256]{2,1,0:T(8,128)(2,1)S(1)}, bf16[8,64,256]{2,1,0:T(8,128)(2,1)S(1)}, u32[]{:S(2)}, u32[]{:S(2)}) collective-permute-start(bf16[8,64,256]{2,1,0:T(8,128)(2,1)S(1)} %bitcast.11), channel_id=1, source_target_pairs={{0,16},{16,0},{32,48},{48,32},{64,80},{80,64},{96,112},{112,96},{1... | collective-permute-start | bytes 786440 | tf_op jit(solution)/shard_map/ppermute | solution.py:220
  21.2 11.7 %collective-permute-start.3 = (bf16[8,64,256]{2,1,0:T(8,128)(2,1)S(1)}, bf16[8,64,256]{2,1,0:T(8,128)(2,1)S(1)}, u32[]{:S(2)}, u32[]{:S(2)}) collective-permute-start(bf16[8,64,256]{2,1,0:T(8,128)(2,1)S(1)} %bitcast.12), channel_id=1, source_target_pairs={{0,12},{1,13},{2,14},{3,15},{4,0},{5,1},{6,2},{7,3},{8,4},{9,5},{1... | collective-permute-start | bytes 786440 | tf_op jit(solution)/shard_map/ppermute | solution.py:223
  26.7 7.1 %collective-permute-start.13 = (bf16[8,64,256]{2,1,0:T(8,128)(2,1)S(1)}, bf16[8,64,256]{2,1,0:T(8,128)(2,1)S(1)}, u32[]{:S(2)}, u32[]{:S(2)}) collective-permute-start(bf16[8,64,256]{2,1,0:T(8,128)(2,1)S(1)} %collective-permute-done.5.refs_3_), channel_id=1, source_target_pairs={{0,240},{16,32},{32,16},{48,64},{64,48},{80,96},{96,80},{112,128},... | collective-permute-start | bytes 786440 | tf_op jit(solution)/shard_map/ppermute | solution.py:227
  26.7 11.3 %collective-permute-start.9 = (bf16[8,64,256]{2,1,0:T(8,128)(2,1)S(1)}, bf16[8,64,256]{2,1,0:T(8,128)(2,1)}, u32[]{:S(2)}, u32[]{:S(2)}) collective-permute-start(bf16[8,64,256]{2,1,0:T(8,128)(2,1)S(1)} %collective-permute-done.5.refs_3_), channel_id=1, source_target_pairs={{0,16},{16,0},{32,48},{48,32},{64,80},{80,64},{96,112},{112,96},{1... | collective-permute-start | bytes 786440 | tf_op jit(solution)/shard_map/ppermute | solution.py:229
  31.3 6.7 %collective-permute-start.12 = (bf16[8,64,256]{2,1,0:T(8,128)(2,1)S(1)}, bf16[8,64,256]{2,1,0:T(8,128)(2,1)}, u32[]{:S(2)}, u32[]{:S(2)}) collective-permute-start(bf16[8,64,256]{2,1,0:T(8,128)(2,1)S(1)} %collective-permute-done.4.refs_2_), channel_id=1, source_target_pairs={{0,240},{16,32},{32,16},{48,64},{64,48},{80,96},{96,80},{112,128},... | collective-permute-start | bytes 786440 | tf_op jit(solution)/shard_map/ppermute | solution.py:227
  31.3 6.7 %collective-permute-start.8 = (bf16[8,64,256]{2,1,0:T(8,128)(2,1)S(1)}, bf16[8,64,256]{2,1,0:T(8,128)(2,1)}, u32[]{:S(2)}, u32[]{:S(2)}) collective-permute-start(bf16[8,64,256]{2,1,0:T(8,128)(2,1)S(1)} %collective-permute-done.4.refs_2_), channel_id=1, source_target_pairs={{0,16},{16,0},{32,48},{48,32},{64,80},{80,64},{96,112},{112,96},{1... | collective-permute-start | bytes 786440 | tf_op jit(solution)/shard_map/ppermute | solution.py:229
  32.9 7.1 %collective-permute-start.11 = (bf16[8,64,256]{2,1,0:T(8,128)(2,1)S(1)}, bf16[8,64,256]{2,1,0:T(8,128)(2,1)}, u32[]{:S(2)}, u32[]{:S(2)}) collective-permute-start(bf16[8,64,256]{2,1,0:T(8,128)(2,1)S(1)} %collective-permute-done.3.refs_1_), channel_id=1, source_target_pairs={{0,240},{16,32},{32,16},{48,64},{64,48},{80,96},{96,80},{112,128},... | collective-permute-start | bytes 786440 | tf_op jit(solution)/shard_map/ppermute | solution.py:227
  33.8 6.2 %collective-permute-start.7 = (bf16[8,64,256]{2,1,0:T(8,128)(2,1)S(1)}, bf16[8,64,256]{2,1,0:T(8,128)(2,1)}, u32[]{:S(2)}, u32[]{:S(2)}) collective-permute-start(bf16[8,64,256]{2,1,0:T(8,128)(2,1)S(1)} %collective-permute-done.3.refs_1_), channel_id=1, source_target_pairs={{0,16},{16,0},{32,48},{48,32},{64,80},{80,64},{96,112},{112,96},{1... | collective-permute-start | bytes 786440 | tf_op jit(solution)/shard_map/ppermute | solution.py:229
  35.8 1.4 copy-start
  37.2 0.7 copy-start.3
  37.9 33.4 %copy-start.1 = (bf16[256,256]{1,0:T(8,128)(2,1)S(1)}, bf16[256,256]{1,0:T(8,128)(2,1)}, u32[]{:S(2)}) copy-start(bf16[256,256]{1,0:T(8,128)(2,1)} %weight.1) | copy-start | bytes 393220
  37.9 33.4 %copy-start.2 = (bf16[128,256]{1,0:T(8,128)(2,1)S(1)}, bf16[128,256]{1,0:T(8,128)(2,1)}, u32[]{:S(2)}) copy-start(bf16[128,256]{1,0:T(8,128)(2,1)} %grad_out.1) | copy-start | bytes 196612
  43.0 10.1 %collective-permute-start.14 = (bf16[8,64,256]{2,1,0:T(8,128)(2,1)S(1)}, bf16[8,64,256]{2,1,0:T(8,128)(2,1)S(1)}, u32[]{:S(2)}, u32[]{:S(2)}) collective-permute-start(bf16[8,64,256]{2,1,0:T(8,128)(2,1)S(1)} %get-tuple-element.31), channel_id=1, source_target_pairs={{0,4},{1,5},{2,6},{3,7},{4,8},{5,9},{6,10},{7,11},{8,12},{9,13},{1... | collective-permute-start | bytes 786440 | tf_op jit(solution)/shard_map/ppermute | solution.py:216
  45.1 13.4 %collective-permute-start.15 = (bf16[8,64,256]{2,1,0:T(8,128)(2,1)S(1)}, bf16[8,64,256]{2,1,0:T(8,128)(2,1)S(1)}, u32[]{:S(2)}, u32[]{:S(2)}) collective-permute-start(bf16[8,64,256]{2,1,0:T(8,128)(2,1)S(1)} %get-tuple-element.32), channel_id=1, source_target_pairs={{0,8},{1,9},{2,10},{3,11},{4,12},{5,13},{6,14},{7,15},{8,0},{9,1},... | collective-permute-start | bytes 786440 | tf_op jit(solution)/shard_map/ppermute | solution.py:216
  46.6 12.2 %collective-permute-start.16 = (bf16[8,64,256]{2,1,0:T(8,128)(2,1)S(1)}, bf16[8,64,256]{2,1,0:T(8,128)(2,1)S(1)}, u32[]{:S(2)}, u32[]{:S(2)}) collective-permute-start(bf16[8,64,256]{2,1,0:T(8,128)(2,1)S(1)} %get-tuple-element.33), channel_id=1, source_target_pairs={{0,12},{1,13},{2,14},{3,15},{4,0},{5,1},{6,2},{7,3},{8,4},{9,5},{1... | collective-permute-start | bytes 786440 | tf_op jit(solution)/shard_map/ppermute | solution.py:216
  59.5 8.5 %collective-permute-start.17 = (bf16[2,64,256]{2,1,0:T(8,128)(2,1)S(1)}, bf16[2,64,256]{2,1,0:T(8,128)(2,1)S(1)}, u32[]{:S(2)}, u32[]{:S(2)}) collective-permute-start(bf16[2,64,256]{2,1,0:T(8,128)(2,1)S(1)} %get-tuple-element.35), channel_id=1, source_target_pairs={{0,1},{1,2},{2,3},{3,0},{4,5},{5,6},{6,7},{7,4},{8,9},{9,10},{10,1... | collective-permute-start | bytes 196616 | tf_op jit(solution)/shard_map/ppermute | solution.py:216
  59.7 9.5 %collective-permute-start.18 = (bf16[2,64,256]{2,1,0:T(8,128)(2,1)S(1)}, bf16[2,64,256]{2,1,0:T(8,128)(2,1)S(1)}, u32[]{:S(2)}, u32[]{:S(2)}) collective-permute-start(bf16[2,64,256]{2,1,0:T(8,128)(2,1)S(1)} %get-tuple-element.36), channel_id=1, source_target_pairs={{0,2},{1,3},{2,0},{3,1},{4,6},{5,7},{6,4},{7,5},{8,10},{9,11},{10,... | collective-permute-start | bytes 196616 | tf_op jit(solution)/shard_map/ppermute | solution.py:216
  64.3 7.0 %collective-permute-start.19 = (bf16[2,64,256]{2,1,0:T(8,128)(2,1)S(1)}, bf16[2,64,256]{2,1,0:T(8,128)(2,1)S(1)}, u32[]{:S(2)}, u32[]{:S(2)}) collective-permute-start(bf16[2,64,256]{2,1,0:T(8,128)(2,1)S(1)} %get-tuple-element.37), channel_id=1, source_target_pairs={{0,3},{1,0},{2,1},{3,2},{4,7},{5,4},{6,5},{7,6},{8,11},{9,8},{10,9... | collective-permute-start | bytes 196616 | tf_op jit(solution)/shard_map/ppermute | solution.py:216
  72.7 11.5 %collective-permute-start.20 = (bf16[3,64,256]{2,1,0:T(8,128)(2,1)S(1)}, bf16[3,64,256]{2,1,0:T(8,128)(2,1)S(1)}, u32[]{:S(2)}, u32[]{:S(2)}) collective-permute-start(bf16[3,64,256]{2,1,0:T(8,128)(2,1)S(1)} %get-tuple-element.40), channel_id=1, source_target_pairs={{0,3},{1,0},{2,1},{3,2},{4,7},{5,4},{6,5},{7,6},{8,11},{9,8},{10,9... | collective-permute-start | bytes 294920 | tf_op jit(solution)/shard_map/ppermute | solution.py:285
  76.3 10.4 %collective-permute-start.21 = (bf16[3,64,256]{2,1,0:T(8,128)(2,1)S(1)}, bf16[3,64,256]{2,1,0:T(8,128)(2,1)S(1)}, u32[]{:S(2)}, u32[]{:S(2)}) collective-permute-start(bf16[3,64,256]{2,1,0:T(8,128)(2,1)S(1)} %get-tuple-element.41), channel_id=1, source_target_pairs={{0,2},{1,3},{2,0},{3,1},{4,6},{5,7},{6,4},{7,5},{8,10},{9,11},{10,... | collective-permute-start | bytes 294920 | tf_op jit(solution)/shard_map/ppermute | solution.py:285
  78.7 8.3 %collective-permute-start.22 = (bf16[3,64,256]{2,1,0:T(8,128)(2,1)S(1)}, bf16[3,64,256]{2,1,0:T(8,128)(2,1)S(1)}, u32[]{:S(2)}, u32[]{:S(2)}) collective-permute-start(bf16[3,64,256]{2,1,0:T(8,128)(2,1)S(1)} %get-tuple-element.42), channel_id=1, source_target_pairs={{0,1},{1,2},{2,3},{3,0},{4,5},{5,6},{6,7},{7,4},{8,9},{9,10},{10,1... | collective-permute-start | bytes 294920 | tf_op jit(solution)/shard_map/ppermute | solution.py:285
  87.0 11.3 %collective-permute-start.25 = (bf16[9,64,256]{2,1,0:T(8,128)(2,1)S(1)}, bf16[9,64,256]{2,1,0:T(8,128)(2,1)S(1)}, u32[]{:S(2)}, u32[]{:S(2)}) collective-permute-start(bf16[9,64,256]{2,1,0:T(8,128)(2,1)S(1)} %spread.1.refs_0_), channel_id=1, source_target_pairs={{0,4},{1,5},{2,6},{3,7},{4,8},{5,9},{6,10},{7,11},{8,12},{9,13},{1... | collective-permute-start | bytes 884744 | tf_op jit(solution)/shard_map/ppermute | solution.py:223
  88.6 15.0 %collective-permute-start.24 = (bf16[9,64,256]{2,1,0:T(8,128)(2,1)S(1)}, bf16[9,64,256]{2,1,0:T(8,128)(2,1)S(1)}, u32[]{:S(2)}, u32[]{:S(2)}) collective-permute-start(bf16[9,64,256]{2,1,0:T(8,128)(2,1)S(1)} %spread.1.refs_0_), channel_id=1, source_target_pairs={{0,12},{1,13},{2,14},{3,15},{4,0},{5,1},{6,2},{7,3},{8,4},{9,5},{1... | collective-permute-start | bytes 884744 | tf_op jit(solution)/shard_map/ppermute | solution.py:223
  91.4 14.0 %collective-permute-start.23 = (bf16[9,64,256]{2,1,0:T(8,128)(2,1)S(1)}, bf16[9,64,256]{2,1,0:T(8,128)(2,1)S(1)}, u32[]{:S(2)}, u32[]{:S(2)}) collective-permute-start(bf16[9,64,256]{2,1,0:T(8,128)(2,1)S(1)} %spread.1.refs_0_), channel_id=1, source_target_pairs={{0,8},{1,9},{2,10},{3,11},{4,12},{5,13},{6,14},{7,15},{8,0},{9,1},... | collective-permute-start | bytes 884744 | tf_op jit(solution)/shard_map/ppermute | solution.py:223
  92.8 14.4 %collective-permute-start.32 = (bf16[9,64,256]{2,1,0:T(8,128)(2,1)S(1)}, bf16[9,64,256]{2,1,0:T(8,128)(2,1)S(1)}, u32[]{:S(2)}, u32[]{:S(2)}) collective-permute-start(bf16[9,64,256]{2,1,0:T(8,128)(2,1)S(1)} %spread.1.refs_0_), channel_id=1, source_target_pairs={{0,240},{16,32},{32,16},{48,64},{64,48},{80,96},{96,80},{112,128},... | collective-permute-start | bytes 884744 | tf_op jit(solution)/shard_map/ppermute | solution.py:227
  92.8 16.2 %collective-permute-start.28 = (bf16[9,64,256]{2,1,0:T(8,128)(2,1)S(1)}, bf16[9,64,256]{2,1,0:T(8,128)(2,1)S(1)}, u32[]{:S(2)}, u32[]{:S(2)}) collective-permute-start(bf16[9,64,256]{2,1,0:T(8,128)(2,1)S(1)} %spread.1.refs_0_), channel_id=1, source_target_pairs={{0,16},{16,0},{32,48},{48,32},{64,80},{80,64},{96,112},{112,96},{1... | collective-permute-start | bytes 884744 | tf_op jit(solution)/shard_map/ppermute | solution.py:220
  98.4 13.5 %collective-permute-start.34 = (bf16[9,64,256]{2,1,0:T(8,128)(2,1)S(1)}, bf16[9,64,256]{2,1,0:T(8,128)(2,1)S(1)}, u32[]{:S(2)}, u32[]{:S(2)}) collective-permute-start(bf16[9,64,256]{2,1,0:T(8,128)(2,1)S(1)} %collective-permute-done.25.refs_2_), channel_id=1, source_target_pairs={{0,240},{16,32},{32,16},{48,64},{64,48},{80,96},{96,80},{112,128},... | collective-permute-start | bytes 884744 | tf_op jit(solution)/shard_map/ppermute | solution.py:227
  105.5 1.3 collective-permute-start.26
  106.8 5.0 %collective-permute-start.27 = (f32[64,256]{1,0:T(8,128)S(1)}, f32[64,256]{1,0:T(8,128)S(1)}, u32[]{:S(2)}, u32[]{:S(2)}) collective-permute-start(f32[64,256]{1,0:T(8,128)S(1)} %add.40), channel_id=1, source_target_pairs={{0,32},{16,48},{32,0},{48,16},{64,96},{80,112},{96,64},{112,80},{1... | collective-permute-start | bytes 196616 | tf_op jit(solution)/shard_map/ppermute | solution.py:296
  106.9 6.3 %collective-permute-start.30 = (bf16[9,64,256]{2,1,0:T(8,128)(2,1)S(1)}, bf16[9,64,256]{2,1,0:T(8,128)(2,1)S(1)}, u32[]{:S(2)}, u32[]{:S(2)}) collective-permute-start(bf16[9,64,256]{2,1,0:T(8,128)(2,1)S(1)} %collective-permute-done.25.refs_2_), channel_id=1, source_target_pairs={{0,16},{16,0},{32,48},{48,32},{64,80},{80,64},{96,112},{112,96},{1... | collective-permute-start | bytes 884744 | tf_op jit(solution)/shard_map/ppermute | solution.py:229
  107.2 7.1 %collective-permute-start.33 = (bf16[9,64,256]{2,1,0:T(8,128)(2,1)S(1)}, bf16[9,64,256]{2,1,0:T(8,128)(2,1)S(1)}, u32[]{:S(2)}, u32[]{:S(2)}) collective-permute-start(bf16[9,64,256]{2,1,0:T(8,128)(2,1)S(1)} %collective-permute-done.24.refs_1_), channel_id=1, source_target_pairs={{0,240},{16,32},{32,16},{48,64},{64,48},{80,96},{96,80},{112,128},... | collective-permute-start | bytes 884744 | tf_op jit(solution)/shard_map/ppermute | solution.py:227
  109.1 5.2 %collective-permute-start.29 = (bf16[9,64,256]{2,1,0:T(8,128)(2,1)S(1)}, bf16[9,64,256]{2,1,0:T(8,128)(2,1)S(1)}, u32[]{:S(2)}, u32[]{:S(2)}) collective-permute-start(bf16[9,64,256]{2,1,0:T(8,128)(2,1)S(1)} %collective-permute-done.24.refs_1_), channel_id=1, source_target_pairs={{0,16},{16,0},{32,48},{48,32},{64,80},{80,64},{96,112},{112,96},{1... | collective-permute-start | bytes 884744 | tf_op jit(solution)/shard_map/ppermute | solution.py:229
  111.9 6.1 %collective-permute-start.35 = (bf16[9,64,256]{2,1,0:T(8,128)(2,1)S(1)}, bf16[9,64,256]{2,1,0:T(8,128)(2,1)S(1)}, u32[]{:S(2)}, u32[]{:S(2)}) collective-permute-start(bf16[9,64,256]{2,1,0:T(8,128)(2,1)S(1)} %collective-permute-done.23.refs_3_), channel_id=1, source_target_pairs={{0,240},{16,32},{32,16},{48,64},{64,48},{80,96},{96,80},{112,128},... | collective-permute-start | bytes 884744 | tf_op jit(solution)/shard_map/ppermute | solution.py:227
  111.9 6.1 %collective-permute-start.31 = (bf16[9,64,256]{2,1,0:T(8,128)(2,1)S(1)}, bf16[9,64,256]{2,1,0:T(8,128)(2,1)S(1)}, u32[]{:S(2)}, u32[]{:S(2)}) collective-permute-start(bf16[9,64,256]{2,1,0:T(8,128)(2,1)S(1)} %collective-permute-done.23.refs_3_), channel_id=1, source_target_pairs={{0,16},{16,0},{32,48},{48,32},{64,80},{80,64},{96,112},{112,96},{1... | collective-permute-start | bytes 884744 | tf_op jit(solution)/shard_map/ppermute | solution.py:229
  120.3 14.6 %collective-permute-start.36 = (bf16[8,64,256]{2,1,0:T(8,128)(2,1)S(1)}, bf16[8,64,256]{2,1,0:T(8,128)(2,1)S(1)}, u32[]{:S(2)}, u32[]{:S(2)}) collective-permute-start(bf16[8,64,256]{2,1,0:T(8,128)(2,1)S(1)} %get-tuple-element.46), channel_id=1, source_target_pairs={{0,4},{1,5},{2,6},{3,7},{4,8},{5,9},{6,10},{7,11},{8,12},{9,13},{1... | collective-permute-start | bytes 786440 | tf_op jit(solution)/shard_map/ppermute | solution.py:216
  121.8 14.8 %collective-permute-start.37 = (bf16[8,64,256]{2,1,0:T(8,128)(2,1)S(1)}, bf16[8,64,256]{2,1,0:T(8,128)(2,1)S(1)}, u32[]{:S(2)}, u32[]{:S(2)}) collective-permute-start(bf16[8,64,256]{2,1,0:T(8,128)(2,1)S(1)} %get-tuple-element.47), channel_id=1, source_target_pairs={{0,8},{1,9},{2,10},{3,11},{4,12},{5,13},{6,14},{7,15},{8,0},{9,1},... | collective-permute-start | bytes 786440 | tf_op jit(solution)/shard_map/ppermute | solution.py:216
  124.0 12.6 %collective-permute-start.38 = (bf16[8,64,256]{2,1,0:T(8,128)(2,1)S(1)}, bf16[8,64,256]{2,1,0:T(8,128)(2,1)S(1)}, u32[]{:S(2)}, u32[]{:S(2)}) collective-permute-start(bf16[8,64,256]{2,1,0:T(8,128)(2,1)S(1)} %get-tuple-element.48), channel_id=1, source_target_pairs={{0,12},{1,13},{2,14},{3,15},{4,0},{5,1},{6,2},{7,3},{8,4},{9,5},{1... | collective-permute-start | bytes 786440 | tf_op jit(solution)/shard_map/ppermute | solution.py:216
  124.6 4.3 %collective-permute-start.39 = (f32[64,256]{1,0:T(8,128)S(1)}, f32[64,256]{1,0:T(8,128)S(1)}, u32[]{:S(2)}, u32[]{:S(2)}) collective-permute-start(f32[64,256]{1,0:T(8,128)S(1)} %add.41), channel_id=1, source_target_pairs={{0,128},{16,144},{32,160},{48,176},{64,192},{80,208},{96,224},{112... | collective-permute-start | bytes 196616 | tf_op jit(solution)/shard_map/ppermute | solution.py:299
  128.9 6.0 %collective-permute-start.40 = (f32[64,256]{1,0:T(8,128)S(1)}, f32[64,256]{1,0:T(8,128)S(1)}, u32[]{:S(2)}, u32[]{:S(2)}) collective-permute-start(f32[64,256]{1,0:T(8,128)S(1)} %add.42), channel_id=1, source_target_pairs={{0,64},{16,80},{32,96},{48,112},{64,0},{80,16},{96,32},{112,48},{1... | collective-permute-start | bytes 196616 | tf_op jit(solution)/shard_map/ppermute | solution.py:299
  137.3 9.4 %collective-permute-start.41 = (bf16[3,64,256]{2,1,0:T(8,128)(2,1)S(1)}, bf16[3,64,256]{2,1,0:T(8,128)(2,1)S(1)}, u32[]{:S(2)}, u32[]{:S(2)}) collective-permute-start(bf16[3,64,256]{2,1,0:T(8,128)(2,1)S(1)} %get-tuple-element.52), channel_id=1, source_target_pairs={{0,1},{1,2},{2,3},{3,0},{4,5},{5,6},{6,7},{7,4},{8,9},{9,10},{10,1... | collective-permute-start | bytes 294920 | tf_op jit(solution)/shard_map/ppermute | solution.py:216
  138.6 9.6 %collective-permute-start.42 = (bf16[3,64,256]{2,1,0:T(8,128)(2,1)S(1)}, bf16[3,64,256]{2,1,0:T(8,128)(2,1)S(1)}, u32[]{:S(2)}, u32[]{:S(2)}) collective-permute-start(bf16[3,64,256]{2,1,0:T(8,128)(2,1)S(1)} %get-tuple-element.53), channel_id=1, source_target_pairs={{0,2},{1,3},{2,0},{3,1},{4,6},{5,7},{6,4},{7,5},{8,10},{9,11},{10,... | collective-permute-start | bytes 294920 | tf_op jit(solution)/shard_map/ppermute | solution.py:216
  142.2 10.1 %collective-permute-start.43 = (bf16[3,64,256]{2,1,0:T(8,128)(2,1)S(1)}, bf16[3,64,256]{2,1,0:T(8,128)(2,1)S(1)}, u32[]{:S(2)}, u32[]{:S(2)}) collective-permute-start(bf16[3,64,256]{2,1,0:T(8,128)(2,1)S(1)} %get-tuple-element.54), channel_id=1, source_target_pairs={{0,3},{1,0},{2,1},{3,2},{4,7},{5,4},{6,5},{7,6},{8,11},{9,8},{10,9... | collective-permute-start | bytes 294920 | tf_op jit(solution)/shard_map/ppermute | solution.py:216

commit v4 on v3

--- a/solution.py
+++ b/solution.py
@@ -14,7 +14,7 @@
 MIB = 1 << 20
 SIDE = 4
 PARTS = 1
-TURNS = (1, 3, 2)
+TURNS = (3, 1, 2)
 SLOTS = 16
 TOGETHER = 8
 COUNTS, ROWS, COLS = 3, 16, 64
@@ -205,6 +205,11 @@
     message[pl.ds(2 * SIDE, PARTS)] = split(total)
 
 
+def join_kernel(zero, one, two, three, quarter):
+    for k, ref in enumerate((zero, one, two, three)):
+        quarter[pl.ds(2 * k, 2)] = ref[...].reshape(2, -1, ref.shape[1])
+
+
 def side_of(block, route, order=(1, 2, 3)):
     got = {0: block}
     for k in order:
@@ -213,7 +218,8 @@
 
 
 def three_ways(sends, route):
-    return [lax.ppermute(s, "team", route(k)) for k, s in enumerate(sends, 1)]
+    got = {k: lax.ppermute(sends[k - 1], "team", route(k)) for k in (2, 1, 3)}
+    return [got[k] for k in range(1, SIDE)]
 
 
 def slabs_of(message):
@@ -263,8 +269,12 @@
         [whole(pl.ANY)],
         [pltpu.SemaphoreType.DMA],
     )
-    quarter = jnp.concatenate(side_of(features, along_z), axis=0)
-    quarter = quarter.reshape(2 * SIDE, half, width)
+    [quarter] = call(
+        join_kernel,
+        [((2 * SIDE, half, width), BF)],
+        side_of(features, along_z),
+        [whole()] * SIDE,
+    )
     own, *sends = aggregate(meta, slabs_of(quarter)[1], blocks)
     arrived = three_ways(sends, along_y)
     kept, *sends = call(

time: 155 us -> 157 us (1.013); the launches traced: 154 us -> 154 us
  starting transfers between devices: 73.6 us -> 68.6 us
  waiting for transfers between devices: 65.3 us -> 69.9 us
    ppermute x12, starting transfers between devices: 26 us -> 23.2 us  [three_ways(): got = {k: lax.ppermute(sends[k - 1], 'team', route(k)) for k in (2, 1, 3)}]
    ppermute x12, waiting for transfers between devices: 22.7 us -> 24.8 us  [three_ways(): got = {k: lax.ppermute(sends[k - 1], 'team', route(k)) for k in (2, 1, 3)}]
    ppermute x4, starting transfers between devices: 5.65 us -> 3.69 us  [on_device(): grad = grad + lax.ppermute(grad, 'blk', flipped(bit))]
    ppermute x6, waiting for transfers between devices: 16.5 us -> 18.3 us  [slabs_of(): messages[k] = lax.ppermute(message, 'team', along_y(-k))]
    pallas_call x8 -> x9, Pallas kernels: 9.39 us -> 10 us  [call(): pl.pallas_call(kernel, in_specs=specs, out_specs=[whole()] * len(outs), o...]
where the time goes in v4:
time: 157 us; the launch traced here: 154 us
  waiting for transfers between devices  69.9 us (45%)
  starting transfers between devices  68.6 us (44%)
  Pallas kernels  10 us (6%)
  local copies, waits for them, and re-layouts  3.01 us (2%)
    ppermute x12, waiting for transfers between devices, three_ways(): got = {k: lax.ppermute(sends[k - 1], 'team', route(k)) for k in (2, 1, 3)}  24.8 us
    ppermute x12, starting transfers between devices, three_ways(): got = {k: lax.ppermute(sends[k - 1], 'team', route(k)) for k in (2, 1, 3)}  23.2 us
    ppermute x6, waiting for transfers between devices, slabs_of(): messages[k] = lax.ppermute(message, 'team', along_y(-k))  18.3 us
    ppermute x6, starting transfers between devices, slabs_of(): messages[k] = lax.ppermute(message, 'team', along_y(-k))  12 us
    ppermute x3, starting transfers between devices, side_of(): got[k] = lax.ppermute(block, 'team', route(-k))  10.2 us
    pallas_call x9, Pallas kernels, call(): pl.pallas_call(kernel, in_specs=specs, out_specs=[whole()] * len(outs), o...  10 us
    ppermute x4, waiting for transfers between devices, on_device(): grad = grad + lax.ppermute(grad, 'blk', flipped(bit))  8.69 us
    ppermute x3, waiting for transfers between devices, on_device(): lax.ppermute(s, 'team', along_z(-k))  7.51 us
  transfers between devices with their start and end apart: 44, of which 26 were waited for; matrix products, arithmetic and copies ran while one was open for 1% of the time, Pallas kernels for 0%

profile of v4, /device:TPU:2, one launch (start us, length us, event | category | flops | bytes accessed | tf_op | source)
XLA Modules:
  0.0 153.8 jit_solution(3500246600828231779)
XLA Ops:
  0.6 7.3 %collective-permute-start.1 = (bf16[128,256]{1,0:T(8,128)(2,1)}, bf16[128,256]{1,0:T(8,128)(2,1)S(1)}, u32[]{:S(2)}, u32[]{:S(2)}) collective-permute-start(bf16[128,256]{1,0:T(8,128)(2,1)} %zero.1), channel_id=1, source_target_pairs={{0,2},{1,3},{2,0},{3,1},{4,6},{5,7},{6,4},{7,5},{8,10},{9,11},{10,... | collective-permute-start | bytes 196616 | tf_op jit(solution)/shard_map/ppermute | solution.py:216
  7.9 2.9 %collective-permute-start.2 = (bf16[128,256]{1,0:T(8,128)(2,1)}, bf16[128,256]{1,0:T(8,128)(2,1)S(1)}, u32[]{:S(2)}, u32[]{:S(2)}) collective-permute-start(bf16[128,256]{1,0:T(8,128)(2,1)} %zero.1), channel_id=1, source_target_pairs={{0,1},{1,2},{2,3},{3,0},{4,5},{5,6},{6,7},{7,4},{8,9},{9,10},{10,1... | collective-permute-start | bytes 196616 | tf_op jit(solution)/shard_map/ppermute | solution.py:216
  10.8 4.2 %collective-permute-done.one = bf16[128,256]{1,0:T(8,128)(2,1)S(1)} collective-permute-done((bf16[128,256]{1,0:T(8,128)(2,1)}, bf16[128,256]{1,0:T(8,128)(2,1)S(1)}, u32[]{:S(2)}, u32[]{:S(2)}) %collective-permute-start) | collective-permute-done | bytes 65568 | tf_op jit(solution)/shard_map/ppermute | solution.py:216
  15.0 0.8 copy-done.3
  15.9 3.3 %collective-permute-start.5 = (bf16[8,64,256]{2,1,0:T(8,128)(2,1)S(1)}, bf16[8,64,256]{2,1,0:T(8,128)(2,1)S(1)}, u32[]{:S(2)}, u32[]{:S(2)}) collective-permute-start(bf16[8,64,256]{2,1,0:T(8,128)(2,1)S(1)} %join.1.refs_0_), channel_id=1, source_target_pairs={{0,8},{1,9},{2,10},{3,11},{4,12},{5,13},{6,14},{7,15},{8,0},{9,1},... | collective-permute-start | bytes 786440 | tf_op jit(solution)/shard_map/ppermute | solution.py:229
  19.2 1.1 collective-permute-start.4
  20.2 1.3 collective-permute-start.6
  21.6 1.0 collective-permute-start.3
  22.5 4.1 %collective-permute-done.5.refs_3_ = bf16[8,64,256]{2,1,0:T(8,128)(2,1)S(1)} collective-permute-done((bf16[8,64,256]{2,1,0:T(8,128)(2,1)S(1)}, bf16[8,64,256]{2,1,0:T(8,128)(2,1)S(1)}, u32[]{:S(2)}, u32[]{:S(2)}) %collective-permute-start.5) | collective-permute-done | bytes 262176 | tf_op jit(solution)/shard_map/ppermute | solution.py:229
  26.7 1.6 %collective-permute-start.9 = (bf16[8,64,256]{2,1,0:T(8,128)(2,1)S(1)}, bf16[8,64,256]{2,1,0:T(8,128)(2,1)}, u32[]{:S(2)}, u32[]{:S(2)}) collective-permute-start(bf16[8,64,256]{2,1,0:T(8,128)(2,1)S(1)} %collective-permute-done.5.refs_3_), channel_id=1, source_target_pairs={{0,16},{16,0},{32,48},{48,32},{64,80},{80,64},{96,112},{112,96},{1... | collective-permute-start | bytes 786440 | tf_op jit(solution)/shard_map/ppermute | solution.py:235
  28.3 3.4 %collective-permute-done.4.refs_2_ = bf16[8,64,256]{2,1,0:T(8,128)(2,1)S(1)} collective-permute-done((bf16[8,64,256]{2,1,0:T(8,128)(2,1)S(1)}, bf16[8,64,256]{2,1,0:T(8,128)(2,1)S(1)}, u32[]{:S(2)}, u32[]{:S(2)}) %collective-permute-start.4) | collective-permute-done | bytes 262176 | tf_op jit(solution)/shard_map/ppermute | solution.py:229
  31.7 1.6 %collective-permute-start.8 = (bf16[8,64,256]{2,1,0:T(8,128)(2,1)S(1)}, bf16[8,64,256]{2,1,0:T(8,128)(2,1)}, u32[]{:S(2)}, u32[]{:S(2)}) collective-permute-start(bf16[8,64,256]{2,1,0:T(8,128)(2,1)S(1)} %collective-permute-done.4.refs_2_), channel_id=1, source_target_pairs={{0,16},{16,0},{32,48},{48,32},{64,80},{80,64},{96,112},{112,96},{1... | collective-permute-start | bytes 786440 | tf_op jit(solution)/shard_map/ppermute | solution.py:235
  33.6 1.1 collective-permute-start.7
  34.6 0.7 reduce
  35.4 0.7 reduce.1
  36.2 1.4 copy-done
  38.4 2.0 %collective-permute-done.11.refs_9_ = bf16[8,64,256]{2,1,0:T(8,128)(2,1)} collective-permute-done((bf16[8,64,256]{2,1,0:T(8,128)(2,1)S(1)}, bf16[8,64,256]{2,1,0:T(8,128)(2,1)}, u32[]{:S(2)}, u32[]{:S(2)}) %collective-permute-start.11) | collective-permute-done | bytes 262176 | tf_op jit(solution)/shard_map/ppermute | solution.py:233
  40.4 3.3 %aggregate.2 = (f32[4,128,256]{2,1,0:T(8,128)S(1)}, bf16[8,64,256]{2,1,0:T(8,128)(2,1)S(1)}, bf16[8,64,256]{2,1,0:T(8,128)(2,1)S(1)}, bf16[8,64,256]{2,1,0:T(8,128)(2,1)S(1)}) custom-call(s32[112]{0:T(128)S(1)} %concatenate.3.meta, bf16[3,16,128,128]{3,2,1,0:T(8,128)(2,1)S(1)} %keep.1.blocks, bf16[8,64,256]{2,1,0:T(8,128)(2,1)S(1)} %join.1.refs_0_, ...), custom_call_target="tpu_custom_call" | custom-call | tf_op jit(solution)/shard_map/aggregate/pallas_call | solution.py:45
  43.7 1.2 collective-permute-start.14
  44.9 2.9 %collective-permute-start.15 = (bf16[8,64,256]{2,1,0:T(8,128)(2,1)S(1)}, bf16[8,64,256]{2,1,0:T(8,128)(2,1)S(1)}, u32[]{:S(2)}, u32[]{:S(2)}) collective-permute-start(bf16[8,64,256]{2,1,0:T(8,128)(2,1)S(1)} %get-tuple-element.32), channel_id=1, source_target_pairs={{0,8},{1,9},{2,10},{3,11},{4,12},{5,13},{6,14},{7,15},{8,0},{9,1},... | collective-permute-start | bytes 786440 | tf_op jit(solution)/shard_map/ppermute | solution.py:221
  48.3 4.8 %collective-permute-done.14.one = bf16[8,64,256]{2,1,0:T(8,128)(2,1)S(1)} collective-permute-done((bf16[8,64,256]{2,1,0:T(8,128)(2,1)S(1)}, bf16[8,64,256]{2,1,0:T(8,128)(2,1)S(1)}, u32[]{:S(2)}, u32[]{:S(2)}) %collective-permute-start.14) | collective-permute-done | bytes 262176 | tf_op jit(solution)/shard_map/ppermute | solution.py:221
  53.0 6.7 %collective-permute-done.15.two = bf16[8,64,256]{2,1,0:T(8,128)(2,1)S(1)} collective-permute-done((bf16[8,64,256]{2,1,0:T(8,128)(2,1)S(1)}, bf16[8,64,256]{2,1,0:T(8,128)(2,1)S(1)}, u32[]{:S(2)}, u32[]{:S(2)}) %collective-permute-start.15) | collective-permute-done | bytes 262176 | tf_op jit(solution)/shard_map/ppermute | solution.py:221
  59.8 0.7 fold.1
  60.5 5.0 %collective-permute-start.18 = (bf16[2,64,256]{2,1,0:T(8,128)(2,1)S(1)}, bf16[2,64,256]{2,1,0:T(8,128)(2,1)S(1)}, u32[]{:S(2)}, u32[]{:S(2)}) collective-permute-start(bf16[2,64,256]{2,1,0:T(8,128)(2,1)S(1)} %get-tuple-element.36), channel_id=1, source_target_pairs={{0,2},{1,3},{2,0},{3,1},{4,6},{5,7},{6,4},{7,5},{8,10},{9,11},{10,... | collective-permute-start | bytes 196616 | tf_op jit(solution)/shard_map/ppermute | solution.py:221
  65.5 2.6 %collective-permute-start.19 = (bf16[2,64,256]{2,1,0:T(8,128)(2,1)S(1)}, bf16[2,64,256]{2,1,0:T(8,128)(2,1)S(1)}, u32[]{:S(2)}, u32[]{:S(2)}) collective-permute-start(bf16[2,64,256]{2,1,0:T(8,128)(2,1)S(1)} %get-tuple-element.37), channel_id=1, source_target_pairs={{0,3},{1,0},{2,1},{3,2},{4,7},{5,4},{6,5},{7,6},{8,11},{9,8},{10,9... | collective-permute-start | bytes 196616 | tf_op jit(solution)/shard_map/ppermute | solution.py:221
  68.1 0.7 collective-permute-done.17.one
  68.8 0.8 collective-permute-done.18.two
  69.7 2.2 %collective-permute-done.19.three = bf16[2,64,256]{2,1,0:T(8,128)(2,1)S(1)} collective-permute-done((bf16[2,64,256]{2,1,0:T(8,128)(2,1)S(1)}, bf16[2,64,256]{2,1,0:T(8,128)(2,1)S(1)}, u32[]{:S(2)}, u32[]{:S(2)}) %collective-permute-start.19) | collective-permute-done | bytes 65568 | tf_op jit(solution)/shard_map/ppermute | solution.py:221
  71.9 1.4 dense.1
  73.3 3.3 %collective-permute-start.20 = (bf16[3,64,256]{2,1,0:T(8,128)(2,1)S(1)}, bf16[3,64,256]{2,1,0:T(8,128)(2,1)S(1)}, u32[]{:S(2)}, u32[]{:S(2)}) collective-permute-start(bf16[3,64,256]{2,1,0:T(8,128)(2,1)S(1)} %get-tuple-element.40), channel_id=1, source_target_pairs={{0,3},{1,0},{2,1},{3,2},{4,7},{5,4},{6,5},{7,6},{8,11},{9,8},{10,9... | collective-permute-start | bytes 294920 | tf_op jit(solution)/shard_map/ppermute | solution.py:295
  76.6 2.4 %collective-permute-start.21 = (bf16[3,64,256]{2,1,0:T(8,128)(2,1)S(1)}, bf16[3,64,256]{2,1,0:T(8,128)(2,1)S(1)}, u32[]{:S(2)}, u32[]{:S(2)}) collective-permute-start(bf16[3,64,256]{2,1,0:T(8,128)(2,1)S(1)} %get-tuple-element.41), channel_id=1, source_target_pairs={{0,2},{1,3},{2,0},{3,1},{4,6},{5,7},{6,4},{7,5},{8,10},{9,11},{10,... | collective-permute-start | bytes 294920 | tf_op jit(solution)/shard_map/ppermute | solution.py:295
  79.1 1.4 collective-permute-done.20.one
  80.5 5.5 %collective-permute-done.21.two = bf16[3,64,256]{2,1,0:T(8,128)(2,1)S(1)} collective-permute-done((bf16[3,64,256]{2,1,0:T(8,128)(2,1)S(1)}, bf16[3,64,256]{2,1,0:T(8,128)(2,1)S(1)}, u32[]{:S(2)}, u32[]{:S(2)}) %collective-permute-start.21) | collective-permute-done | bytes 98336 | tf_op jit(solution)/shard_map/ppermute | solution.py:295
  86.7 3.8 %collective-permute-start.25 = (bf16[9,64,256]{2,1,0:T(8,128)(2,1)S(1)}, bf16[9,64,256]{2,1,0:T(8,128)(2,1)S(1)}, u32[]{:S(2)}, u32[]{:S(2)}) collective-permute-start(bf16[9,64,256]{2,1,0:T(8,128)(2,1)S(1)} %spread.1.refs_0_), channel_id=1, source_target_pairs={{0,4},{1,5},{2,6},{3,7},{4,8},{5,9},{6,10},{7,11},{8,12},{9,13},{1... | collective-permute-start | bytes 884744 | tf_op jit(solution)/shard_map/ppermute | solution.py:229
  90.5 1.5 collective-permute-start.24
  92.0 1.4 collective-permute-start.23
  93.4 1.9 %collective-permute-start.28 = (bf16[9,64,256]{2,1,0:T(8,128)(2,1)S(1)}, bf16[9,64,256]{2,1,0:T(8,128)(2,1)S(1)}, u32[]{:S(2)}, u32[]{:S(2)}) collective-permute-start(bf16[9,64,256]{2,1,0:T(8,128)(2,1)S(1)} %spread.1.refs_0_), channel_id=1, source_target_pairs={{0,16},{16,0},{32,48},{48,32},{64,80},{80,64},{96,112},{112,96},{1... | collective-permute-start | bytes 884744 | tf_op jit(solution)/shard_map/ppermute | solution.py:226
  95.3 3.6 %collective-permute-done.25.refs_1_ = bf16[9,64,256]{2,1,0:T(8,128)(2,1)S(1)} collective-permute-done((bf16[9,64,256]{2,1,0:T(8,128)(2,1)S(1)}, bf16[9,64,256]{2,1,0:T(8,128)(2,1)S(1)}, u32[]{:S(2)}, u32[]{:S(2)}) %collective-permute-start.25) | collective-permute-done | bytes 294944 | tf_op jit(solution)/shard_map/ppermute | solution.py:229
  98.9 5.3 %collective-permute-done.24.refs_2_ = bf16[9,64,256]{2,1,0:T(8,128)(2,1)S(1)} collective-permute-done((bf16[9,64,256]{2,1,0:T(8,128)(2,1)S(1)}, bf16[9,64,256]{2,1,0:T(8,128)(2,1)S(1)}, u32[]{:S(2)}, u32[]{:S(2)}) %collective-permute-start.24) | collective-permute-done | bytes 294944 | tf_op jit(solution)/shard_map/ppermute | solution.py:229
  104.2 1.8 %collective-permute-done.23.refs_3_ = bf16[9,64,256]{2,1,0:T(8,128)(2,1)S(1)} collective-permute-done((bf16[9,64,256]{2,1,0:T(8,128)(2,1)S(1)}, bf16[9,64,256]{2,1,0:T(8,128)(2,1)S(1)}, u32[]{:S(2)}, u32[]{:S(2)}) %collective-permute-start.23) | collective-permute-done | bytes 294944 | tf_op jit(solution)/shard_map/ppermute | solution.py:229
  106.2 1.2 collective-permute-done.26
  107.8 1.9 %collective-permute-start.34 = (bf16[9,64,256]{2,1,0:T(8,128)(2,1)S(1)}, bf16[9,64,256]{2,1,0:T(8,128)(2,1)S(1)}, u32[]{:S(2)}, u32[]{:S(2)}) collective-permute-start(bf16[9,64,256]{2,1,0:T(8,128)(2,1)S(1)} %collective-permute-done.24.refs_2_), channel_id=1, source_target_pairs={{0,240},{16,32},{32,16},{48,64},{64,48},{80,96},{96,80},{112,128},... | collective-permute-start | bytes 884744 | tf_op jit(solution)/shard_map/ppermute | solution.py:233
  109.7 2.0 %collective-permute-start.30 = (bf16[9,64,256]{2,1,0:T(8,128)(2,1)S(1)}, bf16[9,64,256]{2,1,0:T(8,128)(2,1)S(1)}, u32[]{:S(2)}, u32[]{:S(2)}) collective-permute-start(bf16[9,64,256]{2,1,0:T(8,128)(2,1)S(1)} %collective-permute-done.24.refs_2_), channel_id=1, source_target_pairs={{0,16},{16,0},{32,48},{48,32},{64,80},{80,64},{96,112},{112,96},{1... | collective-permute-start | bytes 884744 | tf_op jit(solution)/shard_map/ppermute | solution.py:235
  111.6 0.8 collective-permute-done.27
  112.4 0.8 collective-permute-start.35
  113.3 0.9 collective-permute-start.31
  114.2 0.6 collective-permute-done.34.refs_10_
  114.8 3.8 %collective-permute-done.35.refs_11_ = bf16[9,64,256]{2,1,0:T(8,128)(2,1)S(1)} collective-permute-done((bf16[9,64,256]{2,1,0:T(8,128)(2,1)S(1)}, bf16[9,64,256]{2,1,0:T(8,128)(2,1)S(1)}, u32[]{:S(2)}, u32[]{:S(2)}) %collective-permute-start.35) | collective-permute-done | bytes 294944 | tf_op jit(solution)/shard_map/ppermute | solution.py:233
  118.6 2.6 %aggregate.3 = (f32[4,128,256]{2,1,0:T(8,128)S(1)}, bf16[8,64,256]{2,1,0:T(8,128)(2,1)S(1)}, bf16[8,64,256]{2,1,0:T(8,128)(2,1)S(1)}, bf16[8,64,256]{2,1,0:T(8,128)(2,1)S(1)}) custom-call(s32[112]{0:T(128)S(1)} %concatenate.3.meta, bf16[3,16,128,128]{3,2,1,0:T(8,128)(2,1)S(1)} %keep.1.blocks, bf16[9,64,256]{2,1,0:T(8,128)(2,1)S(1)} %spread.1.refs_0_, ...), custom_call_target="tpu_custom_call" | custom-call | tf_op jit(solution)/shard_map/aggregate/pallas_call | solution.py:45
  121.2 1.2 collective-permute-start.36
  122.4 2.2 %collective-permute-start.37 = (bf16[8,64,256]{2,1,0:T(8,128)(2,1)S(1)}, bf16[8,64,256]{2,1,0:T(8,128)(2,1)S(1)}, u32[]{:S(2)}, u32[]{:S(2)}) collective-permute-start(bf16[8,64,256]{2,1,0:T(8,128)(2,1)S(1)} %get-tuple-element.47), channel_id=1, source_target_pairs={{0,8},{1,9},{2,10},{3,11},{4,12},{5,13},{6,14},{7,15},{8,0},{9,1},... | collective-permute-start | bytes 786440 | tf_op jit(solution)/shard_map/ppermute | solution.py:221
  124.6 0.6 collective-permute-start.38
  125.2 4.3 %collective-permute-done.39 = f32[64,256]{1,0:T(8,128)S(1)} collective-permute-done((f32[64,256]{1,0:T(8,128)S(1)}, f32[64,256]{1,0:T(8,128)S(1)}, u32[]{:S(2)}, u32[]{:S(2)}) %collective-permute-start.39) | collective-permute-done | bytes 65568 | tf_op jit(solution)/shard_map/ppermute | solution.py:309
  129.4 3.5 %collective-permute-start.40 = (f32[64,256]{1,0:T(8,128)S(1)}, f32[64,256]{1,0:T(8,128)S(1)}, u32[]{:S(2)}, u32[]{:S(2)}) collective-permute-start(f32[64,256]{1,0:T(8,128)S(1)} %add.42), channel_id=1, source_target_pairs={{0,64},{16,80},{32,96},{48,112},{64,0},{80,16},{96,32},{112,48},{1... | collective-permute-start | bytes 196616 | tf_op jit(solution)/shard_map/ppermute | solution.py:309
  132.9 2.3 %collective-permute-done.40 = f32[64,256]{1,0:T(8,128)S(1)} collective-permute-done((f32[64,256]{1,0:T(8,128)S(1)}, f32[64,256]{1,0:T(8,128)S(1)}, u32[]{:S(2)}, u32[]{:S(2)}) %collective-permute-start.40) | collective-permute-done | bytes 65568 | tf_op jit(solution)/shard_map/ppermute | solution.py:309
  135.3 1.6 %collective-permute-done.37.two = bf16[8,64,256]{2,1,0:T(8,128)(2,1)S(1)} collective-permute-done((bf16[8,64,256]{2,1,0:T(8,128)(2,1)S(1)}, bf16[8,64,256]{2,1,0:T(8,128)(2,1)S(1)}, u32[]{:S(2)}, u32[]{:S(2)}) %collective-permute-start.37) | collective-permute-done | bytes 262176 | tf_op jit(solution)/shard_map/ppermute | solution.py:221
  137.2 0.7 fold_grad.1
  137.9 1.8 %collective-permute-start.41 = (bf16[3,64,256]{2,1,0:T(8,128)(2,1)S(1)}, bf16[3,64,256]{2,1,0:T(8,128)(2,1)S(1)}, u32[]{:S(2)}, u32[]{:S(2)}) collective-permute-start(bf16[3,64,256]{2,1,0:T(8,128)(2,1)S(1)} %get-tuple-element.52), channel_id=1, source_target_pairs={{0,1},{1,2},{2,3},{3,0},{4,5},{5,6},{6,7},{7,4},{8,9},{9,10},{10,1... | collective-permute-start | bytes 294920 | tf_op jit(solution)/shard_map/ppermute | solution.py:221
  139.6 3.4 %collective-permute-start.42 = (bf16[3,64,256]{2,1,0:T(8,128)(2,1)S(1)}, bf16[3,64,256]{2,1,0:T(8,128)(2,1)S(1)}, u32[]{:S(2)}, u32[]{:S(2)}) collective-permute-start(bf16[3,64,256]{2,1,0:T(8,128)(2,1)S(1)} %get-tuple-element.53), channel_id=1, source_target_pairs={{0,2},{1,3},{2,0},{3,1},{4,6},{5,7},{6,4},{7,5},{8,10},{9,11},{10,... | collective-permute-start | bytes 294920 | tf_op jit(solution)/shard_map/ppermute | solution.py:221
  143.0 1.8 %collective-permute-start.43 = (bf16[3,64,256]{2,1,0:T(8,128)(2,1)S(1)}, bf16[3,64,256]{2,1,0:T(8,128)(2,1)S(1)}, u32[]{:S(2)}, u32[]{:S(2)}) collective-permute-start(bf16[3,64,256]{2,1,0:T(8,128)(2,1)S(1)} %get-tuple-element.54), channel_id=1, source_target_pairs={{0,3},{1,0},{2,1},{3,2},{4,7},{5,4},{6,5},{7,6},{8,11},{9,8},{10,9... | collective-permute-start | bytes 294920 | tf_op jit(solution)/shard_map/ppermute | solution.py:221
  144.8 2.1 %collective-permute-done.41.one = bf16[3,64,256]{2,1,0:T(8,128)(2,1)S(1)} collective-permute-done((bf16[3,64,256]{2,1,0:T(8,128)(2,1)S(1)}, bf16[3,64,256]{2,1,0:T(8,128)(2,1)S(1)}, u32[]{:S(2)}, u32[]{:S(2)}) %collective-permute-start.41) | collective-permute-done | bytes 98336 | tf_op jit(solution)/shard_map/ppermute | solution.py:221
  146.9 3.7 %collective-permute-done.42.two = bf16[3,64,256]{2,1,0:T(8,128)(2,1)S(1)} collective-permute-done((bf16[3,64,256]{2,1,0:T(8,128)(2,1)S(1)}, bf16[3,64,256]{2,1,0:T(8,128)(2,1)S(1)}, u32[]{:S(2)}, u32[]{:S(2)}) %collective-permute-start.42) | collective-permute-done | bytes 98336 | tf_op jit(solution)/shard_map/ppermute | solution.py:221
  150.6 1.9 %collective-permute-done.43.three = bf16[3,64,256]{2,1,0:T(8,128)(2,1)S(1)} collective-permute-done((bf16[3,64,256]{2,1,0:T(8,128)(2,1)S(1)}, bf16[3,64,256]{2,1,0:T(8,128)(2,1)S(1)}, u32[]{:S(2)}, u32[]{:S(2)}) %collective-permute-start.43) | collective-permute-done | bytes 98336 | tf_op jit(solution)/shard_map/ppermute | solution.py:221
  152.5 1.3 finish.1
  (54 shorter events, 3.1 us)
Async XLA Ops:
  0.6 10.2 %collective-permute-start.1 = (bf16[128,256]{1,0:T(8,128)(2,1)}, bf16[128,256]{1,0:T(8,128)(2,1)S(1)}, u32[]{:S(2)}, u32[]{:S(2)}) collective-permute-start(bf16[128,256]{1,0:T(8,128)(2,1)} %zero.1), channel_id=1, source_target_pairs={{0,2},{1,3},{2,0},{3,1},{4,6},{5,7},{6,4},{7,5},{8,10},{9,11},{10,... | collective-permute-start | bytes 196616 | tf_op jit(solution)/shard_map/ppermute | solution.py:216
  7.9 7.1 %collective-permute-start = (bf16[128,256]{1,0:T(8,128)(2,1)}, bf16[128,256]{1,0:T(8,128)(2,1)S(1)}, u32[]{:S(2)}, u32[]{:S(2)}) collective-permute-start(bf16[128,256]{1,0:T(8,128)(2,1)} %zero.1), channel_id=1, source_target_pairs={{0,3},{1,0},{2,1},{3,2},{4,7},{5,4},{6,5},{7,6},{8,11},{9,8},{10,9... | collective-permute-start | bytes 196616 | tf_op jit(solution)/shard_map/ppermute | solution.py:216
  7.9 7.1 %collective-permute-start.2 = (bf16[128,256]{1,0:T(8,128)(2,1)}, bf16[128,256]{1,0:T(8,128)(2,1)S(1)}, u32[]{:S(2)}, u32[]{:S(2)}) collective-permute-start(bf16[128,256]{1,0:T(8,128)(2,1)} %zero.1), channel_id=1, source_target_pairs={{0,1},{1,2},{2,3},{3,0},{4,5},{5,6},{6,7},{7,4},{8,9},{9,10},{10,1... | collective-permute-start | bytes 196616 | tf_op jit(solution)/shard_map/ppermute | solution.py:216
  15.0 0.8 copy-start.3
  15.9 10.8 %collective-permute-start.5 = (bf16[8,64,256]{2,1,0:T(8,128)(2,1)S(1)}, bf16[8,64,256]{2,1,0:T(8,128)(2,1)S(1)}, u32[]{:S(2)}, u32[]{:S(2)}) collective-permute-start(bf16[8,64,256]{2,1,0:T(8,128)(2,1)S(1)} %join.1.refs_0_), channel_id=1, source_target_pairs={{0,8},{1,9},{2,10},{3,11},{4,12},{5,13},{6,14},{7,15},{8,0},{9,1},... | collective-permute-start | bytes 786440 | tf_op jit(solution)/shard_map/ppermute | solution.py:229
  19.2 7.5 %collective-permute-start.10 = (bf16[8,64,256]{2,1,0:T(8,128)(2,1)S(1)}, bf16[8,64,256]{2,1,0:T(8,128)(2,1)S(1)}, u32[]{:S(2)}, u32[]{:S(2)}) collective-permute-start(bf16[8,64,256]{2,1,0:T(8,128)(2,1)S(1)} %join.1.refs_0_), channel_id=1, source_target_pairs={{0,240},{16,32},{32,16},{48,64},{64,48},{80,96},{96,80},{112,128},... | collective-permute-start | bytes 786440 | tf_op jit(solution)/shard_map/ppermute | solution.py:233
  19.2 12.5 %collective-permute-start.4 = (bf16[8,64,256]{2,1,0:T(8,128)(2,1)S(1)}, bf16[8,64,256]{2,1,0:T(8,128)(2,1)S(1)}, u32[]{:S(2)}, u32[]{:S(2)}) collective-permute-start(bf16[8,64,256]{2,1,0:T(8,128)(2,1)S(1)} %join.1.refs_0_), channel_id=1, source_target_pairs={{0,12},{1,13},{2,14},{3,15},{4,0},{5,1},{6,2},{7,3},{8,4},{9,5},{1... | collective-permute-start | bytes 786440 | tf_op jit(solution)/shard_map/ppermute | solution.py:229
  20.2 11.5 %collective-permute-start.6 = (bf16[8,64,256]{2,1,0:T(8,128)(2,1)S(1)}, bf16[8,64,256]{2,1,0:T(8,128)(2,1)S(1)}, u32[]{:S(2)}, u32[]{:S(2)}) collective-permute-start(bf16[8,64,256]{2,1,0:T(8,128)(2,1)S(1)} %join.1.refs_0_), channel_id=1, source_target_pairs={{0,16},{16,0},{32,48},{48,32},{64,80},{80,64},{96,112},{112,96},{1... | collective-permute-start | bytes 786440 | tf_op jit(solution)/shard_map/ppermute | solution.py:226
  21.6 11.8 %collective-permute-start.3 = (bf16[8,64,256]{2,1,0:T(8,128)(2,1)S(1)}, bf16[8,64,256]{2,1,0:T(8,128)(2,1)S(1)}, u32[]{:S(2)}, u32[]{:S(2)}) collective-permute-start(bf16[8,64,256]{2,1,0:T(8,128)(2,1)S(1)} %join.1.refs_0_), channel_id=1, source_target_pairs={{0,4},{1,5},{2,6},{3,7},{4,8},{5,9},{6,10},{7,11},{8,12},{9,13},{1... | collective-permute-start | bytes 786440 | tf_op jit(solution)/shard_map/ppermute | solution.py:229
  26.7 6.9 %collective-permute-start.13 = (bf16[8,64,256]{2,1,0:T(8,128)(2,1)S(1)}, bf16[8,64,256]{2,1,0:T(8,128)(2,1)S(1)}, u32[]{:S(2)}, u32[]{:S(2)}) collective-permute-start(bf16[8,64,256]{2,1,0:T(8,128)(2,1)S(1)} %collective-permute-done.5.refs_3_), channel_id=1, source_target_pairs={{0,240},{16,32},{32,16},{48,64},{64,48},{80,96},{96,80},{112,128},... | collective-permute-start | bytes 786440 | tf_op jit(solution)/shard_map/ppermute | solution.py:233
  26.7 11.7 %collective-permute-start.9 = (bf16[8,64,256]{2,1,0:T(8,128)(2,1)S(1)}, bf16[8,64,256]{2,1,0:T(8,128)(2,1)}, u32[]{:S(2)}, u32[]{:S(2)}) collective-permute-start(bf16[8,64,256]{2,1,0:T(8,128)(2,1)S(1)} %collective-permute-done.5.refs_3_), channel_id=1, source_target_pairs={{0,16},{16,0},{32,48},{48,32},{64,80},{80,64},{96,112},{112,96},{1... | collective-permute-start | bytes 786440 | tf_op jit(solution)/shard_map/ppermute | solution.py:235
  31.7 6.7 %collective-permute-start.12 = (bf16[8,64,256]{2,1,0:T(8,128)(2,1)S(1)}, bf16[8,64,256]{2,1,0:T(8,128)(2,1)}, u32[]{:S(2)}, u32[]{:S(2)}) collective-permute-start(bf16[8,64,256]{2,1,0:T(8,128)(2,1)S(1)} %collective-permute-done.4.refs_2_), channel_id=1, source_target_pairs={{0,240},{16,32},{32,16},{48,64},{64,48},{80,96},{96,80},{112,128},... | collective-permute-start | bytes 786440 | tf_op jit(solution)/shard_map/ppermute | solution.py:233
  31.7 6.7 %collective-permute-start.8 = (bf16[8,64,256]{2,1,0:T(8,128)(2,1)S(1)}, bf16[8,64,256]{2,1,0:T(8,128)(2,1)}, u32[]{:S(2)}, u32[]{:S(2)}) collective-permute-start(bf16[8,64,256]{2,1,0:T(8,128)(2,1)S(1)} %collective-permute-done.4.refs_2_), channel_id=1, source_target_pairs={{0,16},{16,0},{32,48},{48,32},{64,80},{80,64},{96,112},{112,96},{1... | collective-permute-start | bytes 786440 | tf_op jit(solution)/shard_map/ppermute | solution.py:235
  33.3 7.1 %collective-permute-start.11 = (bf16[8,64,256]{2,1,0:T(8,128)(2,1)S(1)}, bf16[8,64,256]{2,1,0:T(8,128)(2,1)}, u32[]{:S(2)}, u32[]{:S(2)}) collective-permute-start(bf16[8,64,256]{2,1,0:T(8,128)(2,1)S(1)} %collective-permute-done.3.refs_1_), channel_id=1, source_target_pairs={{0,240},{16,32},{32,16},{48,64},{64,48},{80,96},{96,80},{112,128},... | collective-permute-start | bytes 786440 | tf_op jit(solution)/shard_map/ppermute | solution.py:233
  33.6 6.9 %collective-permute-start.7 = (bf16[8,64,256]{2,1,0:T(8,128)(2,1)S(1)}, bf16[8,64,256]{2,1,0:T(8,128)(2,1)}, u32[]{:S(2)}, u32[]{:S(2)}) collective-permute-start(bf16[8,64,256]{2,1,0:T(8,128)(2,1)S(1)} %collective-permute-done.3.refs_1_), channel_id=1, source_target_pairs={{0,16},{16,0},{32,48},{48,32},{64,80},{80,64},{96,112},{112,96},{1... | collective-permute-start | bytes 786440 | tf_op jit(solution)/shard_map/ppermute | solution.py:235
  36.2 1.4 copy-start
  37.6 0.7 copy-start.4
  38.4 33.5 %copy-start.1 = (bf16[256,256]{1,0:T(8,128)(2,1)S(1)}, bf16[256,256]{1,0:T(8,128)(2,1)}, u32[]{:S(2)}) copy-start(bf16[256,256]{1,0:T(8,128)(2,1)} %weight.1) | copy-start | bytes 393220
  38.4 33.5 %copy-start.2 = (bf16[128,256]{1,0:T(8,128)(2,1)S(1)}, bf16[128,256]{1,0:T(8,128)(2,1)}, u32[]{:S(2)}) copy-start(bf16[128,256]{1,0:T(8,128)(2,1)} %grad_out.1) | copy-start | bytes 196612
  43.7 9.3 %collective-permute-start.14 = (bf16[8,64,256]{2,1,0:T(8,128)(2,1)S(1)}, bf16[8,64,256]{2,1,0:T(8,128)(2,1)S(1)}, u32[]{:S(2)}, u32[]{:S(2)}) collective-permute-start(bf16[8,64,256]{2,1,0:T(8,128)(2,1)S(1)} %get-tuple-element.31), channel_id=1, source_target_pairs={{0,4},{1,5},{2,6},{3,7},{4,8},{5,9},{6,10},{7,11},{8,12},{9,13},{1... | collective-permute-start | bytes 786440 | tf_op jit(solution)/shard_map/ppermute | solution.py:221
  44.9 14.8 %collective-permute-start.15 = (bf16[8,64,256]{2,1,0:T(8,128)(2,1)S(1)}, bf16[8,64,256]{2,1,0:T(8,128)(2,1)S(1)}, u32[]{:S(2)}, u32[]{:S(2)}) collective-permute-start(bf16[8,64,256]{2,1,0:T(8,128)(2,1)S(1)} %get-tuple-element.32), channel_id=1, source_target_pairs={{0,8},{1,9},{2,10},{3,11},{4,12},{5,13},{6,14},{7,15},{8,0},{9,1},... | collective-permute-start | bytes 786440 | tf_op jit(solution)/shard_map/ppermute | solution.py:221
  47.8 11.9 %collective-permute-start.16 = (bf16[8,64,256]{2,1,0:T(8,128)(2,1)S(1)}, bf16[8,64,256]{2,1,0:T(8,128)(2,1)S(1)}, u32[]{:S(2)}, u32[]{:S(2)}) collective-permute-start(bf16[8,64,256]{2,1,0:T(8,128)(2,1)S(1)} %get-tuple-element.33), channel_id=1, source_target_pairs={{0,12},{1,13},{2,14},{3,15},{4,0},{5,1},{6,2},{7,3},{8,4},{9,5},{1... | collective-permute-start | bytes 786440 | tf_op jit(solution)/shard_map/ppermute | solution.py:221
  60.4 8.4 %collective-permute-start.17 = (bf16[2,64,256]{2,1,0:T(8,128)(2,1)S(1)}, bf16[2,64,256]{2,1,0:T(8,128)(2,1)S(1)}, u32[]{:S(2)}, u32[]{:S(2)}) collective-permute-start(bf16[2,64,256]{2,1,0:T(8,128)(2,1)S(1)} %get-tuple-element.35), channel_id=1, source_target_pairs={{0,1},{1,2},{2,3},{3,0},{4,5},{5,6},{6,7},{7,4},{8,9},{9,10},{10,1... | collective-permute-start | bytes 196616 | tf_op jit(solution)/shard_map/ppermute | solution.py:221
  60.5 9.2 %collective-permute-start.18 = (bf16[2,64,256]{2,1,0:T(8,128)(2,1)S(1)}, bf16[2,64,256]{2,1,0:T(8,128)(2,1)S(1)}, u32[]{:S(2)}, u32[]{:S(2)}) collective-permute-start(bf16[2,64,256]{2,1,0:T(8,128)(2,1)S(1)} %get-tuple-element.36), channel_id=1, source_target_pairs={{0,2},{1,3},{2,0},{3,1},{4,6},{5,7},{6,4},{7,5},{8,10},{9,11},{10,... | collective-permute-start | bytes 196616 | tf_op jit(solution)/shard_map/ppermute | solution.py:221
  65.5 6.4 %collective-permute-start.19 = (bf16[2,64,256]{2,1,0:T(8,128)(2,1)S(1)}, bf16[2,64,256]{2,1,0:T(8,128)(2,1)S(1)}, u32[]{:S(2)}, u32[]{:S(2)}) collective-permute-start(bf16[2,64,256]{2,1,0:T(8,128)(2,1)S(1)} %get-tuple-element.37), channel_id=1, source_target_pairs={{0,3},{1,0},{2,1},{3,2},{4,7},{5,4},{6,5},{7,6},{8,11},{9,8},{10,9... | collective-permute-start | bytes 196616 | tf_op jit(solution)/shard_map/ppermute | solution.py:221
  73.3 7.3 %collective-permute-start.20 = (bf16[3,64,256]{2,1,0:T(8,128)(2,1)S(1)}, bf16[3,64,256]{2,1,0:T(8,128)(2,1)S(1)}, u32[]{:S(2)}, u32[]{:S(2)}) collective-permute-start(bf16[3,64,256]{2,1,0:T(8,128)(2,1)S(1)} %get-tuple-element.40), channel_id=1, source_target_pairs={{0,3},{1,0},{2,1},{3,2},{4,7},{5,4},{6,5},{7,6},{8,11},{9,8},{10,9... | collective-permute-start | bytes 294920 | tf_op jit(solution)/shard_map/ppermute | solution.py:295
  76.6 9.5 %collective-permute-start.21 = (bf16[3,64,256]{2,1,0:T(8,128)(2,1)S(1)}, bf16[3,64,256]{2,1,0:T(8,128)(2,1)S(1)}, u32[]{:S(2)}, u32[]{:S(2)}) collective-permute-start(bf16[3,64,256]{2,1,0:T(8,128)(2,1)S(1)} %get-tuple-element.41), channel_id=1, source_target_pairs={{0,2},{1,3},{2,0},{3,1},{4,6},{5,7},{6,4},{7,5},{8,10},{9,11},{10,... | collective-permute-start | bytes 294920 | tf_op jit(solution)/shard_map/ppermute | solution.py:295
  79.0 7.6 %collective-permute-start.22 = (bf16[3,64,256]{2,1,0:T(8,128)(2,1)S(1)}, bf16[3,64,256]{2,1,0:T(8,128)(2,1)S(1)}, u32[]{:S(2)}, u32[]{:S(2)}) collective-permute-start(bf16[3,64,256]{2,1,0:T(8,128)(2,1)S(1)} %get-tuple-element.42), channel_id=1, source_target_pairs={{0,1},{1,2},{2,3},{3,0},{4,5},{5,6},{6,7},{7,4},{8,9},{9,10},{10,1... | collective-permute-start | bytes 294920 | tf_op jit(solution)/shard_map/ppermute | solution.py:295
  86.7 12.3 %collective-permute-start.25 = (bf16[9,64,256]{2,1,0:T(8,128)(2,1)S(1)}, bf16[9,64,256]{2,1,0:T(8,128)(2,1)S(1)}, u32[]{:S(2)}, u32[]{:S(2)}) collective-permute-start(bf16[9,64,256]{2,1,0:T(8,128)(2,1)S(1)} %spread.1.refs_0_), channel_id=1, source_target_pairs={{0,4},{1,5},{2,6},{3,7},{4,8},{5,9},{6,10},{7,11},{8,12},{9,13},{1... | collective-permute-start | bytes 884744 | tf_op jit(solution)/shard_map/ppermute | solution.py:229
  90.5 13.8 %collective-permute-start.24 = (bf16[9,64,256]{2,1,0:T(8,128)(2,1)S(1)}, bf16[9,64,256]{2,1,0:T(8,128)(2,1)S(1)}, u32[]{:S(2)}, u32[]{:S(2)}) collective-permute-start(bf16[9,64,256]{2,1,0:T(8,128)(2,1)S(1)} %spread.1.refs_0_), channel_id=1, source_target_pairs={{0,12},{1,13},{2,14},{3,15},{4,0},{5,1},{6,2},{7,3},{8,4},{9,5},{1... | collective-permute-start | bytes 884744 | tf_op jit(solution)/shard_map/ppermute | solution.py:229
  92.0 14.0 %collective-permute-start.23 = (bf16[9,64,256]{2,1,0:T(8,128)(2,1)S(1)}, bf16[9,64,256]{2,1,0:T(8,128)(2,1)S(1)}, u32[]{:S(2)}, u32[]{:S(2)}) collective-permute-start(bf16[9,64,256]{2,1,0:T(8,128)(2,1)S(1)} %spread.1.refs_0_), channel_id=1, source_target_pairs={{0,8},{1,9},{2,10},{3,11},{4,12},{5,13},{6,14},{7,15},{8,0},{9,1},... | collective-permute-start | bytes 884744 | tf_op jit(solution)/shard_map/ppermute | solution.py:229
  93.4 14.4 %collective-permute-start.32 = (bf16[9,64,256]{2,1,0:T(8,128)(2,1)S(1)}, bf16[9,64,256]{2,1,0:T(8,128)(2,1)S(1)}, u32[]{:S(2)}, u32[]{:S(2)}) collective-permute-start(bf16[9,64,256]{2,1,0:T(8,128)(2,1)S(1)} %spread.1.refs_0_), channel_id=1, source_target_pairs={{0,240},{16,32},{32,16},{48,64},{64,48},{80,96},{96,80},{112,128},... | collective-permute-start | bytes 884744 | tf_op jit(solution)/shard_map/ppermute | solution.py:233
  93.4 16.3 %collective-permute-start.28 = (bf16[9,64,256]{2,1,0:T(8,128)(2,1)S(1)}, bf16[9,64,256]{2,1,0:T(8,128)(2,1)S(1)}, u32[]{:S(2)}, u32[]{:S(2)}) collective-permute-start(bf16[9,64,256]{2,1,0:T(8,128)(2,1)S(1)} %spread.1.refs_0_), channel_id=1, source_target_pairs={{0,16},{16,0},{32,48},{48,32},{64,80},{80,64},{96,112},{112,96},{1... | collective-permute-start | bytes 884744 | tf_op jit(solution)/shard_map/ppermute | solution.py:226
  98.9 14.4 %collective-permute-start.33 = (bf16[9,64,256]{2,1,0:T(8,128)(2,1)S(1)}, bf16[9,64,256]{2,1,0:T(8,128)(2,1)S(1)}, u32[]{:S(2)}, u32[]{:S(2)}) collective-permute-start(bf16[9,64,256]{2,1,0:T(8,128)(2,1)S(1)} %collective-permute-done.25.refs_1_), channel_id=1, source_target_pairs={{0,240},{16,32},{32,16},{48,64},{64,48},{80,96},{96,80},{112,128},... | collective-permute-start | bytes 884744 | tf_op jit(solution)/shard_map/ppermute | solution.py:233
  106.1 1.3 collective-permute-start.26
  107.4 5.0 %collective-permute-start.27 = (f32[64,256]{1,0:T(8,128)S(1)}, f32[64,256]{1,0:T(8,128)S(1)}, u32[]{:S(2)}, u32[]{:S(2)}) collective-permute-start(f32[64,256]{1,0:T(8,128)S(1)} %add.40), channel_id=1, source_target_pairs={{0,32},{16,48},{32,0},{48,16},{64,96},{80,112},{96,64},{112,80},{1... | collective-permute-start | bytes 196616 | tf_op jit(solution)/shard_map/ppermute | solution.py:306
  107.5 6.7 %collective-permute-start.29 = (bf16[9,64,256]{2,1,0:T(8,128)(2,1)S(1)}, bf16[9,64,256]{2,1,0:T(8,128)(2,1)S(1)}, u32[]{:S(2)}, u32[]{:S(2)}) collective-permute-start(bf16[9,64,256]{2,1,0:T(8,128)(2,1)S(1)} %collective-permute-done.25.refs_1_), channel_id=1, source_target_pairs={{0,16},{16,0},{32,48},{48,32},{64,80},{80,64},{96,112},{112,96},{1... | collective-permute-start | bytes 884744 | tf_op jit(solution)/shard_map/ppermute | solution.py:235
  107.8 7.1 %collective-permute-start.34 = (bf16[9,64,256]{2,1,0:T(8,128)(2,1)S(1)}, bf16[9,64,256]{2,1,0:T(8,128)(2,1)S(1)}, u32[]{:S(2)}, u32[]{:S(2)}) collective-permute-start(bf16[9,64,256]{2,1,0:T(8,128)(2,1)S(1)} %collective-permute-done.24.refs_2_), channel_id=1, source_target_pairs={{0,240},{16,32},{32,16},{48,64},{64,48},{80,96},{96,80},{112,128},... | collective-permute-start | bytes 884744 | tf_op jit(solution)/shard_map/ppermute | solution.py:233
  109.7 5.2 %collective-permute-start.30 = (bf16[9,64,256]{2,1,0:T(8,128)(2,1)S(1)}, bf16[9,64,256]{2,1,0:T(8,128)(2,1)S(1)}, u32[]{:S(2)}, u32[]{:S(2)}) collective-permute-start(bf16[9,64,256]{2,1,0:T(8,128)(2,1)S(1)} %collective-permute-done.24.refs_2_), channel_id=1, source_target_pairs={{0,16},{16,0},{32,48},{48,32},{64,80},{80,64},{96,112},{112,96},{1... | collective-permute-start | bytes 884744 | tf_op jit(solution)/shard_map/ppermute | solution.py:235
  112.4 6.1 %collective-permute-start.35 = (bf16[9,64,256]{2,1,0:T(8,128)(2,1)S(1)}, bf16[9,64,256]{2,1,0:T(8,128)(2,1)S(1)}, u32[]{:S(2)}, u32[]{:S(2)}) collective-permute-start(bf16[9,64,256]{2,1,0:T(8,128)(2,1)S(1)} %collective-permute-done.23.refs_3_), channel_id=1, source_target_pairs={{0,240},{16,32},{32,16},{48,64},{64,48},{80,96},{96,80},{112,128},... | collective-permute-start | bytes 884744 | tf_op jit(solution)/shard_map/ppermute | solution.py:233
  113.3 5.3 %collective-permute-start.31 = (bf16[9,64,256]{2,1,0:T(8,128)(2,1)S(1)}, bf16[9,64,256]{2,1,0:T(8,128)(2,1)S(1)}, u32[]{:S(2)}, u32[]{:S(2)}) collective-permute-start(bf16[9,64,256]{2,1,0:T(8,128)(2,1)S(1)} %collective-permute-done.23.refs_3_), channel_id=1, source_target_pairs={{0,16},{16,0},{32,48},{48,32},{64,80},{80,64},{96,112},{112,96},{1... | collective-permute-start | bytes 884744 | tf_op jit(solution)/shard_map/ppermute | solution.py:235
  121.2 14.1 %collective-permute-start.36 = (bf16[8,64,256]{2,1,0:T(8,128)(2,1)S(1)}, bf16[8,64,256]{2,1,0:T(8,128)(2,1)S(1)}, u32[]{:S(2)}, u32[]{:S(2)}) collective-permute-start(bf16[8,64,256]{2,1,0:T(8,128)(2,1)S(1)} %get-tuple-element.46), channel_id=1, source_target_pairs={{0,4},{1,5},{2,6},{3,7},{4,8},{5,9},{6,10},{7,11},{8,12},{9,13},{1... | collective-permute-start | bytes 786440 | tf_op jit(solution)/shard_map/ppermute | solution.py:221
  122.4 14.6 %collective-permute-start.37 = (bf16[8,64,256]{2,1,0:T(8,128)(2,1)S(1)}, bf16[8,64,256]{2,1,0:T(8,128)(2,1)S(1)}, u32[]{:S(2)}, u32[]{:S(2)}) collective-permute-start(bf16[8,64,256]{2,1,0:T(8,128)(2,1)S(1)} %get-tuple-element.47), channel_id=1, source_target_pairs={{0,8},{1,9},{2,10},{3,11},{4,12},{5,13},{6,14},{7,15},{8,0},{9,1},... | collective-permute-start | bytes 786440 | tf_op jit(solution)/shard_map/ppermute | solution.py:221
  124.6 12.6 %collective-permute-start.38 = (bf16[8,64,256]{2,1,0:T(8,128)(2,1)S(1)}, bf16[8,64,256]{2,1,0:T(8,128)(2,1)S(1)}, u32[]{:S(2)}, u32[]{:S(2)}) collective-permute-start(bf16[8,64,256]{2,1,0:T(8,128)(2,1)S(1)} %get-tuple-element.48), channel_id=1, source_target_pairs={{0,12},{1,13},{2,14},{3,15},{4,0},{5,1},{6,2},{7,3},{8,4},{9,5},{1... | collective-permute-start | bytes 786440 | tf_op jit(solution)/shard_map/ppermute | solution.py:221
  125.2 4.3 %collective-permute-start.39 = (f32[64,256]{1,0:T(8,128)S(1)}, f32[64,256]{1,0:T(8,128)S(1)}, u32[]{:S(2)}, u32[]{:S(2)}) collective-permute-start(f32[64,256]{1,0:T(8,128)S(1)} %add.41), channel_id=1, source_target_pairs={{0,128},{16,144},{32,160},{48,176},{64,192},{80,208},{96,224},{112... | collective-permute-start | bytes 196616 | tf_op jit(solution)/shard_map/ppermute | solution.py:309
  129.4 5.9 %collective-permute-start.40 = (f32[64,256]{1,0:T(8,128)S(1)}, f32[64,256]{1,0:T(8,128)S(1)}, u32[]{:S(2)}, u32[]{:S(2)}) collective-permute-start(f32[64,256]{1,0:T(8,128)S(1)} %add.42), channel_id=1, source_target_pairs={{0,64},{16,80},{32,96},{48,112},{64,0},{80,16},{96,32},{112,48},{1... | collective-permute-start | bytes 196616 | tf_op jit(solution)/shard_map/ppermute | solution.py:309
  137.9 9.0 %collective-permute-start.41 = (bf16[3,64,256]{2,1,0:T(8,128)(2,1)S(1)}, bf16[3,64,256]{2,1,0:T(8,128)(2,1)S(1)}, u32[]{:S(2)}, u32[]{:S(2)}) collective-permute-start(bf16[3,64,256]{2,1,0:T(8,128)(2,1)S(1)} %get-tuple-element.52), channel_id=1, source_target_pairs={{0,1},{1,2},{2,3},{3,0},{4,5},{5,6},{6,7},{7,4},{8,9},{9,10},{10,1... | collective-permute-start | bytes 294920 | tf_op jit(solution)/shard_map/ppermute | solution.py:221
  139.6 10.9 %collective-permute-start.42 = (bf16[3,64,256]{2,1,0:T(8,128)(2,1)S(1)}, bf16[3,64,256]{2,1,0:T(8,128)(2,1)S(1)}, u32[]{:S(2)}, u32[]{:S(2)}) collective-permute-start(bf16[3,64,256]{2,1,0:T(8,128)(2,1)S(1)} %get-tuple-element.53), channel_id=1, source_target_pairs={{0,2},{1,3},{2,0},{3,1},{4,6},{5,7},{6,4},{7,5},{8,10},{9,11},{10,... | collective-permute-start | bytes 294920 | tf_op jit(solution)/shard_map/ppermute | solution.py:221
  143.0 9.5 %collective-permute-start.43 = (bf16[3,64,256]{2,1,0:T(8,128)(2,1)S(1)}, bf16[3,64,256]{2,1,0:T(8,128)(2,1)S(1)}, u32[]{:S(2)}, u32[]{:S(2)}) collective-permute-start(bf16[3,64,256]{2,1,0:T(8,128)(2,1)S(1)} %get-tuple-element.54), channel_id=1, source_target_pairs={{0,3},{1,0},{2,1},{3,2},{4,7},{5,4},{6,5},{7,6},{8,11},{9,8},{10,9... | collective-permute-start | bytes 294920 | tf_op jit(solution)/shard_map/ppermute | solution.py:221
